TPU v7x, 512 devices: a whole 4x8x8 slice. The times are simulated.
512 devices in a mesh: row: 32 (over y_lo, x, core), col: 16 (over z, y_hi).
Axes of the slice: x: 4, y: 8 (y_hi: 2, y_lo: 4; y = y_hi * 4 + y_lo), z: 8, core: 2. Of those that a mesh axis runs over, the one named last changes fastest.
Arguments:
- features: bfloat16 [256, 256, 384], P('row', 'col'), may hold values from -30 to 30
- w_query: bfloat16 [384, 384], replicated, may hold values from -0.3125 to 0.3125
- w_key: bfloat16 [384, 384], replicated, may hold values from -0.3125 to 0.3125
- w_value: bfloat16 [384, 384], replicated, may hold values from -0.3125 to 0.3125
- w_out: bfloat16 [384, 384], replicated, may hold values from -0.625 to 0.625
- logit_scale: float32 [6], replicated, may hold values from 2 to 16
- dw_kernel: float32 [49, 384], replicated, may hold values from -2 to 2
- dw_bias: float32 [384], replicated, may hold values from -3 to 3
- ln_gain: float32 [384], replicated, may hold values from 0.5 to 1.5
- ln_bias: float32 [384], replicated, may hold values from -2 to 2
- w_up: bfloat16 [384, 1280], replicated, may hold values from -0.3125 to 0.3125
- b_up: float32 [1280], replicated, may hold values from -3 to 3
- w_down: bfloat16 [1280, 384], replicated, may hold values from -0.15625 to 0.15625
- b_down: float32 [384], replicated, may hold values from -3 to 3
- layer_scale: float32 [384], replicated, may hold values from 0.5 to 1.5
- cotangent: bfloat16 [256, 256, 384], P('row', 'col'), may hold values from -6 to 6
- tile_list: int32 [32, 16, 8], P('row', 'col'), may hold values from -1 to 7, as said below
Outputs:
- output: bfloat16 [256, 256, 384], P('row', 'col')
- grad_mixed: float32 [256, 256, 384], P('row', 'col')
- grad_w_up: float32 [491520], P(('row', 'col'))
- grad_w_down: float32 [491520], P(('row', 'col'))
- grad_dw_kernel: float32 [49, 384], replicated
- grad_dw_bias: float32 [384], replicated
- grad_ln_gain: float32 [384], replicated
- grad_ln_bias: float32 [384], replicated
- grad_b_up: float32 [1280], replicated
- grad_b_down: float32 [384], replicated
- grad_layer_scale: float32 [384], replicated
Inputs may be any that keep to these rules, and one draw needn't show every extreme that they name: `tile_list`: each device's list names its occupied tiles in increasing order, then -1 to the end. A device and the device whose col index differs by 8 hold exactly 10 occupied tiles together; some device holds all 8.
All inputs are finite; a program needn't handle non-finite values.
Results may differ from a plain program's by a relative error of at most 0.0095.
Values may be sent and summed in bfloat16 or wider, within the bound.
No kernel may reach another device: no remote copies, remote signals or barrier semaphores. Data moves between devices by JAX's collectives and lax.ppermute only.
A program may use at most 64 MiB of HBM per device.

v0:
```python
import jax
import jax.numpy as jnp
from jax import lax
from jax.sharding import PartitionSpec as P

POOL = 8
TS = 4


EPS_NORM = 1e-06
GELU_SCALE = 0.7978845608028654


def extended(array, sides, width):
    for axis, dim in sides:
        size, length = (lax.axis_size(axis), array.shape[dim])
        up = [(i, (i + 1) % size) for i in range(size - 1)]
        down = [(j, i) for i, j in up]
        last = lax.slice_in_dim(array, length - width, length, axis=dim)
        leading = lax.slice_in_dim(array, 0, width, axis=dim)
        before = lax.ppermute(last, axis, up)
        after = lax.ppermute(leading, axis, down)
        array = jnp.concatenate([before, array, after], axis=dim)
    return array


def gelu_parts(preact):
    cubic = 0.044715 * preact * preact
    tanh_val = jnp.tanh(GELU_SCALE * preact * (1.0 + cubic))
    value = 0.5 * preact * (1.0 + tanh_val)
    slope = 0.5 * (1.0 + tanh_val) + 0.5 * preact * (1.0 - tanh_val * tanh_val) * GELU_SCALE * (
        1.0 + 3.0 * cubic
    )
    return (value, slope)


def head_normed(values, heads):
    shaped = values.reshape(values.shape[:-1] + (heads, values.shape[-1] // heads))
    squares = jnp.sum(shaped * shaped, axis=-1, keepdims=True)
    return (shaped / jnp.sqrt(squares + EPS_NORM)).reshape(values.shape)


def sublayer(spatial, cotan, weight, ln_gain, ln_bias, w_up, b_up, w_down, b_down, layer_scale):
    center = spatial - jnp.mean(spatial, axis=-1, keepdims=True)
    inv_std = lax.rsqrt(jnp.mean(center * center, axis=-1, keepdims=True) + EPS_NORM)
    standard = center * inv_std
    lnout = (standard * ln_gain + ln_bias).astype(jnp.bfloat16)
    preact = jnp.dot(lnout, w_up, preferred_element_type=jnp.float32) + b_up
    hid_val, slope = gelu_parts(preact)
    hidden = hid_val.astype(jnp.bfloat16)
    branch = (jnp.dot(hidden, w_down, preferred_element_type=jnp.float32) + b_down) * weight
    d_branch = cotan * layer_scale * weight
    d_branch_b = d_branch.astype(jnp.bfloat16)
    d_hidden = lax.dot_general(
        d_branch_b, w_down, (((1,), (1,)), ((), ())), preferred_element_type=jnp.float32
    )
    d_pre = d_hidden * slope
    d_pre_b = d_pre.astype(jnp.bfloat16)
    d_lnout = lax.dot_general(
        d_pre_b, w_up, (((1,), (1,)), ((), ())), preferred_element_type=jnp.float32
    )
    scaled = d_lnout * ln_gain
    d_spatial = inv_std * (
        scaled
        - jnp.mean(scaled, axis=-1, keepdims=True)
        - standard * jnp.mean(scaled * standard, axis=-1, keepdims=True)
    )
    grad_up = lax.dot_general(
        lnout, d_pre_b, (((0,), (0,)), ((), ())), preferred_element_type=jnp.float32
    )
    grad_down = lax.dot_general(
        hidden, d_branch_b, (((0,), (0,)), ((), ())), preferred_element_type=jnp.float32
    )
    smalls = (
        jnp.sum(d_lnout * standard, axis=0),
        jnp.sum(d_lnout, axis=0),
        jnp.sum(d_pre, axis=0),
        jnp.sum(d_branch, axis=0),
        jnp.sum(cotan * branch, axis=0),
    )
    return (branch, d_spatial, grad_up, grad_down, smalls)


def body(
    features,
    w_query,
    w_key,
    w_value,
    w_out,
    logit_scale,
    dw_kernel,
    dw_bias,
    ln_gain,
    ln_bias,
    w_up,
    b_up,
    w_down,
    b_down,
    layer_scale,
    cotangent,
    tile_list,
):
    rows_here, cols_here, chans = features.shape
    heads = logit_scale.shape[0]
    head_width = chans // heads
    flat_feat = features.reshape(-1, chans)
    query = head_normed(jnp.dot(flat_feat, w_query, preferred_element_type=jnp.float32), heads)
    query = query.astype(jnp.bfloat16).reshape(rows_here, cols_here, heads, head_width)
    pooled = jnp.mean(
        features.reshape(rows_here // POOL, POOL, cols_here, chans), axis=1, dtype=jnp.float32
    )
    flat_pool = pooled.astype(jnp.bfloat16).reshape(-1, chans)
    keys = head_normed(jnp.dot(flat_pool, w_key, preferred_element_type=jnp.float32), heads)
    keys = keys.astype(jnp.bfloat16).reshape(rows_here // POOL, cols_here, heads, head_width)
    values = jnp.dot(flat_pool, w_value, preferred_element_type=jnp.float32)
    values = values.astype(jnp.bfloat16).reshape(rows_here // POOL, cols_here, heads, head_width)
    key_piece = lax.all_gather(keys, "row", axis=0, tiled=True)
    value_piece = lax.all_gather(values, "row", axis=0, tiled=True)
    scores = jnp.einsum("iwhd,jwhd->iwhj", query, key_piece, preferred_element_type=jnp.float32)
    weight = jnp.exp(scores * logit_scale[:, None])
    numer = jnp.einsum(
        "iwhj,jwhd->iwhd",
        weight.astype(jnp.bfloat16),
        value_piece,
        preferred_element_type=jnp.float32,
    )
    numer, total = (numer, jnp.sum(weight, axis=-1))
    attended = (numer / total[..., None]).astype(jnp.bfloat16).reshape(-1, chans)
    mixed = flat_feat.astype(jnp.float32) + jnp.dot(
        attended, w_out, preferred_element_type=jnp.float32
    )
    mixed = mixed.astype(jnp.bfloat16).reshape(rows_here, cols_here, chans)
    padded = extended(mixed, (("row", 0), ("col", 1)), 3)
    spatial = jnp.broadcast_to(dw_bias, (rows_here, cols_here, chans))
    for row_off in range(7):
        for col_off in range(7):
            spatial = (
                spatial
                + padded[row_off : row_off + rows_here, col_off : col_off + cols_here].astype(
                    jnp.float32
                )
                * dw_kernel[7 * row_off + col_off]
            )
    tile_rows = rows_here // TS
    tile_cols = cols_here // TS
    tiles_here = tile_rows * tile_cols
    listing = tile_list[0, 0]
    hits = jnp.any(
        listing[:, None] == jnp.arange(tiles_here, dtype=jnp.int32)[None, :], axis=0
    ).astype(jnp.float32)
    pixel_mask = jnp.broadcast_to(
        hits.reshape(tile_rows, 1, tile_cols, 1), (tile_rows, TS, tile_cols, TS)
    )
    pixel_mask = pixel_mask.reshape(rows_here, cols_here)
    cot_full = cotangent.astype(jnp.float32)
    branch, d_spatial, grad_up, grad_down, smalls = sublayer(
        spatial.reshape(-1, chans),
        cot_full.reshape(-1, chans),
        pixel_mask.reshape(-1, 1),
        ln_gain,
        ln_bias,
        w_up,
        b_up,
        w_down,
        b_down,
        layer_scale,
    )
    branch_full = branch.reshape(rows_here, cols_here, chans)
    d_full = d_spatial.reshape(rows_here, cols_here, chans)
    output = (mixed.astype(jnp.float32) + layer_scale * branch_full).astype(jnp.bfloat16)
    d_padded = extended(d_full.astype(jnp.bfloat16), (("row", 0), ("col", 1)), 3).astype(
        d_full.dtype
    )
    grad_mixed = cot_full
    taps = []
    for row_off in range(7):
        for col_off in range(7):
            grad_mixed = (
                grad_mixed
                + d_padded[
                    6 - row_off : 6 - row_off + rows_here, 6 - col_off : 6 - col_off + cols_here
                ]
                * dw_kernel[7 * row_off + col_off]
            )
            taps.append(
                jnp.sum(
                    d_full
                    * padded[row_off : row_off + rows_here, col_off : col_off + cols_here].astype(
                        jnp.float32
                    ),
                    axis=(0, 1),
                )
            )
    kernel_grad = jnp.stack(taps, axis=0)
    bias_grad = jnp.sum(d_full, axis=(0, 1))
    gain_grad, shift_grad, up_bias_grad, down_bias_grad, scale_grad = smalls
    summed = lax.psum(
        (kernel_grad, bias_grad, gain_grad, shift_grad, up_bias_grad, down_bias_grad, scale_grad),
        ("row", "col"),
    )
    final = (
        lax.psum_scatter(grad_up.reshape(-1), ("row", "col"), scatter_dimension=0, tiled=True),
        lax.psum_scatter(grad_down.reshape(-1), ("row", "col"), scatter_dimension=0, tiled=True),
    )
    up_share = final[0]
    down_share = final[1]
    return (
        output,
        grad_mixed,
        up_share,
        down_share,
        summed[0],
        summed[1],
        summed[2],
        summed[3],
        summed[4],
        summed[5],
        summed[6],
    )


def solution(mesh):
    in_specs = (
        P("row", "col", None),
        P(),
        P(),
        P(),
        P(),
        P(),
        P(),
        P(),
        P(),
        P(),
        P(),
        P(),
        P(),
        P(),
        P(),
        P("row", "col", None),
        P("row", "col", None),
    )
    out_specs = (
        P("row", "col", None),
        P("row", "col", None),
        P(("row", "col")),
        P(("row", "col")),
        P(),
        P(),
        P(),
        P(),
        P(),
        P(),
        P(),
    )
    return jax.shard_map(body, mesh=mesh, in_specs=in_specs, out_specs=out_specs, check_vma=False)
```

profile of v0, /device:TPU:1, one launch (start us, length us, event | category | flops | bytes accessed | tf_op | source)
XLA Modules:
  0.0 448.0 jit_solution(15034873150971426450)
XLA Ops:
  9.5 46.8 %all_gather.6 = bf16[32,16,6,64]{3,1,2,0:T(8,128)(2,1)S(1)} all-gather(bf16[1,16,6,64]{3,1,2,0:T(8,128)(2,1)S(1)} %copy.48), channel_id=1, replica_groups=mesh['row'=32,'col'=16] {'row'}, dimensions={0}, use_global_device_ids=true | all-gather | bytes 405504 | tf_op jit(solution)/shard_map/all_gather | solution.py:118
  58.7 41.3 %all-gather = bf16[512,6,64]{2,0,1:T(8,128)(2,1)S(1)} all-gather(bf16[16,6,64]{2,0,1:T(8,128)(2,1)S(1)} %divide_convert_fusion.1), channel_id=2, replica_groups=mesh['row'=32,'col'=16] {'row'}, dimensions={0}, use_global_device_ids=true | all-gather | bytes 405504 | tf_op jit(solution)/shard_map/all_gather | solution.py:117
  101.8 2.1 collective-permute-start.1
  103.9 3.5 collective-permute-start
  109.3 3.5 collective-permute-start.2
  112.8 1.3 collective-permute-start.3
  114.5 7.1 %collective-permute-done.3 = bf16[14,3,384]{2,1,0:T(4,128)(2,1)S(1)} collective-permute-done((bf16[14,3,384]{2,1,0:T(4,128)(2,1)S(1)}, bf16[14,3,384]{2,1,0:T(4,128)(2,1)S(1)}, u32[]{:S(2)}, u32[]{:S(2)}) %collective-permute-start.3) | collective-permute-done | bytes 32288 | tf_op jit(solution)/shard_map/ppermute | solution.py:22
  122.0 2.4 fusion.178
  125.5 1.6 fusion.159
  129.9 1.8 fusion.176
  134.4 1.4 reshape.215
  136.2 2.6 reshape.216
  140.0 4.4 stack.199
  144.8 2.3 collective-permute-start.5
  147.1 4.4 collective-permute-start.4
  152.6 1.3 collective-permute-start.7
  153.9 7.9 %collective-permute-start.6 = (bf16[14,3,384]{2,1,0:T(4,128)(2,1)S(1)}, bf16[14,3,384]{2,1,0:T(4,128)(2,1)S(1)}, u32[]{:S(2)}, u32[]{:S(2)}) collective-permute-start(bf16[14,3,384]{2,1,0:T(4,128)(2,1)S(1)} %get-tuple-element.135), channel_id=1, source_target_pairs={{0,1},{1,2},{2,3},{3,4},{4,5},{5,6},{6,7},{7,8},{8,9},{9,10},{10,1... | collective-permute-start | bytes 96776 | tf_op jit(solution)/shard_map/ppermute | solution.py:21
  161.8 1.4 fusion.156
  163.2 105.5 %all-reduce.2 = (f32[384]{0:T(512)}, f32[384]{0:T(512)}, f32[384]{0:T(512)}, f32[1280]{0:T(1024)}, f32[384]{0:T(512)}, /*index=5*/f32[384]{0:T(512)}) all-reduce(f32[384]{0:T(512)} %get-tuple-element.66, f32[384]{0:T(512)S(1)} %copy-done.93, f32[384]{0:T(512)} %get-tuple-element.65, ...), channel_id=1, replica_groups=mesh['row'=32,'col'=16] {'row','col'}, use_global_device_ids=true, to_apply=%region_62.0 | all-reduce | flops 3200 | bytes 25600 | tf_op jit(solution)/shard_map/psum | solution.py:197
  269.2 2.6 fusion.106
  271.8 165.1 %all-reduce.6.cloned.1.call-done = (f32[491520]{0:T(1024)}, f32[491520]{0:T(1024)}, f32[49,384]{1,0:T(8,128)}) async-done(((f32[491520]{0:T(1024)}, f32[491520]{0:T(1024)}, f32[49,384]{1,0:T(8,128)}), (f32[491520]{0:T(1024)}, f32[491520]{0:T(1024)}, f32[49,384]{1,0:T(8,128)})) %all-reduce.6.cloned.1.call-update) | async-done | bytes 4007440
  436.9 1.4 dynamic-slice
  438.3 1.4 dynamic-slice.1
  439.6 1.5 copy.69
  (389 shorter events, 16.9 us)
Async XLA Ops:
  7.2 429.7 %all-reduce.6.cloned.1.call-start = ((), (), s32[]{:S(2)}) async-start(), calls=%async_computation | async-start | bytes 8036352
  101.8 7.4 %collective-permute-start.1 = (bf16[3,16,384]{2,1,0:T(8,128)(2,1)S(1)}, bf16[3,16,384]{2,1,0:T(8,128)(2,1)S(1)}, u32[]{:S(2)}, u32[]{:S(2)}) collective-permute-start(bf16[3,16,384]{2,1,0:T(8,128)(2,1)S(1)} %bitcast.131), channel_id=1, source_target_pairs={{16,0},{32,16},{48,32},{64,48},{80,64},{96,80},{112,96},{128,112},... | collective-permute-start | bytes 110600 | tf_op jit(solution)/shard_map/ppermute | solution.py:22
  103.9 5.3 %collective-permute-start = (bf16[3,16,384]{2,1,0:T(8,128)(2,1)S(1)}, bf16[3,16,384]{2,1,0:T(8,128)(2,1)S(1)}, u32[]{:S(2)}, u32[]{:S(2)}) collective-permute-start(bf16[3,16,384]{2,1,0:T(8,128)(2,1)S(1)} %bitcast.130), channel_id=1, source_target_pairs={{0,16},{16,32},{32,48},{48,64},{64,80},{80,96},{96,112},{112,128},... | collective-permute-start | bytes 110600 | tf_op jit(solution)/shard_map/ppermute | solution.py:21
  109.3 5.2 %collective-permute-start.2 = (bf16[14,3,384]{2,1,0:T(4,128)(2,1)S(1)}, bf16[14,3,384]{2,1,0:T(4,128)(2,1)S(1)}, u32[]{:S(2)}, u32[]{:S(2)}) collective-permute-start(bf16[14,3,384]{2,1,0:T(4,128)(2,1)S(1)} %get-tuple-element.139), channel_id=1, source_target_pairs={{0,1},{1,2},{2,3},{3,4},{4,5},{5,6},{6,7},{7,8},{8,9},{9,10},{10,1... | collective-permute-start | bytes 96776 | tf_op jit(solution)/shard_map/ppermute | solution.py:21
  112.8 8.8 %collective-permute-start.3 = (bf16[14,3,384]{2,1,0:T(4,128)(2,1)S(1)}, bf16[14,3,384]{2,1,0:T(4,128)(2,1)S(1)}, u32[]{:S(2)}, u32[]{:S(2)}) collective-permute-start(bf16[14,3,384]{2,1,0:T(4,128)(2,1)S(1)} %get-tuple-element.140), channel_id=1, source_target_pairs={{1,0},{2,1},{3,2},{4,3},{5,4},{6,5},{7,6},{8,7},{9,8},{10,9},{11,1... | collective-permute-start | bytes 96776 | tf_op jit(solution)/shard_map/ppermute | solution.py:22
  144.4 124.4 %copy-start.19 = (f32[384]{0:T(512)S(1)}, f32[384]{0:T(512)}, u32[]{:S(2)}) copy-start(f32[384]{0:T(512)} %copy-done.18) | copy-start | bytes 4612
  144.4 124.4 %copy-start.21 = (f32[384]{0:T(512)S(1)}, f32[384]{0:T(512)}, u32[]{:S(2)}) copy-start(f32[384]{0:T(512)} %copy-done.20) | copy-start | bytes 4612
  144.4 124.4 %copy-start.23 = (f32[384]{0:T(512)S(1)}, f32[384]{0:T(512)}, u32[]{:S(2)}) copy-start(f32[384]{0:T(512)} %copy-done.22) | copy-start | bytes 4612
  144.4 124.4 %copy-start.25 = (f32[384]{0:T(512)S(1)}, f32[384]{0:T(512)}, u32[]{:S(2)}) copy-start(f32[384]{0:T(512)} %copy-done.24) | copy-start | bytes 4612
  144.5 124.4 %copy-start.27 = (f32[384]{0:T(512)S(1)}, f32[384]{0:T(512)}, u32[]{:S(2)}) copy-start(f32[384]{0:T(512)} %copy-done.26) | copy-start | bytes 4612
  144.5 124.4 %copy-start.29 = (f32[384]{0:T(512)S(1)}, f32[384]{0:T(512)}, u32[]{:S(2)}) copy-start(f32[384]{0:T(512)} %copy-done.28) | copy-start | bytes 4612
  144.5 124.4 %copy-start.31 = (f32[384]{0:T(512)S(1)}, f32[384]{0:T(512)}, u32[]{:S(2)}) copy-start(f32[384]{0:T(512)} %copy-done.30) | copy-start | bytes 4612
  144.5 124.4 %copy-start.33 = (f32[384]{0:T(512)S(1)}, f32[384]{0:T(512)}, u32[]{:S(2)}) copy-start(f32[384]{0:T(512)} %copy-done.32) | copy-start | bytes 4612
  144.5 124.4 %copy-start.35 = (f32[384]{0:T(512)S(1)}, f32[384]{0:T(512)}, u32[]{:S(2)}) copy-start(f32[384]{0:T(512)} %copy-done.34) | copy-start | bytes 4612
  144.5 124.4 %copy-start.37 = (f32[384]{0:T(512)S(1)}, f32[384]{0:T(512)}, u32[]{:S(2)}) copy-start(f32[384]{0:T(512)} %copy-done.36) | copy-start | bytes 4612
  144.5 124.4 %copy-start.39 = (f32[384]{0:T(512)S(1)}, f32[384]{0:T(512)}, u32[]{:S(2)}) copy-start(f32[384]{0:T(512)} %copy-done.38) | copy-start | bytes 4612
  144.5 124.4 %copy-start.41 = (f32[384]{0:T(512)S(1)}, f32[384]{0:T(512)}, u32[]{:S(2)}) copy-start(f32[384]{0:T(512)} %copy-done.40) | copy-start | bytes 4612
  144.5 124.4 %copy-start.43 = (f32[384]{0:T(512)S(1)}, f32[384]{0:T(512)}, u32[]{:S(2)}) copy-start(f32[384]{0:T(512)} %copy-done.42) | copy-start | bytes 4612
  144.5 124.4 %copy-start.45 = (f32[384]{0:T(512)S(1)}, f32[384]{0:T(512)}, u32[]{:S(2)}) copy-start(f32[384]{0:T(512)} %copy-done.44) | copy-start | bytes 4612
  144.6 124.4 %copy-start.47 = (f32[384]{0:T(512)S(1)}, f32[384]{0:T(512)}, u32[]{:S(2)}) copy-start(f32[384]{0:T(512)} %copy-done.46) | copy-start | bytes 4612
  144.8 6.8 %collective-permute-start.5 = (bf16[3,16,384]{2,1,0:T(8,128)(2,1)S(1)}, bf16[3,16,384]{2,1,0:T(8,128)(2,1)S(1)}, u32[]{:S(2)}, u32[]{:S(2)}) collective-permute-start(bf16[3,16,384]{2,1,0:T(8,128)(2,1)S(1)} %get-tuple-element.144), channel_id=1, source_target_pairs={{16,0},{32,16},{48,32},{64,48},{80,64},{96,80},{112,96},{128,112},... | collective-permute-start | bytes 110600 | tf_op jit(solution)/shard_map/ppermute | solution.py:22
  147.1 5.5 %collective-permute-start.4 = (bf16[3,16,384]{2,1,0:T(8,128)(2,1)S(1)}, bf16[3,16,384]{2,1,0:T(8,128)(2,1)S(1)}, u32[]{:S(2)}, u32[]{:S(2)}) collective-permute-start(bf16[3,16,384]{2,1,0:T(8,128)(2,1)S(1)} %get-tuple-element.143), channel_id=1, source_target_pairs={{0,16},{16,32},{32,48},{48,64},{64,80},{80,96},{96,112},{112,128},... | collective-permute-start | bytes 110600 | tf_op jit(solution)/shard_map/ppermute | solution.py:21
  152.6 116.1 %collective-permute-start.7 = (bf16[14,3,384]{2,1,0:T(4,128)(2,1)S(1)}, bf16[14,3,384]{2,1,0:T(4,128)(2,1)S(1)}, u32[]{:S(2)}, u32[]{:S(2)}) collective-permute-start(bf16[14,3,384]{2,1,0:T(4,128)(2,1)S(1)} %get-tuple-element.136), channel_id=1, source_target_pairs={{1,0},{2,1},{3,2},{4,3},{5,4},{6,5},{7,6},{8,7},{9,8},{10,9},{11,1... | collective-permute-start | bytes 96776 | tf_op jit(solution)/shard_map/ppermute | solution.py:22
  153.9 114.8 %collective-permute-start.6 = (bf16[14,3,384]{2,1,0:T(4,128)(2,1)S(1)}, bf16[14,3,384]{2,1,0:T(4,128)(2,1)S(1)}, u32[]{:S(2)}, u32[]{:S(2)}) collective-permute-start(bf16[14,3,384]{2,1,0:T(4,128)(2,1)S(1)} %get-tuple-element.135), channel_id=1, source_target_pairs={{0,1},{1,2},{2,3},{3,4},{4,5},{5,6},{6,7},{7,8},{8,9},{9,10},{10,1... | collective-permute-start | bytes 96776 | tf_op jit(solution)/shard_map/ppermute | solution.py:21
  (126 other events, 3838.9 us)
Sparse Core Ops, SparseCore 0:
  144.5 292.3 all-reduce.5
where the time goes:
time: 449 us; the launch traced here: 448 us
  blocking collectives  194 us (43%)
  waiting for transfers between devices  173 us (39%)
  starting transfers between devices  26.3 us (6%)
  local copies, waits for them, and re-layouts  17.6 us (4%)
  between operations  16.6 us (4%)
  other arithmetic  11.3 us (3%)
  matrix products  9.34 us (2%)
    unnamed x2, waiting for transfers between devices  165 us
    psum x1, blocking collectives, body(): lax.psum((kernel_grad, bias_grad, gain_grad, shift_grad, up_bias_grad, do...  106 us
    all_gather x1, blocking collectives, body(): value_piece = lax.all_gather(values, 'row', axis=0, tiled=True)  46.8 us
    all_gather x1, blocking collectives, body(): key_piece = lax.all_gather(keys, 'row', axis=0, tiled=True)  41.3 us
    ppermute x4, starting transfers between devices, extended(): before = lax.ppermute(last, axis, up)  19.3 us
  transfers between devices with their start and end apart: 9, of which 3 were waited for; matrix products, arithmetic and copies ran while one was open for 1% of the time, Pallas kernels for 0%

commit v1 on v0

--- a/solution.py
+++ b/solution.py
@@ -1,7 +1,12 @@
 import jax
 import jax.numpy as jnp
 from jax import lax
-from jax.sharding import PartitionSpec as P
+from jax.sharding import Mesh, PartitionSpec as P
+
+ROW = ("yl", "x", "c")
+COL = ("z", "yh")
+YZ = ("yl", "z", "yh")
+XC = ("x", "c")
 
 POOL = 8
 TS = 4
@@ -79,6 +84,54 @@
         jnp.sum(cotan * branch, axis=0),
     )
     return (branch, d_spatial, grad_up, grad_down, smalls)
+
+
+def reduce_all(grad_up, grad_down, smalls):
+    n_yl, n_x, n_c = (lax.axis_size(a) for a in ROW)
+    n_col = lax.axis_size(COL)
+    n_yz = n_yl * n_col
+    n_all = n_yz * n_x * n_c
+    share = grad_up.size // n_all
+    rows = 2 * share // 128
+    record = jnp.concatenate(
+        [
+            grad_up.astype(jnp.bfloat16).reshape(n_all, share),
+            grad_down.astype(jnp.bfloat16).reshape(n_all, share),
+        ],
+        axis=1,
+    )
+    record = record.reshape(n_yl, n_x, n_c, n_col * rows, 128).transpose(2, 1, 0, 3, 4)
+    record = record.reshape(n_c, n_x, n_yz * rows, 128)
+    flat = jnp.concatenate([v.reshape(-1) for v in smalls])
+    chunk = n_c * n_x * 128
+    small_rows = -(-flat.size // chunk)
+    small_pad = -(-small_rows // 8) * 8
+    flat = jnp.pad(flat, (0, small_rows * chunk - flat.size))
+    flat = flat.reshape(n_c, n_x, small_rows, 128)
+    flat = jnp.pad(flat, ((0, 0), (0, 0), (0, small_pad - small_rows), (0, 0)))
+    both = jnp.concatenate([record, flat.astype(jnp.bfloat16)], axis=2)
+    core = lax.axis_index("c")
+    other = lax.dynamic_index_in_dim(both, 1 - core, 0, keepdims=False)
+    mine = lax.dynamic_index_in_dim(both, core, 0, keepdims=False)
+    got = lax.ppermute(other, "c", [(0, 1), (1, 0)])
+    part = (mine.astype(jnp.float32) + got.astype(jnp.float32)).astype(jnp.bfloat16)
+    part = lax.all_to_all(part, "x", 0, 0, tiled=True)
+    part = jnp.sum(part.astype(jnp.float32), axis=0).astype(jnp.bfloat16)
+    big = part[: n_yz * rows].reshape(n_yz, rows, 128)
+    small = jnp.broadcast_to(part[n_yz * rows :], (n_yz, small_pad, 128))
+    part = jnp.concatenate([big, small], axis=1)
+    part = lax.all_to_all(part, YZ, 0, 0, tiled=True)
+    part = jnp.sum(part.astype(jnp.float32), axis=0)
+    share_up = part[:rows].reshape(-1)[:share]
+    share_down = part[:rows].reshape(-1)[share:]
+    small = jnp.broadcast_to(part[rows:], (n_x * n_c, small_pad, 128))
+    small = lax.all_to_all(small, XC, 0, 0, tiled=True)
+    small = small[:, :small_rows].reshape(n_x, n_c, -1).transpose(1, 0, 2).reshape(-1)
+    outs, at = [], 0
+    for v in smalls:
+        outs.append(small[at : at + v.size].reshape(v.shape))
+        at += v.size
+    return share_up, share_down, tuple(outs)
 
 
 def body(
@@ -109,13 +162,16 @@
     pooled = jnp.mean(
         features.reshape(rows_here // POOL, POOL, cols_here, chans), axis=1, dtype=jnp.float32
     )
-    flat_pool = pooled.astype(jnp.bfloat16).reshape(-1, chans)
+    n_row = lax.axis_size(ROW)
+    pooled = pooled.astype(jnp.bfloat16).reshape(1, cols_here, chans)
+    pooled = lax.all_to_all(
+        jnp.broadcast_to(pooled, (n_row, cols_here, chans)), ROW, 0, 0, tiled=True
+    )
+    flat_pool = pooled.reshape(-1, chans)
     keys = head_normed(jnp.dot(flat_pool, w_key, preferred_element_type=jnp.float32), heads)
-    keys = keys.astype(jnp.bfloat16).reshape(rows_here // POOL, cols_here, heads, head_width)
+    key_piece = keys.astype(jnp.bfloat16).reshape(n_row, cols_here, heads, head_width)
     values = jnp.dot(flat_pool, w_value, preferred_element_type=jnp.float32)
-    values = values.astype(jnp.bfloat16).reshape(rows_here // POOL, cols_here, heads, head_width)
-    key_piece = lax.all_gather(keys, "row", axis=0, tiled=True)
-    value_piece = lax.all_gather(values, "row", axis=0, tiled=True)
+    value_piece = values.astype(jnp.bfloat16).reshape(n_row, cols_here, heads, head_width)
     scores = jnp.einsum("iwhd,jwhd->iwhj", query, key_piece, preferred_element_type=jnp.float32)
     weight = jnp.exp(scores * logit_scale[:, None])
     numer = jnp.einsum(
@@ -130,7 +186,7 @@
         attended, w_out, preferred_element_type=jnp.float32
     )
     mixed = mixed.astype(jnp.bfloat16).reshape(rows_here, cols_here, chans)
-    padded = extended(mixed, (("row", 0), ("col", 1)), 3)
+    padded = extended(mixed, ((ROW, 0), (COL, 1)), 3)
     spatial = jnp.broadcast_to(dw_bias, (rows_here, cols_here, chans))
     for row_off in range(7):
         for col_off in range(7):
@@ -168,7 +224,7 @@
     branch_full = branch.reshape(rows_here, cols_here, chans)
     d_full = d_spatial.reshape(rows_here, cols_here, chans)
     output = (mixed.astype(jnp.float32) + layer_scale * branch_full).astype(jnp.bfloat16)
-    d_padded = extended(d_full.astype(jnp.bfloat16), (("row", 0), ("col", 1)), 3).astype(
+    d_padded = extended(d_full.astype(jnp.bfloat16), ((ROW, 0), (COL, 1)), 3).astype(
         d_full.dtype
     )
     grad_mixed = cot_full
@@ -194,56 +250,40 @@
     kernel_grad = jnp.stack(taps, axis=0)
     bias_grad = jnp.sum(d_full, axis=(0, 1))
     gain_grad, shift_grad, up_bias_grad, down_bias_grad, scale_grad = smalls
-    summed = lax.psum(
+    up_share, down_share, smalls = reduce_all(
+        grad_up,
+        grad_down,
         (kernel_grad, bias_grad, gain_grad, shift_grad, up_bias_grad, down_bias_grad, scale_grad),
-        ("row", "col"),
-    )
-    final = (
-        lax.psum_scatter(grad_up.reshape(-1), ("row", "col"), scatter_dimension=0, tiled=True),
-        lax.psum_scatter(grad_down.reshape(-1), ("row", "col"), scatter_dimension=0, tiled=True),
-    )
-    up_share = final[0]
-    down_share = final[1]
-    return (
-        output,
-        grad_mixed,
-        up_share,
-        down_share,
-        summed[0],
-        summed[1],
-        summed[2],
-        summed[3],
-        summed[4],
-        summed[5],
-        summed[6],
-    )
+    )
+    return (output, grad_mixed, up_share, down_share) + smalls
 
 
 def solution(mesh):
+    mesh = Mesh(mesh.devices.reshape(4, 4, 2, 8, 2), ROW + COL)
     in_specs = (
-        P("row", "col", None),
-        P(),
-        P(),
-        P(),
-        P(),
-        P(),
-        P(),
-        P(),
-        P(),
-        P(),
-        P(),
-        P(),
-        P(),
-        P(),
-        P(),
-        P("row", "col", None),
-        P("row", "col", None),
+        P(ROW, COL, None),
+        P(),
+        P(),
+        P(),
+        P(),
+        P(),
+        P(),
+        P(),
+        P(),
+        P(),
+        P(),
+        P(),
+        P(),
+        P(),
+        P(),
+        P(ROW, COL, None),
+        P(ROW, COL, None),
     )
     out_specs = (
-        P("row", "col", None),
-        P("row", "col", None),
-        P(("row", "col")),
-        P(("row", "col")),
+        P(ROW, COL, None),
+        P(ROW, COL, None),
+        P(ROW + COL),
+        P(ROW + COL),
         P(),
         P(),
         P(),

time: 449 us -> 171 us (0.38)
  the two profiles are of different devices: /device:TPU:1 before, /device:TPU:64 now
where the time goes in v1:
time: 171 us; the launch traced here: 170 us
  starting transfers between devices  69 us (40%)
  waiting for transfers between devices  30.5 us (18%)
  local copies, waits for them, and re-layouts  24.7 us (14%)
  blocking collectives  20.7 us (12%)
  other arithmetic  12.6 us (7%)
  matrix products  9.96 us (6%)
  between operations  2.71 us (2%)
    all_to_all x1, blocking collectives, reduce_all(): part = lax.all_to_all(part, 'x', 0, 0, tiled=True)  20.7 us
    all_to_all x1, starting transfers between devices, reduce_all(): part = lax.all_to_all(part, YZ, 0, 0, tiled=True)  17.3 us
    ppermute x4, starting transfers between devices, extended(): after = lax.ppermute(leading, axis, down)  15.5 us
    ppermute x4, starting transfers between devices, extended(): before = lax.ppermute(last, axis, up)  13.6 us
    all_to_all x1, starting transfers between devices, reduce_all(): small = lax.all_to_all(small, XC, 0, 0, tiled=True)  12.4 us
    all_to_all x1, waiting for transfers between devices, body(): lax.all_to_all(jnp.broadcast_to(pooled, (n_row, cols_here, chans)), ROW,...  9.3 us
    ppermute x4, waiting for transfers between devices, extended(): after = lax.ppermute(leading, axis, down)  8.9 us
    all_to_all x1, starting transfers between devices, body(): lax.all_to_all(jnp.broadcast_to(pooled, (n_row, cols_here, chans)), ROW,...  7.73 us
  transfers between devices with their start and end apart: 12, of which 8 were waited for; matrix products, arithmetic and copies ran while one was open for 4% of the time, Pallas kernels for 0%

profile of v1, /device:TPU:64, one launch (start us, length us, event | category | flops | bytes accessed | tf_op | source)
XLA Modules:
  0.0 170.2 jit_solution(2533226022935101815)
XLA Ops:
  2.5 7.7 %all-to-all-start = ((bf16[32,16,384]{2,1,0:T(8,128)(2,1)}), bf16[32,16,384]{2,1,0:T(8,128)(2,1)S(1)}, u32[]{:S(2)}, u32[]{:S(2)}) async-start(bf16[32,16,384]{2,1,0:T(8,128)(2,1)} %broadcast_in_dim.10), calls=%async_computation | async-start | bytes 786432 | tf_op jit(solution)/shard_map/all_to_all | solution.py:167
  14.4 9.3 %all-to-all-done = bf16[32,16,384]{2,1,0:T(8,128)(2,1)S(1)} async-done(((bf16[32,16,384]{2,1,0:T(8,128)(2,1)}), bf16[32,16,384]{2,1,0:T(8,128)(2,1)S(1)}, u32[]{:S(2)}, u32[]{:S(2)}) %all-to-all-start) | async-done | bytes 393248 | tf_op jit(solution)/shard_map/all_to_all | solution.py:167
  26.4 1.7 %fusion.181 = (f32[8,16,6]{0,2,1:T(8,128)S(1)}, bf16[8,16,6,32]{3,0,2,1:T(8,128)(2,1)S(1)}) fusion(f32[6]{0:T(128)S(1)} %copy-done.87, bf16[8,16,6,64]{3,1,0,2:T(8,128)(2,1)S(1)} %bitcast.146, bf16[32,16,6,64]{3,1,0,2:T(8,128)(2,1)} %bitcast.143), kind=kOutput, calls=%fused_computation.438 | convolution fusion | flops 3218688 | bytes 543768 | tf_op jit(solution)/shard_map/iwhd,jwhd->iwhj/dot_general | solution.py:175
  30.8 3.1 %collective-permute-start = (bf16[3,16,384]{2,1,0:T(8,128)(2,1)S(1)}, bf16[3,16,384]{2,1,0:T(8,128)(2,1)S(1)}, u32[]{:S(2)}, u32[]{:S(2)}) collective-permute-start(bf16[3,16,384]{2,1,0:T(8,128)(2,1)S(1)} %bitcast.147), channel_id=1, source_target_pairs={{0,16},{16,32},{32,48},{48,64},{64,80},{80,96},{96,112},{112,128},... | collective-permute-start | bytes 110600 | tf_op jit(solution)/shard_map/ppermute | solution.py:26
  34.8 5.0 %collective-permute-start.2 = (bf16[14,3,384]{2,1,0:T(4,128)(2,1)S(1)}, bf16[14,3,384]{2,1,0:T(4,128)(2,1)S(1)}, u32[]{:S(2)}, u32[]{:S(2)}) collective-permute-start(bf16[14,3,384]{2,1,0:T(4,128)(2,1)S(1)} %get-tuple-element.130), channel_id=1, source_target_pairs={{0,1},{1,2},{2,3},{3,4},{4,5},{5,6},{6,7},{7,8},{8,9},{9,10},{10,1... | collective-permute-start | bytes 96776 | tf_op jit(solution)/shard_map/ppermute | solution.py:26
  39.9 5.6 %collective-permute-start.3 = (bf16[14,3,384]{2,1,0:T(4,128)(2,1)S(1)}, bf16[14,3,384]{2,1,0:T(4,128)(2,1)S(1)}, u32[]{:S(2)}, u32[]{:S(2)}) collective-permute-start(bf16[14,3,384]{2,1,0:T(4,128)(2,1)S(1)} %get-tuple-element.131), channel_id=1, source_target_pairs={{1,0},{2,1},{3,2},{4,3},{5,4},{6,5},{7,6},{8,7},{9,8},{10,9},{11,1... | collective-permute-start | bytes 96776 | tf_op jit(solution)/shard_map/ppermute | solution.py:27
  46.0 3.7 %collective-permute-done.3 = bf16[14,3,384]{2,1,0:T(4,128)(2,1)S(1)} collective-permute-done((bf16[14,3,384]{2,1,0:T(4,128)(2,1)S(1)}, bf16[14,3,384]{2,1,0:T(4,128)(2,1)S(1)}, u32[]{:S(2)}, u32[]{:S(2)}) %collective-permute-start.3) | collective-permute-done | bytes 32288 | tf_op jit(solution)/shard_map/ppermute | solution.py:27
  50.1 1.8 %fusion.175 = (f32[8,16]{1,0:T(8,128)S(1)}, f32[8,16,384]{2,1,0:T(8,128)S(1)}) fusion(f32[384]{0:T(512)S(1)} %get-tuple-element.121, bf16[14,19,384]{2,1,0:T(8,128)(2,1)S(1)} %get-tuple-element.129, f32[384]{0:T(512)S(1)} %get-tuple-element.122, f32[384]{0:T(512)S(1)} %copy-done.19, f32[384]{0:T(512)S(1)} %copy-done.21, ...), kind=kLoop, calls=%fused_computation.433 | loop fusion | flops 7569280 | bytes 4574720 | tf_op jit(solution)/shard_map/reduce_sum | solution.py:49
  62.7 3.3 %reshape.248 = bf16[512,960]{1,0:T(8,128)(2,1)} reshape(bf16[1280,384]{1,0:T(8,128)(2,1)} %convolution_convert_fusion) | data formatting | bytes 1966080 | tf_op jit(solution)/shard_map/reshape | solution.py:99
  66.0 2.6 %reshape.247 = bf16[512,960]{1,0:T(8,128)(2,1)} reshape(bf16[384,1280]{1,0:T(8,128)(2,1)S(1)} %convolution_convert_fusion.1) | data formatting | bytes 1966080 | tf_op jit(solution)/shard_map/reshape | solution.py:98
  68.7 2.2 %pad_maximum_fusion = bf16[512,1920]{1,0:T(8,128)(2,1)S(1)} fusion(bf16[512,960]{1,0:T(8,128)(2,1)} %reshape.248, bf16[512,960]{1,0:T(8,128)(2,1)} %reshape.247), kind=kLoop, calls=%fused_computation.9 | loop fusion | flops 3932160 | bytes 3932160 | tf_op jit(solution)/shard_map/concatenate | solution.py:96
  70.8 3.5 %reshape.249 = bf16[4,4,2,240,128]{4,3,2,1,0:T(8,128)(2,1)} reshape(bf16[512,1920]{1,0:T(8,128)(2,1)S(1)} %pad_maximum_fusion) | data formatting | bytes 3932160 | tf_op jit(solution)/shard_map/reshape | solution.py:103
  77.2 2.5 %collective-permute-start.8 = (bf16[4,984,128]{2,1,0:T(8,128)(2,1)}, bf16[4,984,128]{2,1,0:T(8,128)(2,1)}, u32[]{:S(2)}, u32[]{:S(2)}) collective-permute-start(bf16[4,984,128]{2,1,0:T(8,128)(2,1)} %dynamic-slice_bitcast_fusion), channel_id=1, source_target_pairs={{0,16},{16,0},{1,17},{17,1},{2,18},{18,2},{3,19},{19,3},{4,20},{20... | collective-permute-start | bytes 3022856 | tf_op jit(solution)/shard_map/ppermute | solution.py:116
  79.7 2.5 %collective-permute-done.8 = bf16[4,984,128]{2,1,0:T(8,128)(2,1)} collective-permute-done((bf16[4,984,128]{2,1,0:T(8,128)(2,1)}, bf16[4,984,128]{2,1,0:T(8,128)(2,1)}, u32[]{:S(2)}, u32[]{:S(2)}) %collective-permute-start.8) | collective-permute-done | bytes 1007648 | tf_op jit(solution)/shard_map/ppermute | solution.py:116
  83.7 20.7 %all_to_all.20 = bf16[4,984,128]{2,1,0:T(8,128)(2,1)S(1)} all-to-all(bf16[4,984,128]{2,1,0:T(8,128)(2,1)S(1)} %fusion.2), channel_id=1, replica_groups=mesh['yl'=4,'x'=4,'c'=2,'z'=8,'yh'=2] {'x'}, dimensions={0} | all-to-all | bytes 2015232 | tf_op jit(solution)/shard_map/all_to_all | solution.py:118
  106.3 17.3 %all-to-all-start.2 = ((bf16[64,39,128]{2,1,0:T(8,128)(2,1)}), bf16[64,39,128]{2,1,0:T(8,128)(2,1)S(1)}, u32[]{:S(2)}, u32[]{:S(2)}) async-start(bf16[64,39,128]{2,1,0:T(8,128)(2,1)} %pad_maximum_fusion.1), calls=%async_computation.2 | async-start | bytes 1310720 | tf_op jit(solution)/shard_map/all_to_all | solution.py:123
  124.9 3.0 %collective-permute-start.4 = (bf16[3,16,384]{2,1,0:T(8,128)(2,1)S(1)}, bf16[3,16,384]{2,1,0:T(8,128)(2,1)S(1)}, u32[]{:S(2)}, u32[]{:S(2)}) collective-permute-start(bf16[3,16,384]{2,1,0:T(8,128)(2,1)S(1)} %get-tuple-element.134), channel_id=1, source_target_pairs={{0,16},{16,32},{32,48},{48,64},{64,80},{80,96},{96,112},{112,128},... | collective-permute-start | bytes 110600 | tf_op jit(solution)/shard_map/ppermute | solution.py:26
  128.8 7.3 %collective-permute-start.7 = (bf16[14,3,384]{2,1,0:T(4,128)(2,1)S(1)}, bf16[14,3,384]{2,1,0:T(4,128)(2,1)S(1)}, u32[]{:S(2)}, u32[]{:S(2)}) collective-permute-start(bf16[14,3,384]{2,1,0:T(4,128)(2,1)S(1)} %get-tuple-element.127), channel_id=1, source_target_pairs={{1,0},{2,1},{3,2},{4,3},{5,4},{6,5},{7,6},{8,7},{9,8},{10,9},{11,1... | collective-permute-start | bytes 96776 | tf_op jit(solution)/shard_map/ppermute | solution.py:27
  136.1 2.5 %collective-permute-start.6 = (bf16[14,3,384]{2,1,0:T(4,128)(2,1)S(1)}, bf16[14,3,384]{2,1,0:T(4,128)(2,1)S(1)}, u32[]{:S(2)}, u32[]{:S(2)}) collective-permute-start(bf16[14,3,384]{2,1,0:T(4,128)(2,1)S(1)} %get-tuple-element.126), channel_id=1, source_target_pairs={{0,1},{1,2},{2,3},{3,4},{4,5},{5,6},{6,7},{7,8},{8,9},{9,10},{10,1... | collective-permute-start | bytes 96776 | tf_op jit(solution)/shard_map/ppermute | solution.py:26
  138.6 5.2 %collective-permute-done.7 = bf16[14,3,384]{2,1,0:T(4,128)(2,1)S(1)} collective-permute-done((bf16[14,3,384]{2,1,0:T(4,128)(2,1)S(1)}, bf16[14,3,384]{2,1,0:T(4,128)(2,1)S(1)}, u32[]{:S(2)}, u32[]{:S(2)}) %collective-permute-start.7) | collective-permute-done | bytes 32288 | tf_op jit(solution)/shard_map/ppermute | solution.py:27
  143.8 3.0 %collective-permute-done.6 = bf16[14,3,384]{2,1,0:T(4,128)(2,1)S(1)} collective-permute-done((bf16[14,3,384]{2,1,0:T(4,128)(2,1)S(1)}, bf16[14,3,384]{2,1,0:T(4,128)(2,1)S(1)}, u32[]{:S(2)}, u32[]{:S(2)}) %collective-permute-start.6) | collective-permute-done | bytes 32288 | tf_op jit(solution)/shard_map/ppermute | solution.py:26
  147.3 1.9 %fusion.109 = f32[8,16,384]{2,1,0:T(8,128)} fusion(f32[14,22,384]{2,1,0:T(8,128)S(1)} %maximum_convert_fusion, bf16[8,16,384]{2,1,0:T(8,128)(2,1)S(1)} %copy-done.3, f32[384]{0:T(512)S(1)} %copy-done.74, f32[384]{0:T(512)S(1)} %copy-done.76, f32[384]{0:T(512)S(1)} %copy-done.20, f32[384]{0:T(512)S(1)} %copy-done.22, f32[384]{0:T(512)S(1)} %copy-done.24, ...), kind=kLoop, calls=%fused_computation.231 | loop fusion | flops 4866048 | bytes 10003968 | tf_op jit(solution)/shard_map/add | solution.py:235
  150.0 12.4 %all-to-all-start.3 = ((f32[8,24,128]{2,1,0:T(8,128)}), f32[8,24,128]{2,1,0:T(8,128)S(1)}, u32[]{:S(2)}, u32[]{:S(2)}) async-start(f32[8,24,128]{2,1,0:T(8,128)} %broadcast_in_dim.14), calls=%async_computation.3 | async-start | bytes 196608 | tf_op jit(solution)/shard_map/all_to_all | solution.py:128
  163.0 5.1 %all-to-all-done.3 = f32[8,24,128]{2,1,0:T(8,128)S(1)} async-done(((f32[8,24,128]{2,1,0:T(8,128)}), f32[8,24,128]{2,1,0:T(8,128)S(1)}, u32[]{:S(2)}, u32[]{:S(2)}) %all-to-all-start.3) | async-done | bytes 98336 | tf_op jit(solution)/shard_map/all_to_all | solution.py:128
  (322 shorter events, 34.4 us)
Async XLA Ops:
  0.6 52.2 %copy-start = (bf16[1280,384]{1,0:T(8,128)(2,1)S(1)}, bf16[1280,384]{1,0:T(8,128)(2,1)}, u32[]{:S(2)}) copy-start(bf16[1280,384]{1,0:T(8,128)(2,1)} %param.29) | copy-start | bytes 2949124
  2.5 21.2 %all-to-all-start = ((bf16[32,16,384]{2,1,0:T(8,128)(2,1)}), bf16[32,16,384]{2,1,0:T(8,128)(2,1)S(1)}, u32[]{:S(2)}, u32[]{:S(2)}) async-start(bf16[32,16,384]{2,1,0:T(8,128)(2,1)} %broadcast_in_dim.10), calls=%async_computation | async-start | bytes 786432 | tf_op jit(solution)/shard_map/all_to_all | solution.py:167
  29.5 4.6 %collective-permute-start.1 = (bf16[3,16,384]{2,1,0:T(8,128)(2,1)S(1)}, bf16[3,16,384]{2,1,0:T(8,128)(2,1)S(1)}, u32[]{:S(2)}, u32[]{:S(2)}) collective-permute-start(bf16[3,16,384]{2,1,0:T(8,128)(2,1)S(1)} %bitcast.148), channel_id=1, source_target_pairs={{16,0},{32,16},{48,32},{64,48},{80,64},{96,80},{112,96},{128,112},... | collective-permute-start | bytes 110600 | tf_op jit(solution)/shard_map/ppermute | solution.py:27
  30.8 3.9 %collective-permute-start = (bf16[3,16,384]{2,1,0:T(8,128)(2,1)S(1)}, bf16[3,16,384]{2,1,0:T(8,128)(2,1)S(1)}, u32[]{:S(2)}, u32[]{:S(2)}) collective-permute-start(bf16[3,16,384]{2,1,0:T(8,128)(2,1)S(1)} %bitcast.147), channel_id=1, source_target_pairs={{0,16},{16,32},{32,48},{48,64},{64,80},{80,96},{96,112},{112,128},... | collective-permute-start | bytes 110600 | tf_op jit(solution)/shard_map/ppermute | solution.py:26
  34.8 11.2 %collective-permute-start.2 = (bf16[14,3,384]{2,1,0:T(4,128)(2,1)S(1)}, bf16[14,3,384]{2,1,0:T(4,128)(2,1)S(1)}, u32[]{:S(2)}, u32[]{:S(2)}) collective-permute-start(bf16[14,3,384]{2,1,0:T(4,128)(2,1)S(1)} %get-tuple-element.130), channel_id=1, source_target_pairs={{0,1},{1,2},{2,3},{3,4},{4,5},{5,6},{6,7},{7,8},{8,9},{9,10},{10,1... | collective-permute-start | bytes 96776 | tf_op jit(solution)/shard_map/ppermute | solution.py:26
  39.9 9.8 %collective-permute-start.3 = (bf16[14,3,384]{2,1,0:T(4,128)(2,1)S(1)}, bf16[14,3,384]{2,1,0:T(4,128)(2,1)S(1)}, u32[]{:S(2)}, u32[]{:S(2)}) collective-permute-start(bf16[14,3,384]{2,1,0:T(4,128)(2,1)S(1)} %get-tuple-element.131), channel_id=1, source_target_pairs={{1,0},{2,1},{3,2},{4,3},{5,4},{6,5},{7,6},{8,7},{9,8},{10,9},{11,1... | collective-permute-start | bytes 96776 | tf_op jit(solution)/shard_map/ppermute | solution.py:27
  77.2 5.1 %collective-permute-start.8 = (bf16[4,984,128]{2,1,0:T(8,128)(2,1)}, bf16[4,984,128]{2,1,0:T(8,128)(2,1)}, u32[]{:S(2)}, u32[]{:S(2)}) collective-permute-start(bf16[4,984,128]{2,1,0:T(8,128)(2,1)} %dynamic-slice_bitcast_fusion), channel_id=1, source_target_pairs={{0,16},{16,0},{1,17},{17,1},{2,18},{18,2},{3,19},{19,3},{4,20},{20... | collective-permute-start | bytes 3022856 | tf_op jit(solution)/shard_map/ppermute | solution.py:116
  104.9 42.1 %copy-start.10 = (f32[384]{0:T(512)S(1)}, f32[384]{0:T(512)}, u32[]{:S(2)}) copy-start(f32[384]{0:T(512)} %get-tuple-element.108) | copy-start | bytes 4612
  104.9 42.1 %copy-start.12 = (f32[384]{0:T(512)S(1)}, f32[384]{0:T(512)}, u32[]{:S(2)}) copy-start(f32[384]{0:T(512)} %get-tuple-element.109) | copy-start | bytes 4612
  104.9 42.1 %copy-start.14 = (f32[384]{0:T(512)S(1)}, f32[384]{0:T(512)}, u32[]{:S(2)}) copy-start(f32[384]{0:T(512)} %get-tuple-element.110) | copy-start | bytes 4612
  104.9 42.1 %copy-start.16 = (f32[384]{0:T(512)S(1)}, f32[384]{0:T(512)}, u32[]{:S(2)}) copy-start(f32[384]{0:T(512)} %get-tuple-element.111) | copy-start | bytes 4612
  104.9 42.1 %copy-start.18 = (f32[384]{0:T(512)S(1)}, f32[384]{0:T(512)}, u32[]{:S(2)}) copy-start(f32[384]{0:T(512)} %get-tuple-element.74) | copy-start | bytes 4612
  104.9 42.1 %copy-start.20 = (f32[384]{0:T(512)S(1)}, f32[384]{0:T(512)}, u32[]{:S(2)}) copy-start(f32[384]{0:T(512)} %get-tuple-element.75) | copy-start | bytes 4612
  104.9 42.1 %copy-start.22 = (f32[384]{0:T(512)S(1)}, f32[384]{0:T(512)}, u32[]{:S(2)}) copy-start(f32[384]{0:T(512)} %get-tuple-element.76) | copy-start | bytes 4612
  104.9 42.1 %copy-start.24 = (f32[384]{0:T(512)S(1)}, f32[384]{0:T(512)}, u32[]{:S(2)}) copy-start(f32[384]{0:T(512)} %get-tuple-element.77) | copy-start | bytes 4612
  104.9 42.1 %copy-start.26 = (f32[384]{0:T(512)S(1)}, f32[384]{0:T(512)}, u32[]{:S(2)}) copy-start(f32[384]{0:T(512)} %get-tuple-element.78) | copy-start | bytes 4612
  105.0 42.1 %copy-start.28 = (f32[384]{0:T(512)S(1)}, f32[384]{0:T(512)}, u32[]{:S(2)}) copy-start(f32[384]{0:T(512)} %get-tuple-element.79) | copy-start | bytes 4612
  105.0 42.1 %copy-start.30 = (f32[384]{0:T(512)S(1)}, f32[384]{0:T(512)}, u32[]{:S(2)}) copy-start(f32[384]{0:T(512)} %get-tuple-element.80) | copy-start | bytes 4612
  106.3 43.0 %all-to-all-start.2 = ((bf16[64,39,128]{2,1,0:T(8,128)(2,1)}), bf16[64,39,128]{2,1,0:T(8,128)(2,1)S(1)}, u32[]{:S(2)}, u32[]{:S(2)}) async-start(bf16[64,39,128]{2,1,0:T(8,128)(2,1)} %pad_maximum_fusion.1), calls=%async_computation.2 | async-start | bytes 1310720 | tf_op jit(solution)/shard_map/all_to_all | solution.py:123
  123.6 4.3 %collective-permute-start.5 = (bf16[3,16,384]{2,1,0:T(8,128)(2,1)S(1)}, bf16[3,16,384]{2,1,0:T(8,128)(2,1)S(1)}, u32[]{:S(2)}, u32[]{:S(2)}) collective-permute-start(bf16[3,16,384]{2,1,0:T(8,128)(2,1)S(1)} %get-tuple-element.135), channel_id=1, source_target_pairs={{16,0},{32,16},{48,32},{64,48},{80,64},{96,80},{112,96},{128,112},... | collective-permute-start | bytes 110600 | tf_op jit(solution)/shard_map/ppermute | solution.py:27
  124.9 3.9 %collective-permute-start.4 = (bf16[3,16,384]{2,1,0:T(8,128)(2,1)S(1)}, bf16[3,16,384]{2,1,0:T(8,128)(2,1)S(1)}, u32[]{:S(2)}, u32[]{:S(2)}) collective-permute-start(bf16[3,16,384]{2,1,0:T(8,128)(2,1)S(1)} %get-tuple-element.134), channel_id=1, source_target_pairs={{0,16},{16,32},{32,48},{48,64},{64,80},{80,96},{96,112},{112,128},... | collective-permute-start | bytes 110600 | tf_op jit(solution)/shard_map/ppermute | solution.py:26
  128.8 15.0 %collective-permute-start.7 = (bf16[14,3,384]{2,1,0:T(4,128)(2,1)S(1)}, bf16[14,3,384]{2,1,0:T(4,128)(2,1)S(1)}, u32[]{:S(2)}, u32[]{:S(2)}) collective-permute-start(bf16[14,3,384]{2,1,0:T(4,128)(2,1)S(1)} %get-tuple-element.127), channel_id=1, source_target_pairs={{1,0},{2,1},{3,2},{4,3},{5,4},{6,5},{7,6},{8,7},{9,8},{10,9},{11,1... | collective-permute-start | bytes 96776 | tf_op jit(solution)/shard_map/ppermute | solution.py:27
  136.1 10.7 %collective-permute-start.6 = (bf16[14,3,384]{2,1,0:T(4,128)(2,1)S(1)}, bf16[14,3,384]{2,1,0:T(4,128)(2,1)S(1)}, u32[]{:S(2)}, u32[]{:S(2)}) collective-permute-start(bf16[14,3,384]{2,1,0:T(4,128)(2,1)S(1)} %get-tuple-element.126), channel_id=1, source_target_pairs={{0,1},{1,2},{2,3},{3,4},{4,5},{5,6},{6,7},{7,8},{8,9},{9,10},{10,1... | collective-permute-start | bytes 96776 | tf_op jit(solution)/shard_map/ppermute | solution.py:26
  150.0 18.2 %all-to-all-start.3 = ((f32[8,24,128]{2,1,0:T(8,128)}), f32[8,24,128]{2,1,0:T(8,128)S(1)}, u32[]{:S(2)}, u32[]{:S(2)}) async-start(f32[8,24,128]{2,1,0:T(8,128)} %broadcast_in_dim.14), calls=%async_computation.3 | async-start | bytes 196608 | tf_op jit(solution)/shard_map/all_to_all | solution.py:128
  (77 other events, 1766.7 us)

commit v2 on v0

v2 whole, which is shorter than its diff:
```python
import numpy as np
import jax
import jax.numpy as jnp
from jax import lax
from jax.experimental import pallas as pl
from jax.experimental.pallas import tpu as pltpu
from jax.sharding import Mesh, PartitionSpec as P

ROW = ("yl", "x", "c")
COL = ("z", "yh")
YZ = ("yl", "z", "yh")
CX = ("c", "x")

F32 = jnp.float32
BF16 = jnp.bfloat16
EPS_NORM = 1e-06
GELU_SCALE = 0.7978845608028654
TS = 4
HB = 8
WB = 16
PIX = HB * WB
C = 384
HID = 1280
HEADS = 6
TILES_L = C // 128
N_YL, N_X, N_C, N_Z, N_YH = 4, 4, 2, 8, 2
N_ROW = N_YL * N_X * N_C
N_YZ = N_YL * N_Z * N_YH
SHARE = 960
SMALL = 24
REC = 1056
WCOL = 32

UP_TILES = (
    [(0, t) for t in range(8)],
    [(0, 7), (0, 8), (0, 9)] + [(1, t) for t in range(5)],
    [(1, t) for t in range(5, 10)] + [(2, t) for t in range(3)],
    [(2, t) for t in range(2, 10)],
)
DOWN_TILES = (
    [(0, t) for t in range(3)] + [(1, t) for t in range(3)] + [(2, 0), (2, 1)],
    [(2, 1), (2, 2)] + [(3, t) for t in range(3)] + [(4, t) for t in range(3)],
)


def call(kernel, outs, *args, scratch=(), smem=(), flops=0, nbytes=0, trans=0):
    specs = [
        pl.BlockSpec(memory_space=pltpu.SMEM if i in smem else pltpu.VMEM)
        for i in range(len(args))
    ]
    return pl.pallas_call(
        kernel,
        out_shape=[jax.ShapeDtypeStruct(s, d) for s, d in outs],
        in_specs=specs,
        out_specs=[pl.BlockSpec(memory_space=pltpu.VMEM) for _ in outs],
        scratch_shapes=list(scratch),
        compiler_params=pltpu.CompilerParams(vmem_limit_bytes=40 * 1024 * 1024),
        cost_estimate=pl.CostEstimate(flops=flops, bytes_accessed=nbytes, transcendentals=trans),
    )(*args)


def mm(a, b, dims=((1,), (0,))):
    return lax.dot_general(a, b, (dims, ((), ())), preferred_element_type=F32)


def head_scaled(values):
    block = lax.broadcasted_iota(jnp.int32, (C, C), 0) // 64
    same = (block == lax.broadcasted_iota(jnp.int32, (C, C), 1) // 64).astype(F32).astype(BF16)
    squares = values * values
    high = squares.astype(BF16)
    low = (squares - high.astype(F32)).astype(BF16)
    return values * lax.rsqrt(mm(high, same) + mm(low, same) + EPS_NORM)


def pool_kernel(feat, out):
    total = feat[0].astype(F32)
    for r in range(1, HB):
        total = total + feat[r].astype(F32)
    mean = (total * (1.0 / HB)).astype(BF16)
    for i in range(N_ROW):
        out[i] = mean


def query_kernel(feat, w_query, out):
    out[...] = head_scaled(mm(feat[...], w_query[...])).astype(BF16)


def attention_kernel(scale, pooled, query, feat, w_key, w_value, w_out, mixed, first, last):
    rows = pooled[...]
    keys = head_scaled(mm(rows, w_key[...])).astype(BF16)
    values = mm(rows, w_value[...]).astype(BF16)
    n_keys = N_ROW * WB
    same = (
        lax.broadcasted_iota(jnp.int32, (PIX, n_keys), 0) % WB
        == lax.broadcasted_iota(jnp.int32, (PIX, n_keys), 1) % WB
    )
    lower = lax.broadcasted_iota(jnp.int32, (PIX, 128), 1) < 64
    pairs = []
    for pair in range(HEADS // 2):
        lanes = slice(128 * pair, 128 * pair + 128)
        q = query[:, lanes].astype(F32)
        parts = []
        for half in range(2):
            q_half = jnp.where(lower if half == 0 else ~lower, q, 0.0).astype(BF16)
            scores = mm(q_half, keys[:, lanes], ((1,), (1,)))
            weight = jnp.where(same, jnp.exp(scores * scale[2 * pair + half]), 0.0)
            total = jnp.sum(weight, axis=1, keepdims=True)
            parts.append(mm(weight.astype(BF16), values[:, lanes]) / total)
        pairs.append(jnp.where(lower, parts[0], parts[1]).astype(BF16))
    attended = jnp.concatenate(pairs, axis=1)
    out = (feat[...].astype(F32) + mm(attended, w_out[...])).astype(BF16)
    mixed[...] = out
    first[...] = out[: 3 * WB]
    last[...] = out[PIX - 3 * WB :]


def fill_window(win, own, above, below, left, right):
    for r in range(3):
        win[r, 8 : 8 + WB, :] = above[r * WB : (r + 1) * WB, :].astype(F32)
        win[3 + HB + r, 8 : 8 + WB, :] = below[r * WB : (r + 1) * WB, :].astype(F32)
    for r in range(HB):
        win[3 + r, 8 : 8 + WB, :] = own[r * WB : (r + 1) * WB, :].astype(F32)
    lcols = left[...].astype(F32)
    rcols = right[...].astype(F32)
    for r in range(HB + 6):
        win[r, 5:8, :] = lcols[3 * r : 3 * r + 3]
        win[r, 8 + WB : 11 + WB, :] = rcols[3 * r : 3 * r + 3]


def depthwise(win, taps, start, flip, store):
    for t in range(TILES_L):
        lanes = slice(128 * t, 128 * t + 128)
        acc = [start(r, lanes) for r in range(HB)]
        for dj in range(7):
            cols = [win[r, 5 + dj : 5 + dj + WB, lanes] for r in range(HB + 6)]
            for di in range(7):
                tap = 7 * di + dj if not flip else 7 * (6 - di) + (6 - dj)
                k = taps[tap : tap + 1, lanes]
                for r in range(HB):
                    acc[r] = acc[r] + cols[r + di] * k
        for r in range(HB):
            store(r, lanes, acc[r])


def rowsum(a):
    return jnp.sum(a, axis=0, keepdims=True)


def sublayer_kernel(
    own, above, below, left, right, cot, occ, taps, dw_bias, ln_gain, ln_bias,
    w_up, b_up, w_down, b_down, layer_scale,
    output, d_out, d_first, d_last, win_out, lnout_out, hidden_out, d_pre_out, d_branch_out, sums,
    win, spat,
):
    fill_window(win, own, above, below, left, right)
    win_out[...] = win[...].astype(BF16)

    def store(r, lanes, value):
        spat[r * WB : (r + 1) * WB, lanes] = value

    depthwise(
        win, taps, lambda r, lanes: jnp.broadcast_to(dw_bias[:, lanes], (WB, 128)), False, store
    )
    spatial = spat[...]
    center = spatial - jnp.mean(spatial, axis=1, keepdims=True)
    inv_std = lax.rsqrt(jnp.mean(center * center, axis=1, keepdims=True) + EPS_NORM)
    standard = center * inv_std
    gain = ln_gain[...]
    lnout = (standard * gain + ln_bias[...]).astype(BF16)
    lnout_out[...] = lnout
    preact = mm(lnout, w_up[...]) + b_up[...]
    square = 0.044715 * preact * preact
    tanh_val = jnp.tanh(GELU_SCALE * preact * (1.0 + square))
    hidden = (0.5 * preact * (1.0 + tanh_val)).astype(BF16)
    slope = 0.5 * (1.0 + tanh_val) + 0.5 * preact * (1.0 - tanh_val * tanh_val) * GELU_SCALE * (
        1.0 + 3.0 * square
    )
    hidden_out[...] = hidden
    weight = occ[...]
    scale = layer_scale[...]
    cotan = cot[...].astype(F32)
    d_branch = cotan * scale * weight
    d_branch_b = d_branch.astype(BF16)
    d_branch_out[...] = d_branch_b
    d_pre = mm(d_branch_b, w_down[...], ((1,), (1,))) * slope
    d_pre_b = d_pre.astype(BF16)
    d_pre_out[...] = d_pre_b
    d_lnout = mm(d_pre_b, w_up[...], ((1,), (1,)))
    e = d_lnout * gain
    d_spatial = inv_std * (
        e
        - jnp.mean(e, axis=1, keepdims=True)
        - standard * jnp.mean(e * standard, axis=1, keepdims=True)
    )
    d_out[...] = d_spatial
    d_first[...] = d_spatial[: 3 * WB].astype(BF16)
    d_last[...] = d_spatial[PIX - 3 * WB :].astype(BF16)
    branch = (mm(hidden, w_down[...]) + b_down[...]) * weight
    output[...] = (own[...].astype(F32) + scale * branch).astype(BF16)
    sums[0:1, :C] = rowsum(d_spatial)
    sums[1:2, :C] = rowsum(d_lnout * standard)
    sums[2:3, :C] = rowsum(d_lnout)
    sums[3:4, :C] = rowsum(d_branch)
    sums[4:5, :C] = rowsum(cotan * branch)
    sums[5:6, :] = rowsum(d_pre)


def up_order():
    chan = np.arange(C).reshape(N_YL, N_X, N_C, N_Z // 2, 3).transpose(4, 2, 1, 0, 3).reshape(-1)
    return (np.arange(C)[:, None] == chan[None, :]).astype(np.float32)


def gradient_kernel(
    core, order, lnout, hidden, d_pre, d_branch, win_in, d_spatial, sums, mine, other, win, down, small
):
    is_zero = core[0] == 0

    def put(row, x, zero, one):
        size = zero.shape[0]
        mine[x, row : row + size, :] = jnp.where(is_zero, zero, one).astype(BF16)
        other[x, row : row + size, :] = jnp.where(is_zero, one, zero).astype(BF16)

    ordered = mm(lnout[...], order[...]).astype(BF16)
    ups = [mm(ordered[:, 128 * r : 128 * r + 128], d_pre[...], ((0,), (0,))) for r in range(3)]
    for q in range(4):
        for k, (r, t) in enumerate(UP_TILES[q]):
            for x in range(N_X):
                pair = [ups[r][64 * c + 16 * x : 64 * c + 16 * x + 16, 128 * t : 128 * t + 128] for c in range(2)]
                put((q * 8 + k) * 16, x, *pair)
    full = mm(hidden[...], d_branch[...], ((0,), (0,)))
    for t in range(TILES_L):
        down[t] = full[:, 128 * t : 128 * t + 128]
    for yh in range(2):
        for k, (s, t) in enumerate(DOWN_TILES[yh]):
            for x in range(N_X):
                for two in range(2):
                    pair = [
                        jnp.concatenate(
                            [
                                down[t, pl.ds(5 * (64 * yl + 16 * x + 8 * c) + s, 8, stride=5), :]
                                for yl in (2 * two, 2 * two + 1)
                            ],
                            axis=0,
                        )
                        for c in range(2)
                    ]
                    put(512 + (yh * 8 + k) * 32 + 16 * two, x, *pair)
    win[...] = win_in[...].astype(F32)
    small[...] = jnp.zeros_like(small)
    for t in range(TILES_L):
        lanes = slice(128 * t, 128 * t + 128)
        d_rows = [d_spatial[r * WB : (r + 1) * WB, lanes] for r in range(HB)]
        for dj in range(7):
            cols = [win[r, 5 + dj : 5 + dj + WB, lanes] for r in range(HB + 6)]
            for di in range(7):
                acc = cols[di] * d_rows[0]
                for r in range(1, HB):
                    acc = acc + cols[r + di] * d_rows[r]
                at = 56 * t + 7 * di + dj
                small[at : at + 1, :] = rowsum(acc)
    for i in range(5):
        for t in range(TILES_L):
            small[161 + 3 * i + t : 162 + 3 * i + t, :] = sums[i : i + 1, 128 * t : 128 * t + 128]
    for t in range(HID // 128):
        small[176 + t : 177 + t, :] = sums[5:6, 128 * t : 128 * t + 128]
    for x in range(N_X):
        pair = [
            jnp.concatenate([small[96 * c + 24 * x : 96 * c + 24 * x + 24], jnp.zeros((8, 128), F32)], axis=0)
            for c in range(2)
        ]
        put(1024, x, *pair)


def spread_kernel(part, out, total):
    total[...] = (
        (part[0].astype(F32) + part[1].astype(F32)) + (part[2].astype(F32) + part[3].astype(F32))
    )
    small = total[1024 : 1024 + SMALL, :]
    for yl in range(N_YL):
        for z in range(N_Z):
            for yh in range(N_YH):
                q = (z % 2) * 2 + yh
                up = total[pl.ds(q * 128 + yl * 4 + z // 2, 8, stride=16), :]
                down = total[pl.ds(512 + yh * 256 + yl * 8 + z, 8, stride=32), :]
                record = jnp.concatenate([up, down, small], axis=0)
                out[(yl * N_Z + z) * N_YH + yh] = record.astype(BF16)


def gather_kernel(part, share, small):
    total = part[0].astype(F32)
    for i in range(1, N_YZ):
        total = total + part[i].astype(F32)
    share[...] = total[:16]
    for i in range(N_X * N_C):
        small[i] = total[16:]


def final_kernel(small, dw, *vectors):
    for t in range(TILES_L):
        dw[:, 128 * t : 128 * t + 128] = small[56 * t : 56 * t + 49, :]
    for i in range(5):
        for t in range(TILES_L):
            vectors[i][:, 128 * t : 128 * t + 128] = small[161 + 3 * i + t : 162 + 3 * i + t, :]
    for t in range(HID // 128):
        vectors[5][:, 128 * t : 128 * t + 128] = small[176 + t : 177 + t, :]


def spread_grad_kernel(own, above, below, left, right, cot, taps, out, win):
    fill_window(win, own, above, below, left, right)

    def store(r, lanes, value):
        out[r * WB : (r + 1) * WB, lanes] = value

    depthwise(
        win, taps, lambda r, lanes: cot[r * WB : (r + 1) * WB, lanes].astype(F32), True, store
    )


def core_sum_kernel(mine, got, first, last, out):
    out[...] = (mine[...].astype(F32) + got[...].astype(F32)).astype(BF16)


def neighbours(before_edge, after_edge, axes):
    size = lax.axis_size(axes)
    up = [(i, i + 1) for i in range(size - 1)]
    down = [(i + 1, i) for i in range(size - 1)]
    return lax.ppermute(after_edge, axes, up), lax.ppermute(before_edge, axes, down)


def column_edges(own, above, below):
    rows = jnp.concatenate([above, own, below], axis=0).reshape(HB + 6, WB, C)
    return rows[:, :3].reshape(-1, C), rows[:, WB - 3 :].reshape(-1, C)


def body(
    features, w_query, w_key, w_value, w_out, logit_scale, dw_kernel, dw_bias, ln_gain, ln_bias,
    w_up, b_up, w_down, b_down, layer_scale, cotangent, tile_list,
):
    row = lambda v: v.reshape(1, -1)
    flat = features.reshape(PIX, C)
    cot = cotangent.reshape(PIX, C)

    (copies,) = call(pool_kernel, [((N_ROW, WB, C), BF16)], features, nbytes=500_000)
    pooled = lax.all_to_all(copies, ROW, 0, 0, tiled=True).reshape(N_ROW * WB, C)
    (query,) = call(query_kernel, [((PIX, C), BF16)], flat, w_query, flops=10**8, nbytes=500_000)
    tiles = jnp.arange(HB // TS * (WB // TS), dtype=jnp.int32)
    hits = jnp.any(tile_list[0, 0][:, None] == tiles[None, :], axis=0).astype(F32)
    occ = jnp.broadcast_to(hits.reshape(HB // TS, 1, WB // TS, 1), (HB // TS, TS, WB // TS, TS))
    occ = occ.reshape(PIX, 1)

    edge = ((3 * WB, C), BF16)
    mixed, first, last = call(
        attention_kernel, [((PIX, C), BF16), edge, edge],
        logit_scale, pooled, query, flat, w_key, w_value, w_out,
        smem=(0,), flops=10**9, nbytes=2_000_000, trans=400_000,
    )
    above, below = neighbours(first, last, ROW)
    left, right = neighbours(*column_edges(mixed, above, below), COL)

    output, d_spatial, d_first, d_last, win, lnout, hidden, d_pre, d_branch, sums = call(
        sublayer_kernel,
        [
            ((PIX, C), BF16), ((PIX, C), F32), edge, edge, ((HB + 6, WCOL, C), BF16),
            ((PIX, C), BF16), ((PIX, HID), BF16), ((PIX, HID), BF16), ((PIX, C), BF16), ((8, HID), F32),
        ],
        mixed, above, below, left, right, cot, occ, dw_kernel, row(dw_bias), row(ln_gain),
        row(ln_bias), w_up, row(b_up), w_down, row(b_down), row(layer_scale),
        scratch=[pltpu.VMEM((HB + 6, WCOL, C), F32), pltpu.VMEM((PIX, C), F32)],
        flops=10**9, nbytes=4_000_000, trans=160_000,
    )

    d_above, d_below = neighbours(d_first, d_last, ROW)
    core = lax.axis_index("c").reshape(1)
    order = jnp.asarray(up_order(), BF16)
    record = ((N_X, REC, 128), BF16)
    mine, other = call(
        gradient_kernel, [record, record],
        core, order, lnout, hidden, d_pre, d_branch, win, d_spatial, sums,
        scratch=[
            pltpu.VMEM((HB + 6, WCOL, C), F32),
            pltpu.VMEM((TILES_L, HID, 128), F32),
            pltpu.VMEM((8 * SMALL, 128), F32),
        ],
        smem=(0,), flops=2 * 10**9, nbytes=4_000_000,
    )
    d_edges = column_edges(d_spatial.astype(BF16), d_above, d_below)
    d_left, d_right = neighbours(*d_edges, COL)

    got = lax.ppermute(other, "c", [(0, 1), (1, 0)])
    (part,) = call(core_sum_kernel, [record], mine, got, *d_edges, nbytes=3_000_000)
    part = lax.all_to_all(part, "x", 0, 0, tiled=True)
    (part,) = call(
        spread_kernel_after, [((N_YZ, 16 + SMALL, 128), BF16)], part, d_left, d_right,
        scratch=[pltpu.VMEM((REC, 128), F32)], nbytes=2_000_000,
    )
    part = lax.all_to_all(part, YZ, 0, 0, tiled=True)
    share, small = call(
        gather_kernel, [((16, 128), F32), ((N_X * N_C, SMALL, 128), F32)], part, nbytes=800_000
    )
    small = lax.all_to_all(small, CX, 0, 0, tiled=True)
    vectors = call(
        final_kernel, [((49, C), F32)] + [((1, C), F32)] * 5 + [((1, HID), F32)],
        small.reshape(-1, 128), nbytes=200_000,
    )
    share = share.reshape(2, 8 * 128)
    share = jnp.where(lax.axis_index("yh") == 0, share[:, :SHARE], share[:, 8 * 128 - SHARE :])
    (grad_mixed,) = call(
        spread_grad_kernel, [((PIX, C), F32)],
        d_spatial, d_above, d_below, d_left, d_right, cot, dw_kernel,
        scratch=[pltpu.VMEM((HB + 6, WCOL, C), F32)], flops=10**7, nbytes=1_000_000,
    )
    bias, gain, shift, b_down_grad, scale_grad, b_up_grad = [v.reshape(-1) for v in vectors[1:]]
    return (
        output.reshape(HB, WB, C), grad_mixed.reshape(HB, WB, C), share[0], share[1],
        vectors[0], bias, gain, shift, b_up_grad, b_down_grad, scale_grad,
    )


def spread_kernel_after(part, left, right, out, total):
    spread_kernel(part, out, total)


def solution(mesh):
    mesh = Mesh(mesh.devices.reshape(N_YL, N_X, N_C, N_Z, N_YH), ROW + COL)
    block = P(ROW, COL, None)
    in_specs = (block,) + (P(),) * 14 + (block, block)
    out_specs = (block, block, P(ROW + COL), P(ROW + COL)) + (P(),) * 7
    return jax.shard_map(body, mesh=mesh, in_specs=in_specs, out_specs=out_specs, check_vma=False)
```

time: 449 us -> 147 us (0.33)
  blocking collectives: 194 us -> 0 us
  waiting for transfers between devices: 173 us -> 56.1 us
  starting transfers between devices: 26.3 us -> 65 us
  Pallas kernels: 0 us -> 17 us
  between operations: 16.6 us -> 1.11 us
  local copies, waits for them, and re-layouts: 17.6 us -> 3.28 us
  matrix products: 9.34 us -> 0 us
  other arithmetic: 11.3 us -> 3.82 us
    unnamed x2 -> x0, waiting for transfers between devices: 165 us -> none
    psum x1 -> x0, blocking collectives: 106 us -> none  [body(): lax.psum((kernel_grad, bias_grad, gain_grad, shift_grad, up_bias_grad, do...]
    all_gather x2 -> x0, blocking collectives: 88.1 us -> none  [the longest x1 46.8 us: body(): value_piece = lax.all_gather(values, 'row', axis=0, tiled=True)]
    all_to_all x0 -> x4, starting transfers between devices: none -> 40.1 us  [the longest x1 14.3 us: body(): part = lax.all_to_all(part, YZ, 0, 0, tiled=True)]
    all_to_all x0 -> x4, waiting for transfers between devices: none -> 35.8 us  [the longest x1 18.1 us: body(): part = lax.all_to_all(part, YZ, 0, 0, tiled=True)]
    pallas_call x0 -> x10, Pallas kernels: none -> 17 us  [call(): pl.pallas_call(kernel, out_shape=[jax.ShapeDtypeStruct(s, d) for s, d in...]
    ppermute x8 -> x9, waiting for transfers between devices: 8.08 us -> 20.3 us  [the longest x4 20 us: neighbours(): lax.ppermute(before_edge, axes, down)]
    dot_general x12 -> x0, matrix products: 9.34 us -> none  [the longest x1 1.78 us: sublayer(): lax.dot_general(hidden, d_branch_b, (((0,), (0,)), ((), ())), preferred_e...]
  transfers between devices with their start and end apart: 9 -> 13, of which waited for: 3 -> 8; matrix products, arithmetic and copies ran while one was open for 1% -> 1% of each run, Pallas kernels for 0% -> 2%
where the time goes in v2:
time: 147 us; the launch traced here: 146 us
  starting transfers between devices  65 us (44%)
  waiting for transfers between devices  56.1 us (38%)
  Pallas kernels  17 us (12%)
  other arithmetic  3.82 us (3%)
  local copies, waits for them, and re-layouts  3.28 us (2%)
    ppermute x4, waiting for transfers between devices, neighbours(): lax.ppermute(before_edge, axes, down)  20 us
    all_to_all x1, waiting for transfers between devices, body(): part = lax.all_to_all(part, YZ, 0, 0, tiled=True)  18.1 us
    pallas_call x10, Pallas kernels, call(): pl.pallas_call(kernel, out_shape=[jax.ShapeDtypeStruct(s, d) for s, d in...  17 us
    ppermute x4, starting transfers between devices, neighbours(): lax.ppermute(after_edge, axes, up)  15.9 us
    all_to_all x1, starting transfers between devices, body(): part = lax.all_to_all(part, YZ, 0, 0, tiled=True)  14.3 us
    all_to_all x1, waiting for transfers between devices, body(): lax.all_to_all(copies, ROW, 0, 0, tiled=True).reshape(N_ROW * WB, C)  13.4 us
    all_to_all x1, starting transfers between devices, body(): lax.all_to_all(copies, ROW, 0, 0, tiled=True).reshape(N_ROW * WB, C)  10.4 us
    all_to_all x1, starting transfers between devices, body(): part = lax.all_to_all(part, 'x', 0, 0, tiled=True)  8.41 us
  transfers between devices with their start and end apart: 13, of which 8 were waited for; matrix products, arithmetic and copies ran while one was open for 1% of the time, Pallas kernels for 2%

profile of v2, /device:TPU:1, one launch (start us, length us, event | category | flops | bytes accessed | tf_op | source)
XLA Modules:
  0.0 146.3 jit_solution(8008562141001527555)
XLA Ops:
  2.4 10.4 %all-to-all-start = ((bf16[32,16,384]{2,1,0:T(8,128)(2,1)}), bf16[32,16,384]{2,1,0:T(8,128)(2,1)S(1)}, u32[]{:S(2)}, u32[]{:S(2)}) async-start(bf16[32,16,384]{2,1,0:T(8,128)(2,1)} %shard_map.257), calls=%async_computation | async-start | bytes 786432 | tf_op jit(solution)/shard_map/all_to_all | solution.py:344
  13.3 13.4 %all-to-all-done = bf16[32,16,384]{2,1,0:T(8,128)(2,1)S(1)} async-done(((bf16[32,16,384]{2,1,0:T(8,128)(2,1)}), bf16[32,16,384]{2,1,0:T(8,128)(2,1)S(1)}, u32[]{:S(2)}, u32[]{:S(2)}) %all-to-all-start) | async-done | bytes 393248 | tf_op jit(solution)/shard_map/all_to_all | solution.py:344
  26.8 2.8 %shard_map.259 = (bf16[128,384]{1,0:T(8,128)(2,1)S(1)}, bf16[48,384]{1,0:T(8,128)(2,1)S(1)}, bf16[48,384]{1,0:T(8,128)(2,1)S(1)}) custom-call(f32[6]{0:T(128)S(1)} %copy-done.10, bf16[512,384]{1,0:T(8,128)(2,1)S(1)} %bitcast.12, bf16[128,384]{1,0:T(8,128)(2,1)S(1)} %shard_map.258.query, bf16[128,384]{1,0:T(8,128)(2,1)S(1)} %bitcast.15, ...), custom_call_target="tpu_custom_call" | custom-call | flops 1000000000 | bytes 2000000 | tf_op jit(solution)/shard_map/pallas_call | solution.py:51
  29.6 1.9 %collective-permute-start = (bf16[48,384]{1,0:T(8,128)(2,1)S(1)}, bf16[48,384]{1,0:T(8,128)(2,1)S(1)}, u32[]{:S(2)}, u32[]{:S(2)}) collective-permute-start(bf16[48,384]{1,0:T(8,128)(2,1)S(1)} %get-tuple-element.36), channel_id=1, source_target_pairs={{0,16},{16,32},{32,48},{48,64},{64,80},{80,96},{96,112},{112,128},... | collective-permute-start | bytes 110600 | tf_op jit(solution)/shard_map/ppermute | solution.py:327
  31.5 2.4 %collective-permute-start.1 = (bf16[48,384]{1,0:T(8,128)(2,1)S(1)}, bf16[48,384]{1,0:T(8,128)(2,1)S(1)}, u32[]{:S(2)}, u32[]{:S(2)}) collective-permute-start(bf16[48,384]{1,0:T(8,128)(2,1)S(1)} %get-tuple-element.37), channel_id=1, source_target_pairs={{16,0},{32,16},{48,32},{64,48},{80,64},{96,80},{112,96},{128,112},... | collective-permute-start | bytes 110600 | tf_op jit(solution)/shard_map/ppermute | solution.py:327
  33.9 2.9 %collective-permute-done.1.below = bf16[48,384]{1,0:T(8,128)(2,1)S(1)} collective-permute-done((bf16[48,384]{1,0:T(8,128)(2,1)S(1)}, bf16[48,384]{1,0:T(8,128)(2,1)S(1)}, u32[]{:S(2)}, u32[]{:S(2)}) %collective-permute-start.1) | collective-permute-done | bytes 36896 | tf_op jit(solution)/shard_map/ppermute | solution.py:327
  36.9 3.2 %collective-permute-start.2 = (bf16[42,384]{1,0:T(8,128)(2,1)S(1)}, bf16[42,384]{1,0:T(8,128)(2,1)S(1)}, u32[]{:S(2)}, u32[]{:S(2)}) collective-permute-start(bf16[42,384]{1,0:T(8,128)(2,1)S(1)} %reshape.115), channel_id=1, source_target_pairs={{0,1},{1,2},{2,3},{3,4},{4,5},{5,6},{6,7},{7,8},{8,9},{9,10},{10,1... | collective-permute-start | bytes 96776 | tf_op jit(solution)/shard_map/ppermute | solution.py:327
  40.2 1.3 collective-permute-start.3
  42.0 6.8 %collective-permute-done.3.right = bf16[42,384]{1,0:T(8,128)(2,1)S(1)} collective-permute-done((bf16[42,384]{1,0:T(8,128)(2,1)S(1)}, bf16[42,384]{1,0:T(8,128)(2,1)S(1)}, u32[]{:S(2)}, u32[]{:S(2)}) %collective-permute-start.3) | collective-permute-done | bytes 32288 | tf_op jit(solution)/shard_map/ppermute | solution.py:327
  50.0 3.7 %shard_map.260 = (bf16[128,384]{1,0:T(8,128)(2,1)}, f32[128,384]{1,0:T(8,128)S(1)}, bf16[48,384]{1,0:T(8,128)(2,1)S(1)}, bf16[48,384]{1,0:T(8,128)(2,1)S(1)}, bf...) custom-call(bf16[128,384]{1,0:T(8,128)(2,1)S(1)} %get-tuple-element., ...), custom_call_target="tpu_custom_call" | custom-call | flops 1000000000 | bytes 4000000 | tf_op jit(solution)/shard_map/pallas_call | solution.py:51
  53.7 3.2 %shard_map.262 = (bf16[4,1056,128]{2,1,0:T(8,128)(2,1)S(1)}, bf16[4,1056,128]{2,1,0:T(8,128)(2,1)}) custom-call(s32[1]{0:T(128)} %bitcast.8.core, bf16[384,384]{1,0:T(8,128)(2,1)S(1)} %copy-done.11, bf16[128,384]{1,0:T(8,128)(2,1)S(1)} %get-tuple-element.42.lnout, bf16[128,1280]{1,0:T(8,128)(2,1)S(1)} %get-tuple-element.43.hidden, ...), custom_call_target="tpu_custom_call" | custom-call | flops 2000000000 | bytes 4000000 | tf_op jit(solution)/shard_map/pallas_call | solution.py:51
  56.9 2.0 %collective-permute-start.8 = (bf16[4,1056,128]{2,1,0:T(8,128)(2,1)}, bf16[4,1056,128]{2,1,0:T(8,128)(2,1)S(1)}, u32[]{:S(2)}, u32[]{:S(2)}) collective-permute-start(bf16[4,1056,128]{2,1,0:T(8,128)(2,1)} %get-tuple-element.49), channel_id=1, source_target_pairs={{0,16},{16,0},{1,17},{17,1},{2,18},{18,2},{3,19},{19,3},{4,20},{20... | collective-permute-start | bytes 3244040 | tf_op jit(solution)/shard_map/ppermute | solution.py:389
  59.0 3.6 %collective-permute-start.4 = (bf16[48,384]{1,0:T(8,128)(2,1)S(1)}, bf16[48,384]{1,0:T(8,128)(2,1)S(1)}, u32[]{:S(2)}, u32[]{:S(2)}) collective-permute-start(bf16[48,384]{1,0:T(8,128)(2,1)S(1)} %get-tuple-element.40), channel_id=1, source_target_pairs={{0,16},{16,32},{32,48},{48,64},{64,80},{80,96},{96,112},{112,128},... | collective-permute-start | bytes 110600 | tf_op jit(solution)/shard_map/ppermute | solution.py:327
  62.6 1.9 %collective-permute-start.5 = (bf16[48,384]{1,0:T(8,128)(2,1)S(1)}, bf16[48,384]{1,0:T(8,128)(2,1)S(1)}, u32[]{:S(2)}, u32[]{:S(2)}) collective-permute-start(bf16[48,384]{1,0:T(8,128)(2,1)S(1)} %get-tuple-element.41), channel_id=1, source_target_pairs={{16,0},{32,16},{48,32},{64,48},{80,64},{96,80},{112,96},{128,112},... | collective-permute-start | bytes 110600 | tf_op jit(solution)/shard_map/ppermute | solution.py:327
  64.6 3.3 %collective-permute-done.5.below = bf16[48,384]{1,0:T(8,128)(2,1)S(1)} collective-permute-done((bf16[48,384]{1,0:T(8,128)(2,1)S(1)}, bf16[48,384]{1,0:T(8,128)(2,1)S(1)}, u32[]{:S(2)}, u32[]{:S(2)}) %collective-permute-start.5) | collective-permute-done | bytes 36896 | tf_op jit(solution)/shard_map/ppermute | solution.py:327
  69.3 8.4 %all-to-all-start.1 = ((bf16[4,1056,128]{2,1,0:T(8,128)(2,1)}), bf16[4,1056,128]{2,1,0:T(8,128)(2,1)S(1)}, u32[]{:S(2)}, u32[]{:S(2)}) async-start(bf16[4,1056,128]{2,1,0:T(8,128)(2,1)} %shard_map.263), calls=%async_computation.1 | async-start | bytes 2162688 | tf_op jit(solution)/shard_map/all_to_all | solution.py:391
  77.7 7.1 %collective-permute-start.6 = (bf16[42,384]{1,0:T(8,128)(2,1)S(1)}, bf16[42,384]{1,0:T(8,128)(2,1)S(1)}, u32[]{:S(2)}, u32[]{:S(2)}) collective-permute-start(bf16[42,384]{1,0:T(8,128)(2,1)S(1)} %reshape.127.last), channel_id=1, source_target_pairs={{0,1},{1,2},{2,3},{3,4},{4,5},{5,6},{6,7},{7,8},{8,9},{9,10},{10,1... | collective-permute-start | bytes 96776 | tf_op jit(solution)/shard_map/ppermute | solution.py:327
  86.4 7.0 %collective-permute-done.7.right = bf16[42,384]{1,0:T(8,128)(2,1)S(1)} collective-permute-done((bf16[42,384]{1,0:T(8,128)(2,1)S(1)}, bf16[42,384]{1,0:T(8,128)(2,1)S(1)}, u32[]{:S(2)}, u32[]{:S(2)}) %collective-permute-start.7) | collective-permute-done | bytes 32288 | tf_op jit(solution)/shard_map/ppermute | solution.py:327
  93.5 1.3 shard_map.264
  94.8 14.3 %all-to-all-start.2 = ((bf16[64,40,128]{2,1,0:T(8,128)(2,1)}), bf16[64,40,128]{2,1,0:T(8,128)(2,1)S(1)}, u32[]{:S(2)}, u32[]{:S(2)}) async-start(bf16[64,40,128]{2,1,0:T(8,128)(2,1)} %shard_map.264), calls=%async_computation.2 | async-start | bytes 1310720 | tf_op jit(solution)/shard_map/all_to_all | solution.py:396
  109.2 2.1 %shard_map.261 = f32[128,384]{1,0:T(8,128)} custom-call(f32[128,384]{1,0:T(8,128)S(1)} %get-tuple-element.39.own.d_spatial, bf16[48,384]{1,0:T(8,128)(2,1)S(1)} %collective-permute-done.4.above, bf16[48,384]{1,0:T(8,128)(2,1)S(1)} %collective-permute-done.5.below, bf16[42,384]{1,0:T(8,128)(2,1)S(1)} %collective-permute-done.6.left, ...), custom_call_target="tpu_custom_call" | custom-call | flops 10000000 | bytes 1000000 | tf_op jit(solution)/shard_map/pallas_call | solution.py:51
  111.3 18.1 %all-to-all-done.2.part = bf16[64,40,128]{2,1,0:T(8,128)(2,1)S(1)} async-done(((bf16[64,40,128]{2,1,0:T(8,128)(2,1)}), bf16[64,40,128]{2,1,0:T(8,128)(2,1)S(1)}, u32[]{:S(2)}, u32[]{:S(2)}) %all-to-all-start.2) | async-done | bytes 655392 | tf_op jit(solution)/shard_map/all_to_all | solution.py:396
  130.1 6.9 %all-to-all-start.3 = ((f32[8,24,128]{2,1,0:T(8,128)}), f32[8,24,128]{2,1,0:T(8,128)S(1)}, u32[]{:S(2)}, u32[]{:S(2)}) async-start(f32[8,24,128]{2,1,0:T(8,128)} %get-tuple-element.51), calls=%async_computation.3 | async-start | bytes 196608 | tf_op jit(solution)/shard_map/all_to_all | solution.py:400
  137.8 4.3 %all-to-all-done.3 = f32[8,24,128]{2,1,0:T(8,128)S(1)} async-done(((f32[8,24,128]{2,1,0:T(8,128)}), f32[8,24,128]{2,1,0:T(8,128)S(1)}, u32[]{:S(2)}, u32[]{:S(2)}) %all-to-all-start.3) | async-done | bytes 98336 | tf_op jit(solution)/shard_map/all_to_all | solution.py:400
  (79 shorter events, 12.5 us)
Async XLA Ops:
  1.5 25.1 %copy-start.7 = (bf16[384,384]{1,0:T(8,128)(2,1)S(1)}, bf16[384,384]{1,0:T(8,128)(2,1)}, u32[]{:S(2)}) copy-start(bf16[384,384]{1,0:T(8,128)(2,1)} %w_key.1) | copy-start | bytes 884740
  1.5 25.1 %copy-start.8 = (bf16[384,384]{1,0:T(8,128)(2,1)S(1)}, bf16[384,384]{1,0:T(8,128)(2,1)}, u32[]{:S(2)}) copy-start(bf16[384,384]{1,0:T(8,128)(2,1)} %w_value.1) | copy-start | bytes 884740
  1.6 25.1 %copy-start.9 = (bf16[384,384]{1,0:T(8,128)(2,1)S(1)}, bf16[384,384]{1,0:T(8,128)(2,1)}, u32[]{:S(2)}) copy-start(bf16[384,384]{1,0:T(8,128)(2,1)} %w_out.1) | copy-start | bytes 884740
  1.6 25.1 %copy-start.10 = (f32[6]{0:T(128)S(1)}, f32[6]{0:T(128)}, u32[]{:S(2)}) copy-start(f32[6]{0:T(128)} %scale.1) | copy-start | bytes 76
  2.4 24.3 %all-to-all-start = ((bf16[32,16,384]{2,1,0:T(8,128)(2,1)}), bf16[32,16,384]{2,1,0:T(8,128)(2,1)S(1)}, u32[]{:S(2)}, u32[]{:S(2)}) async-start(bf16[32,16,384]{2,1,0:T(8,128)(2,1)} %shard_map.257), calls=%async_computation | async-start | bytes 786432 | tf_op jit(solution)/shard_map/all_to_all | solution.py:344
  26.7 15.2 %copy-start.14 = (f32[384]{0:T(512)S(1)}, f32[384]{0:T(512)}, u32[]{:S(2)}) copy-start(f32[384]{0:T(512)} %param.26) | copy-start | bytes 4612
  26.7 15.2 %copy-start.15 = (f32[384]{0:T(512)S(1)}, f32[384]{0:T(512)}, u32[]{:S(2)}) copy-start(f32[384]{0:T(512)} %param.27) | copy-start | bytes 4612
  26.8 15.2 %copy-start.16 = (f32[384]{0:T(512)S(1)}, f32[384]{0:T(512)}, u32[]{:S(2)}) copy-start(f32[384]{0:T(512)} %param.31) | copy-start | bytes 4612
  26.8 15.2 %copy-start.17 = (f32[384]{0:T(512)S(1)}, f32[384]{0:T(512)}, u32[]{:S(2)}) copy-start(f32[384]{0:T(512)} %param.32) | copy-start | bytes 4612
  26.8 22.0 %copy-start.3 = (bf16[8,16,384]{2,1,0:T(8,128)(2,1)S(1)}, bf16[8,16,384]{2,1,0:T(8,128)(2,1)}, u32[]{:S(2)}) copy-start(bf16[8,16,384]{2,1,0:T(8,128)(2,1)} %param.33) | copy-start | bytes 294916
  26.8 22.0 %copy-start.4 = (f32[49,384]{1,0:T(8,128)S(1)}, f32[49,384]{1,0:T(8,128)}, u32[]{:S(2)}) copy-start(f32[49,384]{1,0:T(8,128)} %taps.3) | copy-start | bytes 225796
  26.8 22.0 %copy-start.5 = (bf16[384,1280]{1,0:T(8,128)(2,1)S(1)}, bf16[384,1280]{1,0:T(8,128)(2,1)}, u32[]{:S(2)}) copy-start(bf16[384,1280]{1,0:T(8,128)(2,1)} %w_up.1) | copy-start | bytes 2949124
  29.6 4.3 %collective-permute-start = (bf16[48,384]{1,0:T(8,128)(2,1)S(1)}, bf16[48,384]{1,0:T(8,128)(2,1)S(1)}, u32[]{:S(2)}, u32[]{:S(2)}) collective-permute-start(bf16[48,384]{1,0:T(8,128)(2,1)S(1)} %get-tuple-element.36), channel_id=1, source_target_pairs={{0,16},{16,32},{32,48},{48,64},{64,80},{80,96},{96,112},{112,128},... | collective-permute-start | bytes 110600 | tf_op jit(solution)/shard_map/ppermute | solution.py:327
  31.5 5.3 %collective-permute-start.1 = (bf16[48,384]{1,0:T(8,128)(2,1)S(1)}, bf16[48,384]{1,0:T(8,128)(2,1)S(1)}, u32[]{:S(2)}, u32[]{:S(2)}) collective-permute-start(bf16[48,384]{1,0:T(8,128)(2,1)S(1)} %get-tuple-element.37), channel_id=1, source_target_pairs={{16,0},{32,16},{48,32},{64,48},{80,64},{96,80},{112,96},{128,112},... | collective-permute-start | bytes 110600 | tf_op jit(solution)/shard_map/ppermute | solution.py:327
  36.9 5.1 %collective-permute-start.2 = (bf16[42,384]{1,0:T(8,128)(2,1)S(1)}, bf16[42,384]{1,0:T(8,128)(2,1)S(1)}, u32[]{:S(2)}, u32[]{:S(2)}) collective-permute-start(bf16[42,384]{1,0:T(8,128)(2,1)S(1)} %reshape.115), channel_id=1, source_target_pairs={{0,1},{1,2},{2,3},{3,4},{4,5},{5,6},{6,7},{7,8},{8,9},{9,10},{10,1... | collective-permute-start | bytes 96776 | tf_op jit(solution)/shard_map/ppermute | solution.py:327
  40.2 8.6 %collective-permute-start.3 = (bf16[42,384]{1,0:T(8,128)(2,1)S(1)}, bf16[42,384]{1,0:T(8,128)(2,1)S(1)}, u32[]{:S(2)}, u32[]{:S(2)}) collective-permute-start(bf16[42,384]{1,0:T(8,128)(2,1)S(1)} %reshape.116), channel_id=1, source_target_pairs={{1,0},{2,1},{3,2},{4,3},{5,4},{6,5},{7,6},{8,7},{9,8},{10,9},{11,1... | collective-permute-start | bytes 96776 | tf_op jit(solution)/shard_map/ppermute | solution.py:327
  56.9 11.1 %collective-permute-start.8 = (bf16[4,1056,128]{2,1,0:T(8,128)(2,1)}, bf16[4,1056,128]{2,1,0:T(8,128)(2,1)S(1)}, u32[]{:S(2)}, u32[]{:S(2)}) collective-permute-start(bf16[4,1056,128]{2,1,0:T(8,128)(2,1)} %get-tuple-element.49), channel_id=1, source_target_pairs={{0,16},{16,0},{1,17},{17,1},{2,18},{18,2},{3,19},{19,3},{4,20},{20... | collective-permute-start | bytes 3244040 | tf_op jit(solution)/shard_map/ppermute | solution.py:389
  59.0 5.6 %collective-permute-start.4 = (bf16[48,384]{1,0:T(8,128)(2,1)S(1)}, bf16[48,384]{1,0:T(8,128)(2,1)S(1)}, u32[]{:S(2)}, u32[]{:S(2)}) collective-permute-start(bf16[48,384]{1,0:T(8,128)(2,1)S(1)} %get-tuple-element.40), channel_id=1, source_target_pairs={{0,16},{16,32},{32,48},{48,64},{64,80},{80,96},{96,112},{112,128},... | collective-permute-start | bytes 110600 | tf_op jit(solution)/shard_map/ppermute | solution.py:327
  62.6 5.3 %collective-permute-start.5 = (bf16[48,384]{1,0:T(8,128)(2,1)S(1)}, bf16[48,384]{1,0:T(8,128)(2,1)S(1)}, u32[]{:S(2)}, u32[]{:S(2)}) collective-permute-start(bf16[48,384]{1,0:T(8,128)(2,1)S(1)} %get-tuple-element.41), channel_id=1, source_target_pairs={{16,0},{32,16},{48,32},{64,48},{80,64},{96,80},{112,96},{128,112},... | collective-permute-start | bytes 110600 | tf_op jit(solution)/shard_map/ppermute | solution.py:327
  69.3 24.2 %all-to-all-start.1 = ((bf16[4,1056,128]{2,1,0:T(8,128)(2,1)}), bf16[4,1056,128]{2,1,0:T(8,128)(2,1)S(1)}, u32[]{:S(2)}, u32[]{:S(2)}) async-start(bf16[4,1056,128]{2,1,0:T(8,128)(2,1)} %shard_map.263), calls=%async_computation.1 | async-start | bytes 2162688 | tf_op jit(solution)/shard_map/all_to_all | solution.py:391
  77.7 8.7 %collective-permute-start.6 = (bf16[42,384]{1,0:T(8,128)(2,1)S(1)}, bf16[42,384]{1,0:T(8,128)(2,1)S(1)}, u32[]{:S(2)}, u32[]{:S(2)}) collective-permute-start(bf16[42,384]{1,0:T(8,128)(2,1)S(1)} %reshape.127.last), channel_id=1, source_target_pairs={{0,1},{1,2},{2,3},{3,4},{4,5},{5,6},{6,7},{7,8},{8,9},{9,10},{10,1... | collective-permute-start | bytes 96776 | tf_op jit(solution)/shard_map/ppermute | solution.py:327
  84.9 8.6 %collective-permute-start.7 = (bf16[42,384]{1,0:T(8,128)(2,1)S(1)}, bf16[42,384]{1,0:T(8,128)(2,1)S(1)}, u32[]{:S(2)}, u32[]{:S(2)}) collective-permute-start(bf16[42,384]{1,0:T(8,128)(2,1)S(1)} %reshape.128.first), channel_id=1, source_target_pairs={{1,0},{2,1},{3,2},{4,3},{5,4},{6,5},{7,6},{8,7},{9,8},{10,9},{11,1... | collective-permute-start | bytes 96776 | tf_op jit(solution)/shard_map/ppermute | solution.py:327
  94.8 34.6 %all-to-all-start.2 = ((bf16[64,40,128]{2,1,0:T(8,128)(2,1)}), bf16[64,40,128]{2,1,0:T(8,128)(2,1)S(1)}, u32[]{:S(2)}, u32[]{:S(2)}) async-start(bf16[64,40,128]{2,1,0:T(8,128)(2,1)} %shard_map.264), calls=%async_computation.2 | async-start | bytes 1310720 | tf_op jit(solution)/shard_map/all_to_all | solution.py:396
  130.1 11.9 %all-to-all-start.3 = ((f32[8,24,128]{2,1,0:T(8,128)}), f32[8,24,128]{2,1,0:T(8,128)S(1)}, u32[]{:S(2)}, u32[]{:S(2)}) async-start(f32[8,24,128]{2,1,0:T(8,128)} %get-tuple-element.51), calls=%async_computation.3 | async-start | bytes 196608 | tf_op jit(solution)/shard_map/all_to_all | solution.py:400
  (8 other events, 73.4 us)

commit v3 on v2

v3 whole, which is shorter than its diff:
```python
import numpy as np
import jax
import jax.numpy as jnp
from jax import lax
from jax.experimental import pallas as pl
from jax.experimental.pallas import tpu as pltpu
from jax.sharding import Mesh, PartitionSpec as P

ROW = ("yl", "x", "c")
COL = ("z", "yh")
YZ = ("yl", "z", "yh")
CX = ("c", "x")

F32 = jnp.float32
BF16 = jnp.bfloat16
EPS_NORM = 1e-06
GELU_SCALE = 0.7978845608028654
TS = 4
HB = 8
WB = 16
PIX = HB * WB
C = 384
HID = 1280
HEADS = 6
TILES_L = C // 128
N_YL, N_X, N_C, N_Z, N_YH = 4, 4, 2, 8, 2
N_ROW = N_YL * N_X * N_C
N_YZ = N_YL * N_Z * N_YH
SHARE = 960
SMALL = 24
REC = 1056
WCOL = 32
TILES = 8
HALO = 3
ROWS_M = HB + 4 * HALO
ROWS_D = HB + 2 * HALO
OWN = slice(HALO * WB, HALO * WB + PIX)

UP_TILES = (
    [(0, t) for t in range(8)],
    [(0, 7), (0, 8), (0, 9)] + [(1, t) for t in range(5)],
    [(1, t) for t in range(5, 10)] + [(2, t) for t in range(3)],
    [(2, t) for t in range(2, 10)],
)
DOWN_TILES = (
    [(0, t) for t in range(3)] + [(1, t) for t in range(3)] + [(2, 0), (2, 1)],
    [(2, 1), (2, 2)] + [(3, t) for t in range(3)] + [(4, t) for t in range(3)],
)


def call(kernel, outs, *args, scratch=(), smem=(), fence=(), flops=0, nbytes=0, trans=0, vmem=16):
    specs = [
        pl.BlockSpec(
            memory_space=pltpu.SMEM if i in smem else pl.ANY if i in fence else pltpu.VMEM
        )
        for i in range(len(args))
    ]
    return pl.pallas_call(
        kernel,
        out_shape=[jax.ShapeDtypeStruct(s, d) for s, d in outs],
        in_specs=specs,
        out_specs=[pl.BlockSpec(memory_space=pltpu.VMEM) for _ in outs],
        scratch_shapes=list(scratch),
        compiler_params=pltpu.CompilerParams(vmem_limit_bytes=vmem * 1024 * 1024),
        cost_estimate=pl.CostEstimate(flops=flops, bytes_accessed=nbytes, transcendentals=trans),
    )(*args)


def mm(a, b, dims=((1,), (0,))):
    return lax.dot_general(a, b, (dims, ((), ())), preferred_element_type=F32)


def head_scaled(values):
    block = lax.broadcasted_iota(jnp.int32, (C, C), 0) // 64
    same = (block == lax.broadcasted_iota(jnp.int32, (C, C), 1) // 64).astype(F32).astype(BF16)
    squares = values * values
    high = squares.astype(BF16)
    low = (squares - high.astype(F32)).astype(BF16)
    return values * lax.rsqrt(mm(high, same) + mm(low, same) + EPS_NORM)


def pool_kernel(feat, out):
    total = feat[0].astype(F32)
    for r in range(1, HB):
        total = total + feat[r].astype(F32)
    mean = (total * (1.0 / HB)).astype(BF16)
    for i in range(N_ROW):
        out[i] = mean


def prepare_kernel(tiles, after, feat, cot, layer_scale, d_branch, occ, first, last):
    pixel = lax.broadcasted_iota(jnp.int32, (PIX, 1), 0)
    tile = (pixel // (TS * WB)) * (WB // TS) + (pixel % WB) // TS
    weight = jnp.zeros((PIX, 1), F32)
    for i in range(TILES):
        weight = jnp.where(tile == tiles[i], 1.0, weight)
    occ[...] = weight
    value = (cot[...].astype(F32) * layer_scale[...] * weight).astype(BF16)
    d_branch[...] = value
    n = 2 * HALO * WB
    m = HALO * WB
    first[:n, :] = feat[:n, :]
    first[n:, :] = value[:m]
    last[:n, :] = feat[PIX - n :, :]
    last[n:, :] = value[PIX - m :]


def split_columns(rows):
    shaped = rows.reshape(rows.shape[0] // WB, 2, WB // 2, rows.shape[1])
    return [shaped[:, h].reshape(-1, rows.shape[1]) for h in range(2)]


def stacked_rows(feat, above, below):
    n = 2 * HALO * WB
    return jnp.concatenate([above[:n, :], feat[...], below[:n, :]], axis=0)


def query_kernel(feat, above, below, w_query, out):
    query = head_scaled(mm(stacked_rows(feat, above, below), w_query[...]))
    for h, half in enumerate(split_columns(query)):
        out[h] = half.astype(BF16)


def attention_kernel(
    scale, valid, pooled, query, feat, above, below, w_key, w_value, w_out,
    mixed, first, last, grid, edges,
):
    rows = pooled[...]
    all_keys = split_columns(head_scaled(mm(rows, w_key[...])))
    all_values = split_columns(mm(rows, w_value[...]))
    all_feat = split_columns(stacked_rows(feat, above, below).astype(F32))
    half = WB // 2
    n_query, n_keys = ROWS_M * half, N_ROW * half
    same = (
        lax.broadcasted_iota(jnp.int32, (n_query, n_keys), 0) % half
        == lax.broadcasted_iota(jnp.int32, (n_query, n_keys), 1) % half
    )
    lower = lax.broadcasted_iota(jnp.int32, (n_query, 128), 1) < 64
    row = lax.broadcasted_iota(jnp.int32, (n_query, 1), 0) // half
    inside = ((row >= 2 * HALO) | (valid[0] > 0)) & ((row < 2 * HALO + HB) | (valid[1] > 0))
    for h in range(2):
        keys, values = all_keys[h].astype(BF16), all_values[h].astype(BF16)
        pairs = []
        for pair in range(HEADS // 2):
            lanes = slice(128 * pair, 128 * pair + 128)
            q = query[h, :, lanes].astype(F32)
            parts = []
            for sub in range(2):
                q_half = jnp.where(lower if sub == 0 else ~lower, q, 0.0).astype(BF16)
                scores = mm(q_half, keys[:, lanes], ((1,), (1,)))
                weight = jnp.where(same, jnp.exp(scores * scale[2 * pair + sub]), 0.0)
                total = jnp.sum(weight, axis=1, keepdims=True)
                parts.append(mm(weight.astype(BF16), values[:, lanes]) / total)
            pairs.append(jnp.where(lower, parts[0], parts[1]).astype(BF16))
        attended = jnp.concatenate(pairs, axis=1)
        out = jnp.where(inside, all_feat[h] + mm(attended, w_out[...]), 0.0)
        grid[:, half * h : half * h + half, :] = out.reshape(ROWS_M, half, C)
    mixed[...] = grid[...].reshape(ROWS_M * WB, C).astype(BF16)
    column_edges(grid, edges, ROWS_M, first, last)


def column_edges(grid, edges, n_rows, first, last):
    edges[...] = jnp.zeros_like(edges)
    for r in range(n_rows):
        edges[0, HALO * r : HALO * r + HALO, :] = grid[r, :HALO, :]
        edges[1, HALO * r : HALO * r + HALO, :] = grid[r, WB - HALO :, :]
    first[...] = edges[0].astype(BF16)
    last[...] = edges[1].astype(BF16)


def fill_window(win, own, left, right, n_rows):
    for r in range(n_rows):
        win[r, 8 : 8 + WB, :] = own[r * WB : (r + 1) * WB, :].astype(F32)
    lcols = left[...].astype(F32)
    rcols = right[...].astype(F32)
    for r in range(n_rows):
        win[r, 8 - HALO : 8, :] = lcols[HALO * r : HALO * r + HALO]
        win[r, 8 + WB : 8 + WB + HALO, :] = rcols[HALO * r : HALO * r + HALO]


def depthwise(win, taps, n_out, start, flip, store):
    half = WB // 2
    for t in range(TILES_L):
        lanes = slice(128 * t, 128 * t + 128)
        for h in range(2):
            acc = [start(r, half * h, lanes) for r in range(n_out)]
            for dj in range(7):
                at = 8 - HALO + half * h + dj
                cols = [win[r, at : at + half, lanes] for r in range(n_out + 6)]
                for di in range(7):
                    tap = 7 * di + dj if not flip else 7 * (6 - di) + (6 - dj)
                    k = taps[tap : tap + 1, lanes]
                    for r in range(n_out):
                        acc[r] = acc[r] + cols[r + di] * k
            for r in range(n_out):
                store(r, half * h, lanes, acc[r])


def rowsum(a):
    return jnp.sum(a, axis=0, keepdims=True)


def sublayer_kernel(
    mixed, left, right, d_branch_own, above, below, cot, occ, taps, dw_bias, ln_gain, ln_bias,
    w_up, b_up, w_down, b_down, layer_scale,
    output, d_out, d_first, d_last, win_out, lnout_out, hidden_out, d_pre_out, sums,
    win, spat, grid, edges,
):
    fill_window(win, mixed, left, right, ROWS_M)
    win_out[...] = win[HALO : HALO + ROWS_D].astype(BF16)

    def start(r, j, lanes):
        return jnp.broadcast_to(dw_bias[:, lanes], (WB // 2, 128))

    def store(r, j, lanes, value):
        spat[r * WB + j : r * WB + j + WB // 2, lanes] = value

    depthwise(win, taps, ROWS_D, start, False, store)
    spatial = spat[...]
    center = spatial - jnp.mean(spatial, axis=1, keepdims=True)
    inv_std = lax.rsqrt(jnp.mean(center * center, axis=1, keepdims=True) + EPS_NORM)
    standard = center * inv_std
    gain = ln_gain[...]
    lnout = (standard * gain + ln_bias[...]).astype(BF16)
    lnout_out[...] = lnout[OWN]
    preact = mm(lnout, w_up[...]) + b_up[...]
    square = 0.044715 * preact * preact
    tanh_val = jnp.tanh(GELU_SCALE * preact * (1.0 + square))
    hidden = (0.5 * preact[OWN] * (1.0 + tanh_val[OWN])).astype(BF16)
    slope = 0.5 * (1.0 + tanh_val) + 0.5 * preact * (1.0 - tanh_val * tanh_val) * GELU_SCALE * (
        1.0 + 3.0 * square
    )
    hidden_out[...] = hidden
    n = 2 * HALO * WB
    d_branch_b = jnp.concatenate([above[n:, :], d_branch_own[...], below[n:, :]], axis=0)
    d_pre = mm(d_branch_b, w_down[...], ((1,), (1,))) * slope
    d_pre_b = d_pre.astype(BF16)
    d_pre_out[...] = d_pre_b[OWN]
    d_lnout = mm(d_pre_b, w_up[...], ((1,), (1,)))
    e = d_lnout * gain
    d_spatial = inv_std * (
        e
        - jnp.mean(e, axis=1, keepdims=True)
        - standard * jnp.mean(e * standard, axis=1, keepdims=True)
    )
    d_out[...] = d_spatial
    grid[...] = d_spatial.reshape(ROWS_D, WB, C)
    column_edges(grid, edges, ROWS_D, d_first, d_last)
    weight = occ[...]
    scale = layer_scale[...]
    cotan = cot[...].astype(F32)
    branch = (mm(hidden, w_down[...]) + b_down[...]) * weight
    output[...] = (mixed[2 * HALO * WB : 2 * HALO * WB + PIX, :].astype(F32) + scale * branch).astype(BF16)
    d_lnout = d_lnout[OWN]
    sums[0:1, :C] = rowsum(d_spatial[OWN])
    sums[1:2, :C] = rowsum(d_lnout * standard[OWN])
    sums[2:3, :C] = rowsum(d_lnout)
    sums[3:4, :C] = rowsum(cotan * scale * weight)
    sums[4:5, :C] = rowsum(cotan * branch)
    sums[5:6, :] = rowsum(d_pre[OWN])


def up_order():
    chan = np.arange(C).reshape(N_YL, N_X, N_C, N_Z // 2, 3).transpose(4, 2, 1, 0, 3).reshape(-1)
    return (np.arange(C)[:, None] == chan[None, :]).astype(np.float32)


def gradient_kernel(
    core, order, lnout, hidden, d_pre, d_branch, win_in, d_spatial, sums, mine, other, win, down, small
):
    is_zero = core[0] == 0

    def put(row, x, zero, one):
        size = zero.shape[0]
        mine[x, row : row + size, :] = jnp.where(is_zero, zero, one).astype(BF16)
        other[x, row : row + size, :] = jnp.where(is_zero, one, zero).astype(BF16)

    ordered = mm(lnout[...], order[...]).astype(BF16)
    ups = [mm(ordered[:, 128 * r : 128 * r + 128], d_pre[...], ((0,), (0,))) for r in range(3)]
    for q in range(4):
        for k, (r, t) in enumerate(UP_TILES[q]):
            for x in range(N_X):
                pair = [ups[r][64 * c + 16 * x : 64 * c + 16 * x + 16, 128 * t : 128 * t + 128] for c in range(2)]
                put((q * 8 + k) * 16, x, *pair)
    full = mm(hidden[...], d_branch[...], ((0,), (0,)))
    for t in range(TILES_L):
        down[t] = full[:, 128 * t : 128 * t + 128]
    for yh in range(2):
        for k, (s, t) in enumerate(DOWN_TILES[yh]):
            for x in range(N_X):
                for two in range(2):
                    pair = [
                        jnp.concatenate(
                            [
                                down[t, pl.ds(5 * (64 * yl + 16 * x + 8 * c) + s, 8, stride=5), :]
                                for yl in (2 * two, 2 * two + 1)
                            ],
                            axis=0,
                        )
                        for c in range(2)
                    ]
                    put(512 + (yh * 8 + k) * 32 + 16 * two, x, *pair)
    win[...] = win_in[...].astype(F32)
    small[...] = jnp.zeros_like(small)
    for t in range(TILES_L):
        lanes = slice(128 * t, 128 * t + 128)
        d_rows = [d_spatial[(HALO + r) * WB : (HALO + r + 1) * WB, lanes] for r in range(HB)]
        for dj in range(7):
            cols = [win[r, 5 + dj : 5 + dj + WB, lanes] for r in range(HB + 6)]
            for di in range(7):
                acc = cols[di] * d_rows[0]
                for r in range(1, HB):
                    acc = acc + cols[r + di] * d_rows[r]
                at = 56 * t + 7 * di + dj
                small[at : at + 1, :] = rowsum(acc)
    for i in range(5):
        for t in range(TILES_L):
            small[161 + 3 * i + t : 162 + 3 * i + t, :] = sums[i : i + 1, 128 * t : 128 * t + 128]
    for t in range(HID // 128):
        small[176 + t : 177 + t, :] = sums[5:6, 128 * t : 128 * t + 128]
    for x in range(N_X):
        pair = [
            jnp.concatenate([small[96 * c + 24 * x : 96 * c + 24 * x + 24], jnp.zeros((8, 128), F32)], axis=0)
            for c in range(2)
        ]
        put(1024, x, *pair)


def spread_kernel(part, d_first, d_last, out, d_first_out, d_last_out, total):
    d_first_out[...] = d_first[...]
    d_last_out[...] = d_last[...]
    total[...] = (
        (part[0].astype(F32) + part[1].astype(F32)) + (part[2].astype(F32) + part[3].astype(F32))
    )
    small = total[1024 : 1024 + SMALL, :]
    for yl in range(N_YL):
        for z in range(N_Z):
            for yh in range(N_YH):
                q = (z % 2) * 2 + yh
                up = total[pl.ds(q * 128 + yl * 4 + z // 2, 8, stride=16), :]
                down = total[pl.ds(512 + yh * 256 + yl * 8 + z, 8, stride=32), :]
                record = jnp.concatenate([up, down, small], axis=0)
                out[(yl * N_Z + z) * N_YH + yh] = record.astype(BF16)


def gather_kernel(part, share, small):
    total = part[0].astype(F32)
    for i in range(1, N_YZ):
        total = total + part[i].astype(F32)
    share[...] = total[:16]
    for i in range(N_X * N_C):
        small[i] = total[16:]


def final_kernel(small, dw, *vectors):
    for t in range(TILES_L):
        dw[:, 128 * t : 128 * t + 128] = small[56 * t : 56 * t + 49, :]
    for i in range(5):
        for t in range(TILES_L):
            vectors[i][pl.ds(128 * t, 128)] = small[161 + 3 * i + t, :]
    for t in range(HID // 128):
        vectors[5][pl.ds(128 * t, 128)] = small[176 + t, :]


def grad_mixed_kernel(d_all, left, right, cot, taps, out, win):
    fill_window(win, d_all, left, right, ROWS_D)

    def start(r, j, lanes):
        return cot[r * WB : (r + 1) * WB, lanes].astype(F32)[j : j + WB // 2]

    def store(r, j, lanes, value):
        out[r * WB + j : r * WB + j + WB // 2, lanes] = value

    depthwise(win, taps, HB, start, True, store)


def core_sum_kernel(mine, got, out):
    out[...] = (mine[...].astype(F32) + got[...].astype(F32)).astype(BF16)


def neighbours(before_edge, after_edge, axes):
    size = lax.axis_size(axes)
    up = [(i, i + 1) for i in range(size - 1)]
    down = [(i + 1, i) for i in range(size - 1)]
    return lax.ppermute(after_edge, axes, up), lax.ppermute(before_edge, axes, down)


def body(
    features, w_query, w_key, w_value, w_out, logit_scale, dw_kernel, dw_bias, ln_gain, ln_bias,
    w_up, b_up, w_down, b_down, layer_scale, cotangent, tile_list,
):
    row = lambda v: v.reshape(1, -1)
    flat = features.reshape(PIX, C)
    cot = cotangent.reshape(PIX, C)

    (copies,) = call(pool_kernel, [((N_ROW, WB, C), BF16)], features, nbytes=500_000)
    pooled = lax.all_to_all(copies, ROW, 0, 0, tiled=True).reshape(N_ROW * WB, C)

    shared = ((3 * HALO * WB, C), BF16)
    d_branch, occ, feat_first, feat_last = call(
        prepare_kernel, [((PIX, C), BF16), ((PIX, 1), F32), shared, shared],
        tile_list.reshape(-1), copies, flat, cot, row(layer_scale), smem=(0,), fence=(1,), nbytes=800_000,
    )
    above, below = neighbours(feat_first, feat_last, ROW)
    (query,) = call(
        query_kernel, [((2, ROWS_M * WB // 2, C), BF16)], flat, above, below, w_query,
        flops=2 * 10**8, nbytes=900_000,
    )
    at_row = lax.axis_index(ROW)
    valid = jnp.stack([at_row > 0, at_row < N_ROW - 1]).astype(jnp.int32)
    edge = ((64, C), BF16)
    mixed, first, last = call(
        attention_kernel, [((ROWS_M * WB, C), BF16), edge, edge],
        logit_scale, valid, pooled, query, flat, above, below, w_key, w_value, w_out,
        scratch=[pltpu.VMEM((ROWS_M, WB, C), F32), pltpu.VMEM((2, 64, C), F32)],
        smem=(0, 1), flops=10**9, nbytes=2_000_000, trans=500_000,
    )
    left, right = neighbours(first, last, COL)

    d_edge = ((48, C), BF16)
    output, d_all, d_first, d_last, win, lnout, hidden, d_pre, sums = call(
        sublayer_kernel,
        [
            ((PIX, C), BF16), ((ROWS_D * WB, C), F32), d_edge, d_edge, ((ROWS_D, WCOL, C), BF16),
            ((PIX, C), BF16), ((PIX, HID), BF16), ((PIX, HID), BF16), ((8, HID), F32),
        ],
        mixed, left, right, d_branch, above, below, cot, occ, dw_kernel, row(dw_bias),
        row(ln_gain), row(ln_bias), w_up, row(b_up), w_down, row(b_down), row(layer_scale),
        scratch=[
            pltpu.VMEM((ROWS_M, WCOL, C), F32), pltpu.VMEM((ROWS_D * WB, C), F32),
            pltpu.VMEM((ROWS_D, WB, C), F32), pltpu.VMEM((2, 48, C), F32),
        ],
        flops=10**9, nbytes=4_000_000, trans=300_000, vmem=24,
    )

    core = lax.axis_index("c").reshape(1)
    order = jnp.asarray(up_order(), BF16)
    record = ((N_X, REC, 128), BF16)
    mine, other = call(
        gradient_kernel, [record, record],
        core, order, lnout, hidden, d_pre, d_branch, win, d_all, sums,
        scratch=[
            pltpu.VMEM((ROWS_D, WCOL, C), F32),
            pltpu.VMEM((TILES_L, HID, 128), F32),
            pltpu.VMEM((8 * SMALL, 128), F32),
        ],
        smem=(0,), flops=2 * 10**9, nbytes=4_000_000,
    )
    got = lax.ppermute(other, "c", [(0, 1), (1, 0)])
    (part,) = call(core_sum_kernel, [record], mine, got, nbytes=3_000_000)
    part = lax.all_to_all(part, "x", 0, 0, tiled=True)
    part, d_first, d_last = call(
        spread_kernel, [((N_YZ, 16 + SMALL, 128), BF16), d_edge, d_edge], part, d_first, d_last,
        scratch=[pltpu.VMEM((REC, 128), F32)], nbytes=2_000_000,
    )
    part = lax.all_to_all(part, YZ, 0, 0, tiled=True)
    d_left, d_right = neighbours(d_first, d_last, COL)
    share, small = call(
        gather_kernel, [((16, 128), F32), ((N_X * N_C, SMALL, 128), F32)], part, nbytes=800_000
    )
    small = lax.all_to_all(small, CX, 0, 0, tiled=True)
    vectors = call(
        final_kernel, [((49, C), F32)] + [((C,), F32)] * 5 + [((HID,), F32)],
        small.reshape(-1, 128), nbytes=200_000,
    )
    share = share.reshape(2, 8 * 128)
    share = jnp.where(lax.axis_index("yh") == 0, share[:, :SHARE], share[:, 8 * 128 - SHARE :])
    (grad_mixed,) = call(
        grad_mixed_kernel, [((PIX, C), F32)], d_all, d_left, d_right, cot, dw_kernel,
        scratch=[pltpu.VMEM((ROWS_D, WCOL, C), F32)], flops=10**7, nbytes=1_000_000,
    )
    bias, gain, shift, b_down_grad, scale_grad, b_up_grad = vectors[1:]
    return (
        output.reshape(HB, WB, C), grad_mixed.reshape(HB, WB, C), share[0], share[1],
        vectors[0], bias, gain, shift, b_up_grad, b_down_grad, scale_grad,
    )


def solution(mesh):
    mesh = Mesh(mesh.devices.reshape(N_YL, N_X, N_C, N_Z, N_YH), ROW + COL)
    block = P(ROW, COL, None)
    in_specs = (block,) + (P(),) * 14 + (block, block)
    out_specs = (block, block, P(ROW + COL), P(ROW + COL)) + (P(),) * 7
    return jax.shard_map(body, mesh=mesh, in_specs=in_specs, out_specs=out_specs, check_vma=False)
```

time: 147 us -> 127 us (0.86)
  waiting for transfers between devices: 56.1 us -> 32.3 us
  blocking collectives: 0 us -> 17.5 us
  starting transfers between devices: 65 us -> 54.8 us
  other arithmetic: 3.82 us -> 0.15 us
  Pallas kernels: 17 us -> 19 us
  local copies, waits for them, and re-layouts: 3.28 us -> 1.62 us
    all_to_all x1, waiting for transfers between devices: 18.1 us -> 0.01 us  [body(): part = lax.all_to_all(part, YZ, 0, 0, tiled=True)]
    all_to_all x0 -> x1, blocking collectives: none -> 17.5 us  [body(): part = lax.all_to_all(part, 'x', 0, 0, tiled=True)]
    all_to_all x1, waiting for transfers between devices: 13.4 us -> 2.24 us  [body(): lax.all_to_all(copies, ROW, 0, 0, tiled=True).reshape(N_ROW * WB, C)]
    all_to_all x1 -> x0, starting transfers between devices: 8.41 us -> none  [body(): part = lax.all_to_all(part, 'x', 0, 0, tiled=True)]
    pallas_call x6 -> x0, other arithmetic: 3.59 us -> none  [call(): pl.pallas_call(kernel, out_shape=[jax.ShapeDtypeStruct(s, d) for s, d in...]
    ppermute x4 -> x3, starting transfers between devices: 6.91 us -> 4.5 us  [neighbours(): lax.ppermute(before_edge, axes, down)]
    ppermute x1, waiting for transfers between devices: 0.01 us -> 2.31 us  [body(): got = lax.ppermute(other, 'c', [(0, 1), (1, 0)])]
    ppermute x4 -> x3, starting transfers between devices: 15.9 us -> 13.6 us  [neighbours(): lax.ppermute(after_edge, axes, up)]
  transfers between devices with their start and end apart: 13 -> 10, of which waited for: 8 -> 8; matrix products, arithmetic and copies ran while one was open for 1% -> 1% of each run, Pallas kernels for 2% -> 3%
where the time goes in v3:
time: 127 us; the launch traced here: 126 us
  starting transfers between devices  54.8 us (43%)
  waiting for transfers between devices  32.3 us (25%)
  Pallas kernels  19 us (15%)
  blocking collectives  17.5 us (14%)
  local copies, waits for them, and re-layouts  1.62 us (1%)
    ppermute x3, waiting for transfers between devices, neighbours(): lax.ppermute(before_edge, axes, down)  21.5 us
    pallas_call x11, Pallas kernels, call(): pl.pallas_call(kernel, out_shape=[jax.ShapeDtypeStruct(s, d) for s, d in...  19 us
    all_to_all x1, blocking collectives, body(): part = lax.all_to_all(part, 'x', 0, 0, tiled=True)  17.5 us
    all_to_all x1, starting transfers between devices, body(): part = lax.all_to_all(part, YZ, 0, 0, tiled=True)  16.3 us
    ppermute x3, starting transfers between devices, neighbours(): lax.ppermute(after_edge, axes, up)  13.6 us
    all_to_all x1, starting transfers between devices, body(): lax.all_to_all(copies, ROW, 0, 0, tiled=True).reshape(N_ROW * WB, C)  10.6 us
    all_to_all x1, starting transfers between devices, body(): small = lax.all_to_all(small, CX, 0, 0, tiled=True)  6.56 us
    ppermute x3, starting transfers between devices, neighbours(): lax.ppermute(before_edge, axes, down)  4.5 us
  transfers between devices with their start and end apart: 10, of which 8 were waited for; matrix products, arithmetic and copies ran while one was open for 1% of the time, Pallas kernels for 3%

profile of v3, /device:TPU:1, one launch (start us, length us, event | category | flops | bytes accessed | tf_op | source)
XLA Modules:
  0.0 126.3 jit_solution(10943627570297546535)
XLA Ops:
  0.7 0.9 copy-done
  2.4 10.6 %all-to-all-start = ((bf16[32,16,384]{2,1,0:T(8,128)(2,1)}), bf16[32,16,384]{2,1,0:T(8,128)(2,1)S(1)}, u32[]{:S(2)}, u32[]{:S(2)}) async-start(bf16[32,16,384]{2,1,0:T(8,128)(2,1)} %shard_map.257.after), calls=%async_computation | async-start | bytes 786432 | tf_op jit(solution)/shard_map/all_to_all | solution.py:397
  13.6 3.5 %collective-permute-start = (bf16[144,384]{1,0:T(8,128)(2,1)S(1)}, bf16[144,384]{1,0:T(8,128)(2,1)S(1)}, u32[]{:S(2)}, u32[]{:S(2)}) collective-permute-start(bf16[144,384]{1,0:T(8,128)(2,1)S(1)} %get-tuple-element.41), channel_id=1, source_target_pairs={{0,16},{16,32},{32,48},{48,64},{64,80},{80,96},{96,112},{112,128},... | collective-permute-start | bytes 331784 | tf_op jit(solution)/shard_map/ppermute | solution.py:385
  17.2 1.9 %collective-permute-start.1 = (bf16[144,384]{1,0:T(8,128)(2,1)S(1)}, bf16[144,384]{1,0:T(8,128)(2,1)S(1)}, u32[]{:S(2)}, u32[]{:S(2)}) collective-permute-start(bf16[144,384]{1,0:T(8,128)(2,1)S(1)} %get-tuple-element.42), channel_id=1, source_target_pairs={{16,0},{32,16},{48,32},{64,48},{80,64},{96,80},{112,96},{128,112},... | collective-permute-start | bytes 331784 | tf_op jit(solution)/shard_map/ppermute | solution.py:385
  19.3 4.6 %collective-permute-done.1.below = bf16[144,384]{1,0:T(8,128)(2,1)S(1)} collective-permute-done((bf16[144,384]{1,0:T(8,128)(2,1)S(1)}, bf16[144,384]{1,0:T(8,128)(2,1)S(1)}, u32[]{:S(2)}, u32[]{:S(2)}) %collective-permute-start.1) | collective-permute-done | bytes 110624 | tf_op jit(solution)/shard_map/ppermute | solution.py:385
  24.6 2.2 %all-to-all-done = bf16[32,16,384]{2,1,0:T(8,128)(2,1)S(1)} async-done(((bf16[32,16,384]{2,1,0:T(8,128)(2,1)}), bf16[32,16,384]{2,1,0:T(8,128)(2,1)S(1)}, u32[]{:S(2)}, u32[]{:S(2)}) %all-to-all-start) | async-done | bytes 393248 | tf_op jit(solution)/shard_map/all_to_all | solution.py:397
  26.9 2.8 %shard_map.260 = (bf16[320,384]{1,0:T(8,128)(2,1)S(1)}, bf16[64,384]{1,0:T(8,128)(2,1)S(1)}, bf16[64,384]{1,0:T(8,128)(2,1)S(1)}) custom-call(f32[6]{0:T(128)S(1)} %copy-done.11, s32[2]{0:T(128)S(1)} %add_convert_fusion.valid, bf16[512,384]{1,0:T(8,128)(2,1)S(1)} %bitcast.18, bf16[2,160,384]{2,1,0:T(8,128)(2,1)S(1)} %shard_map.259.query, ...), custom_call_target="tpu_custom_call" | custom-call | flops 1000000000 | bytes 2000000 | tf_op jit(solution)/shard_map/pallas_call | solution.py:58
  29.7 3.2 %collective-permute-start.2 = (bf16[64,384]{1,0:T(8,128)(2,1)S(1)}, bf16[64,384]{1,0:T(8,128)(2,1)S(1)}, u32[]{:S(2)}, u32[]{:S(2)}) collective-permute-start(bf16[64,384]{1,0:T(8,128)(2,1)S(1)} %get-tuple-element.44), channel_id=1, source_target_pairs={{0,1},{1,2},{2,3},{3,4},{4,5},{5,6},{6,7},{7,8},{8,9},{9,10},{10,1... | collective-permute-start | bytes 147464 | tf_op jit(solution)/shard_map/ppermute | solution.py:385
  32.9 1.3 %collective-permute-start.3 = (bf16[64,384]{1,0:T(8,128)(2,1)S(1)}, bf16[64,384]{1,0:T(8,128)(2,1)S(1)}, u32[]{:S(2)}, u32[]{:S(2)}) collective-permute-start(bf16[64,384]{1,0:T(8,128)(2,1)S(1)} %get-tuple-element.45), channel_id=1, source_target_pairs={{1,0},{2,1},{3,2},{4,3},{5,4},{6,5},{7,6},{8,7},{9,8},{10,9},{11,1... | collective-permute-start | bytes 147464 | tf_op jit(solution)/shard_map/ppermute | solution.py:385
  34.4 7.3 %collective-permute-done.3.right = bf16[64,384]{1,0:T(8,128)(2,1)S(1)} collective-permute-done((bf16[64,384]{1,0:T(8,128)(2,1)S(1)}, bf16[64,384]{1,0:T(8,128)(2,1)S(1)}, u32[]{:S(2)}, u32[]{:S(2)}) %collective-permute-start.3) | collective-permute-done | bytes 49184 | tf_op jit(solution)/shard_map/ppermute | solution.py:385
  41.7 6.5 %shard_map.261 = (bf16[128,384]{1,0:T(8,128)(2,1)}, f32[224,384]{1,0:T(8,128)S(1)}, bf16[48,384]{1,0:T(8,128)(2,1)S(1)}, bf16[48,384]{1,0:T(8,128)(2,1)S(1)}, bf...) custom-call(bf16[320,384]{1,0:T(8,128)(2,1)S(1)} %get-tuple-element., ...), custom_call_target="tpu_custom_call" | custom-call | flops 1000000000 | bytes 4000000 | tf_op jit(solution)/shard_map/pallas_call | solution.py:58
  48.2 2.2 %shard_map.262 = (bf16[4,1056,128]{2,1,0:T(8,128)(2,1)S(1)}, bf16[4,1056,128]{2,1,0:T(8,128)(2,1)S(1)}) custom-call(s32[1]{0:T(128)} %bitcast.7.core, bf16[384,384]{1,0:T(8,128)(2,1)S(1)} %copy-done.12, bf16[128,384]{1,0:T(8,128)(2,1)S(1)} %get-tuple-element.50.lnout, bf16[128,1280]{1,0:T(8,128)(2,1)S(1)} %get-tuple-element.51.hidden, ...), custom_call_target="tpu_custom_call" | custom-call | flops 2000000000 | bytes 4000000 | tf_op jit(solution)/shard_map/pallas_call | solution.py:58
  50.4 3.3 %collective-permute-start.4 = (bf16[4,1056,128]{2,1,0:T(8,128)(2,1)S(1)}, bf16[4,1056,128]{2,1,0:T(8,128)(2,1)S(1)}, u32[]{:S(2)}, u32[]{:S(2)}) collective-permute-start(bf16[4,1056,128]{2,1,0:T(8,128)(2,1)S(1)} %get-tuple-element.56), channel_id=1, source_target_pairs={{0,16},{16,0},{1,17},{17,1},{2,18},{18,2},{3,19},{19,3},{4,20},{20... | collective-permute-start | bytes 3244040 | tf_op jit(solution)/shard_map/ppermute | solution.py:449
  53.7 2.3 %collective-permute-done.4.got = bf16[4,1056,128]{2,1,0:T(8,128)(2,1)S(1)} collective-permute-done((bf16[4,1056,128]{2,1,0:T(8,128)(2,1)S(1)}, bf16[4,1056,128]{2,1,0:T(8,128)(2,1)S(1)}, u32[]{:S(2)}, u32[]{:S(2)}) %collective-permute-start.4) | collective-permute-done | bytes 1081376 | tf_op jit(solution)/shard_map/ppermute | solution.py:449
  56.3 17.5 %all_to_all.20.part = bf16[4,1056,128]{2,1,0:T(8,128)(2,1)S(1)} all-to-all(bf16[4,1056,128]{2,1,0:T(8,128)(2,1)S(1)} %shard_map.263), channel_id=1, replica_groups=mesh['yl'=4,'x'=4,'c'=2,'z'=8,'yh'=2] {'x'}, dimensions={0} | all-to-all | bytes 2162688 | tf_op jit(solution)/shard_map/all_to_all | solution.py:451
  73.8 1.3 %shard_map.264 = (bf16[64,40,128]{2,1,0:T(8,128)(2,1)}, bf16[48,384]{1,0:T(8,128)(2,1)S(1)}, bf16[48,384]{1,0:T(8,128)(2,1)S(1)}) custom-call(bf16[4,1056,128]{2,1,0:T(8,128)(2,1)S(1)} %all_to_all.20.part, bf16[48,384]{1,0:T(8,128)(2,1)S(1)} %get-tuple-element.57.d_first, bf16[48,384]{1,0:T(8,128)(2,1)S(1)} %get-tuple-element.58.d_last), custom_call_target="tpu_custom_call" | custom-call | bytes 2000000 | tf_op jit(solution)/shard_map/pallas_call | solution.py:58
  75.1 16.3 %all-to-all-start.2 = ((bf16[64,40,128]{2,1,0:T(8,128)(2,1)}), bf16[64,40,128]{2,1,0:T(8,128)(2,1)S(1)}, u32[]{:S(2)}, u32[]{:S(2)}) async-start(bf16[64,40,128]{2,1,0:T(8,128)(2,1)} %get-tuple-element.61), calls=%async_computation.2 | async-start | bytes 1310720 | tf_op jit(solution)/shard_map/all_to_all | solution.py:456
  91.4 6.8 %collective-permute-start.5 = (bf16[48,384]{1,0:T(8,128)(2,1)S(1)}, bf16[48,384]{1,0:T(8,128)(2,1)S(1)}, u32[]{:S(2)}, u32[]{:S(2)}) collective-permute-start(bf16[48,384]{1,0:T(8,128)(2,1)S(1)} %get-tuple-element.59), channel_id=1, source_target_pairs={{0,1},{1,2},{2,3},{3,4},{4,5},{5,6},{6,7},{7,8},{8,9},{9,10},{10,1... | collective-permute-start | bytes 110600 | tf_op jit(solution)/shard_map/ppermute | solution.py:385
  98.2 1.3 %collective-permute-start.6 = (bf16[48,384]{1,0:T(8,128)(2,1)S(1)}, bf16[48,384]{1,0:T(8,128)(2,1)S(1)}, u32[]{:S(2)}, u32[]{:S(2)}) collective-permute-start(bf16[48,384]{1,0:T(8,128)(2,1)S(1)} %get-tuple-element.60), channel_id=1, source_target_pairs={{1,0},{2,1},{3,2},{4,3},{5,4},{6,5},{7,6},{8,7},{9,8},{10,9},{11,1... | collective-permute-start | bytes 110600 | tf_op jit(solution)/shard_map/ppermute | solution.py:385
  99.5 1.8 %collective-permute-done.5.left = bf16[48,384]{1,0:T(8,128)(2,1)S(1)} collective-permute-done((bf16[48,384]{1,0:T(8,128)(2,1)S(1)}, bf16[48,384]{1,0:T(8,128)(2,1)S(1)}, u32[]{:S(2)}, u32[]{:S(2)}) %collective-permute-start.5) | collective-permute-done | bytes 36896 | tf_op jit(solution)/shard_map/ppermute | solution.py:385
  101.4 9.6 %collective-permute-done.6.right = bf16[48,384]{1,0:T(8,128)(2,1)S(1)} collective-permute-done((bf16[48,384]{1,0:T(8,128)(2,1)S(1)}, bf16[48,384]{1,0:T(8,128)(2,1)S(1)}, u32[]{:S(2)}, u32[]{:S(2)}) %collective-permute-start.6) | collective-permute-done | bytes 36896 | tf_op jit(solution)/shard_map/ppermute | solution.py:385
  110.9 2.4 %shard_map.265 = f32[128,384]{1,0:T(8,128)} custom-call(f32[224,384]{1,0:T(8,128)S(1)} %get-tuple-element.49.d_spatial.d_all, bf16[48,384]{1,0:T(8,128)(2,1)S(1)} %collective-permute-done.5.left, bf16[48,384]{1,0:T(8,128)(2,1)S(1)} %collective-permute-done.6.right, bf16[128,384]{1,0:T(8,128)(2,1)S(1)} %bitcast.17, f32[49,384]{1,0:T(8,128)S(1)} %copy-done.4), custom_call_target="tpu_custom_call" | custom-call | flops 10000000 | bytes 1000000 | tf_op jit(solution)/shard_map/pallas_call | solution.py:58
  114.1 6.6 %all-to-all-start.3 = ((f32[8,24,128]{2,1,0:T(8,128)}), f32[8,24,128]{2,1,0:T(8,128)S(1)}, u32[]{:S(2)}, u32[]{:S(2)}) async-start(f32[8,24,128]{2,1,0:T(8,128)} %get-tuple-element.63), calls=%async_computation.3 | async-start | bytes 196608 | tf_op jit(solution)/shard_map/all_to_all | solution.py:461
  121.4 4.3 %all-to-all-done.3 = f32[8,24,128]{2,1,0:T(8,128)S(1)} async-done(((f32[8,24,128]{2,1,0:T(8,128)}), f32[8,24,128]{2,1,0:T(8,128)S(1)}, u32[]{:S(2)}, u32[]{:S(2)}) %all-to-all-start.3) | async-done | bytes 98336 | tf_op jit(solution)/shard_map/all_to_all | solution.py:461
  (56 shorter events, 4.8 us)
Async XLA Ops:
  1.5 11.4 %copy-start.14 = (f32[384]{0:T(512)S(1)}, f32[384]{0:T(512)}, u32[]{:S(2)}) copy-start(f32[384]{0:T(512)} %param.32) | copy-start | bytes 4612
  1.5 11.4 %copy-start.1 = (bf16[8,16,384]{2,1,0:T(8,128)(2,1)S(1)}, bf16[8,16,384]{2,1,0:T(8,128)(2,1)}, u32[]{:S(2)}) copy-start(bf16[8,16,384]{2,1,0:T(8,128)(2,1)} %feat.1) | copy-start | bytes 294916
  1.5 11.4 %copy-start.2 = (bf16[8,16,384]{2,1,0:T(8,128)(2,1)S(1)}, bf16[8,16,384]{2,1,0:T(8,128)(2,1)}, u32[]{:S(2)}) copy-start(bf16[8,16,384]{2,1,0:T(8,128)(2,1)} %param.33) | copy-start | bytes 294916
  1.5 11.4 %copy-start.5 = (s32[1,1,8]{2,1,0:T(1,128)S(1)}, s32[1,1,8]{2,1,0:T(1,128)}, u32[]{:S(2)}) copy-start(s32[1,1,8]{2,1,0:T(1,128)} %param.34) | copy-start | bytes 100
  1.6 22.3 %copy-start.3 = (bf16[384,384]{1,0:T(8,128)(2,1)S(1)}, bf16[384,384]{1,0:T(8,128)(2,1)}, u32[]{:S(2)}) copy-start(bf16[384,384]{1,0:T(8,128)(2,1)} %w_query.1) | copy-start | bytes 884740
  2.4 24.5 %copy-start.8 = (bf16[384,384]{1,0:T(8,128)(2,1)S(1)}, bf16[384,384]{1,0:T(8,128)(2,1)}, u32[]{:S(2)}) copy-start(bf16[384,384]{1,0:T(8,128)(2,1)} %w_key.1) | copy-start | bytes 884740
  2.4 24.5 %copy-start.9 = (bf16[384,384]{1,0:T(8,128)(2,1)S(1)}, bf16[384,384]{1,0:T(8,128)(2,1)}, u32[]{:S(2)}) copy-start(bf16[384,384]{1,0:T(8,128)(2,1)} %w_value.1) | copy-start | bytes 884740
  2.4 24.5 %copy-start.10 = (bf16[384,384]{1,0:T(8,128)(2,1)S(1)}, bf16[384,384]{1,0:T(8,128)(2,1)}, u32[]{:S(2)}) copy-start(bf16[384,384]{1,0:T(8,128)(2,1)} %w_out.1) | copy-start | bytes 884740
  2.4 24.5 %copy-start.11 = (f32[6]{0:T(128)S(1)}, f32[6]{0:T(128)}, u32[]{:S(2)}) copy-start(f32[6]{0:T(128)} %scale.1) | copy-start | bytes 76
  2.4 24.5 %all-to-all-start = ((bf16[32,16,384]{2,1,0:T(8,128)(2,1)}), bf16[32,16,384]{2,1,0:T(8,128)(2,1)S(1)}, u32[]{:S(2)}, u32[]{:S(2)}) async-start(bf16[32,16,384]{2,1,0:T(8,128)(2,1)} %shard_map.257.after), calls=%async_computation | async-start | bytes 786432 | tf_op jit(solution)/shard_map/all_to_all | solution.py:397
  13.6 5.7 %collective-permute-start = (bf16[144,384]{1,0:T(8,128)(2,1)S(1)}, bf16[144,384]{1,0:T(8,128)(2,1)S(1)}, u32[]{:S(2)}, u32[]{:S(2)}) collective-permute-start(bf16[144,384]{1,0:T(8,128)(2,1)S(1)} %get-tuple-element.41), channel_id=1, source_target_pairs={{0,16},{16,32},{32,48},{48,64},{64,80},{80,96},{96,112},{112,128},... | collective-permute-start | bytes 331784 | tf_op jit(solution)/shard_map/ppermute | solution.py:385
  17.2 6.7 %collective-permute-start.1 = (bf16[144,384]{1,0:T(8,128)(2,1)S(1)}, bf16[144,384]{1,0:T(8,128)(2,1)S(1)}, u32[]{:S(2)}, u32[]{:S(2)}) collective-permute-start(bf16[144,384]{1,0:T(8,128)(2,1)S(1)} %get-tuple-element.42), channel_id=1, source_target_pairs={{16,0},{32,16},{48,32},{64,48},{80,64},{96,80},{112,96},{128,112},... | collective-permute-start | bytes 331784 | tf_op jit(solution)/shard_map/ppermute | solution.py:385
  26.9 7.4 %copy-start.18 = (f32[384]{0:T(512)S(1)}, f32[384]{0:T(512)}, u32[]{:S(2)}) copy-start(f32[384]{0:T(512)} %param.31) | copy-start | bytes 4612
  26.9 7.4 %copy-start.13 = (f32[1280]{0:T(1024)S(1)}, f32[1280]{0:T(1024)}, u32[]{:S(2)}) copy-start(f32[1280]{0:T(1024)} %param.29) | copy-start | bytes 15364
  26.9 14.8 %copy-start.4 = (f32[49,384]{1,0:T(8,128)S(1)}, f32[49,384]{1,0:T(8,128)}, u32[]{:S(2)}) copy-start(f32[49,384]{1,0:T(8,128)} %taps.3) | copy-start | bytes 225796
  26.9 14.8 %copy-start.6 = (bf16[384,1280]{1,0:T(8,128)(2,1)S(1)}, bf16[384,1280]{1,0:T(8,128)(2,1)}, u32[]{:S(2)}) copy-start(bf16[384,1280]{1,0:T(8,128)(2,1)} %w_up.1) | copy-start | bytes 2949124
  26.9 14.8 %copy-start.7 = (bf16[1280,384]{1,0:T(8,128)(2,1)S(1)}, bf16[1280,384]{1,0:T(8,128)(2,1)}, u32[]{:S(2)}) copy-start(bf16[1280,384]{1,0:T(8,128)(2,1)} %w_down.1) | copy-start | bytes 2949124
  29.7 4.6 %collective-permute-start.2 = (bf16[64,384]{1,0:T(8,128)(2,1)S(1)}, bf16[64,384]{1,0:T(8,128)(2,1)S(1)}, u32[]{:S(2)}, u32[]{:S(2)}) collective-permute-start(bf16[64,384]{1,0:T(8,128)(2,1)S(1)} %get-tuple-element.44), channel_id=1, source_target_pairs={{0,1},{1,2},{2,3},{3,4},{4,5},{5,6},{6,7},{7,8},{8,9},{9,10},{10,1... | collective-permute-start | bytes 147464 | tf_op jit(solution)/shard_map/ppermute | solution.py:385
  32.9 8.7 %collective-permute-start.3 = (bf16[64,384]{1,0:T(8,128)(2,1)S(1)}, bf16[64,384]{1,0:T(8,128)(2,1)S(1)}, u32[]{:S(2)}, u32[]{:S(2)}) collective-permute-start(bf16[64,384]{1,0:T(8,128)(2,1)S(1)} %get-tuple-element.45), channel_id=1, source_target_pairs={{1,0},{2,1},{3,2},{4,3},{5,4},{6,5},{7,6},{8,7},{9,8},{10,9},{11,1... | collective-permute-start | bytes 147464 | tf_op jit(solution)/shard_map/ppermute | solution.py:385
  50.4 5.6 %collective-permute-start.4 = (bf16[4,1056,128]{2,1,0:T(8,128)(2,1)S(1)}, bf16[4,1056,128]{2,1,0:T(8,128)(2,1)S(1)}, u32[]{:S(2)}, u32[]{:S(2)}) collective-permute-start(bf16[4,1056,128]{2,1,0:T(8,128)(2,1)S(1)} %get-tuple-element.56), channel_id=1, source_target_pairs={{0,16},{16,0},{1,17},{17,1},{2,18},{18,2},{3,19},{19,3},{4,20},{20... | collective-permute-start | bytes 3244040 | tf_op jit(solution)/shard_map/ppermute | solution.py:449
  75.1 38.3 %all-to-all-start.2 = ((bf16[64,40,128]{2,1,0:T(8,128)(2,1)}), bf16[64,40,128]{2,1,0:T(8,128)(2,1)S(1)}, u32[]{:S(2)}, u32[]{:S(2)}) async-start(bf16[64,40,128]{2,1,0:T(8,128)(2,1)} %get-tuple-element.61), calls=%async_computation.2 | async-start | bytes 1310720 | tf_op jit(solution)/shard_map/all_to_all | solution.py:456
  91.4 10.0 %collective-permute-start.5 = (bf16[48,384]{1,0:T(8,128)(2,1)S(1)}, bf16[48,384]{1,0:T(8,128)(2,1)S(1)}, u32[]{:S(2)}, u32[]{:S(2)}) collective-permute-start(bf16[48,384]{1,0:T(8,128)(2,1)S(1)} %get-tuple-element.59), channel_id=1, source_target_pairs={{0,1},{1,2},{2,3},{3,4},{4,5},{5,6},{6,7},{7,8},{8,9},{9,10},{10,1... | collective-permute-start | bytes 110600 | tf_op jit(solution)/shard_map/ppermute | solution.py:385
  98.2 12.7 %collective-permute-start.6 = (bf16[48,384]{1,0:T(8,128)(2,1)S(1)}, bf16[48,384]{1,0:T(8,128)(2,1)S(1)}, u32[]{:S(2)}, u32[]{:S(2)}) collective-permute-start(bf16[48,384]{1,0:T(8,128)(2,1)S(1)} %get-tuple-element.60), channel_id=1, source_target_pairs={{1,0},{2,1},{3,2},{4,3},{5,4},{6,5},{7,6},{8,7},{9,8},{10,9},{11,1... | collective-permute-start | bytes 110600 | tf_op jit(solution)/shard_map/ppermute | solution.py:385
  114.1 11.6 %all-to-all-start.3 = ((f32[8,24,128]{2,1,0:T(8,128)}), f32[8,24,128]{2,1,0:T(8,128)S(1)}, u32[]{:S(2)}, u32[]{:S(2)}) async-start(f32[8,24,128]{2,1,0:T(8,128)} %get-tuple-element.63), calls=%async_computation.3 | async-start | bytes 196608 | tf_op jit(solution)/shard_map/all_to_all | solution.py:461
  (5 other events, 29.7 us)

commit v4 on v3

--- a/solution.py
+++ b/solution.py
@@ -34,7 +34,14 @@
 HALO = 3
 ROWS_M = HB + 4 * HALO
 ROWS_D = HB + 2 * HALO
-OWN = slice(HALO * WB, HALO * WB + PIX)
+RIGHT_COT = 2 * HALO * ROWS_M
+RIGHT_HIT = RIGHT_COT + HALO * ROWS_D
+RIGHT = 176
+LEFT_OUT = 2 * HALO * ROWS_D
+LEFT = 112
+HALF = WB // 2
+PIX_H = HB * HALF
+OWN = slice(HALO * HALF, HALO * HALF + PIX_H)
 
 UP_TILES = (
     [(0, t) for t in range(8)],
@@ -88,15 +95,10 @@
         out[i] = mean
 
 
-def prepare_kernel(tiles, after, feat, cot, layer_scale, d_branch, occ, first, last):
+def prepare_kernel(tiles, after, feat, cot, masked, first, last):
     pixel = lax.broadcasted_iota(jnp.int32, (PIX, 1), 0)
-    tile = (pixel // (TS * WB)) * (WB // TS) + (pixel % WB) // TS
-    weight = jnp.zeros((PIX, 1), F32)
-    for i in range(TILES):
-        weight = jnp.where(tile == tiles[i], 1.0, weight)
-    occ[...] = weight
-    value = (cot[...].astype(F32) * layer_scale[...] * weight).astype(BF16)
-    d_branch[...] = value
+    value = (cot[...].astype(F32) * occupied(tiles, pixel // WB, pixel % WB)).astype(BF16)
+    masked[...] = value
     n = 2 * HALO * WB
     m = HALO * WB
     first[:n, :] = feat[:n, :]
@@ -105,6 +107,14 @@
     last[n:, :] = value[PIX - m :]
 
 
+def occupied(tiles, row, col):
+    tile = (row // TS) * (WB // TS) + col // TS
+    weight = jnp.zeros(tile.shape, F32)
+    for i in range(TILES):
+        weight = jnp.where(tile == tiles[i], 1.0, weight)
+    return weight
+
+
 def split_columns(rows):
     shaped = rows.reshape(rows.shape[0] // WB, 2, WB // 2, rows.shape[1])
     return [shaped[:, h].reshape(-1, rows.shape[1]) for h in range(2)]
@@ -122,8 +132,8 @@
 
 
 def attention_kernel(
-    scale, valid, pooled, query, feat, above, below, w_key, w_value, w_out,
-    mixed, first, last, grid, edges,
+    scale, valid, tiles, pooled, query, feat, masked, above, below, w_key, w_value, w_out,
+    mixed, send, grid, cot_grid, edges,
 ):
     rows = pooled[...]
     all_keys = split_columns(head_scaled(mm(rows, w_key[...])))
@@ -156,66 +166,101 @@
         out = jnp.where(inside, all_feat[h] + mm(attended, w_out[...]), 0.0)
         grid[:, half * h : half * h + half, :] = out.reshape(ROWS_M, half, C)
     mixed[...] = grid[...].reshape(ROWS_M * WB, C).astype(BF16)
-    column_edges(grid, edges, ROWS_M, first, last)
-
-
-def column_edges(grid, edges, n_rows, first, last):
+    cot_grid[...] = cot_rows(masked, above, below).astype(F32).reshape(ROWS_D, WB, C)
     edges[...] = jnp.zeros_like(edges)
-    for r in range(n_rows):
-        edges[0, HALO * r : HALO * r + HALO, :] = grid[r, :HALO, :]
-        edges[1, HALO * r : HALO * r + HALO, :] = grid[r, WB - HALO :, :]
-    first[...] = edges[0].astype(BF16)
-    last[...] = edges[1].astype(BF16)
-
-
-def fill_window(win, own, left, right, n_rows):
-    for r in range(n_rows):
-        win[r, 8 : 8 + WB, :] = own[r * WB : (r + 1) * WB, :].astype(F32)
-    lcols = left[...].astype(F32)
-    rcols = right[...].astype(F32)
-    for r in range(n_rows):
-        win[r, 8 - HALO : 8, :] = lcols[HALO * r : HALO * r + HALO]
-        win[r, 8 + WB : 8 + WB + HALO, :] = rcols[HALO * r : HALO * r + HALO]
-
-
-def depthwise(win, taps, n_out, start, flip, store):
-    half = WB // 2
+    for r in range(ROWS_M):
+        edges[6 * r : 6 * r + 6, :] = grid[r, WB - 6 :, :]
+    for r in range(ROWS_D):
+        at = RIGHT_COT + HALO * r
+        edges[at : at + HALO, :] = cot_grid[r, WB - HALO :, :]
+    tile_row = lax.broadcasted_iota(jnp.int32, (1, C), 1) // 128 * TS
+    edges[RIGHT_HIT : RIGHT_HIT + 1, :] = occupied(tiles, tile_row, jnp.full((1, C), WB - 1))
+    send[...] = edges[...].astype(BF16)
+
+
+def cot_rows(masked, above, below):
+    n = 2 * HALO * WB
+    return jnp.concatenate([above[n:, :], masked[...], below[n:, :]], axis=0)
+
+
+def border_mask(is_first, dj, start, size):
+    u = lax.broadcasted_iota(jnp.int32, (size, 128), 0) + start
+    crosses = (u < HALO) != (u + dj < 2 * HALO)
+    return jnp.where(crosses & is_first, 0.0, 1.0)
+
+
+def depthwise(win, taps, n_out, base, halves, start, flip, store, is_first=None):
+    masks = [None] * 7
+    if is_first is not None:
+        masks = [border_mask(is_first, dj, 0, HALF) for dj in range(7)]
     for t in range(TILES_L):
         lanes = slice(128 * t, 128 * t + 128)
-        for h in range(2):
-            acc = [start(r, half * h, lanes) for r in range(n_out)]
+        for h in halves:
+            acc = [start(r, h, lanes) for r in range(n_out)]
             for dj in range(7):
-                at = 8 - HALO + half * h + dj
-                cols = [win[r, at : at + half, lanes] for r in range(n_out + 6)]
+                at = base + HALF * h + dj
+                cols = [win[r, at : at + HALF, lanes] for r in range(n_out + 6)]
+                if h == 0 and dj != 3 and is_first is not None:
+                    cols = [col * masks[dj] for col in cols]
                 for di in range(7):
                     tap = 7 * di + dj if not flip else 7 * (6 - di) + (6 - dj)
                     k = taps[tap : tap + 1, lanes]
                     for r in range(n_out):
                         acc[r] = acc[r] + cols[r + di] * k
             for r in range(n_out):
-                store(r, half * h, lanes, acc[r])
+                store(r, h, lanes, acc[r])
 
 
 def rowsum(a):
     return jnp.sum(a, axis=0, keepdims=True)
 
 
-def sublayer_kernel(
-    mixed, left, right, d_branch_own, above, below, cot, occ, taps, dw_bias, ln_gain, ln_bias,
-    w_up, b_up, w_down, b_down, layer_scale,
-    output, d_out, d_first, d_last, win_out, lnout_out, hidden_out, d_pre_out, sums,
-    win, spat, grid, edges,
+def right_half_kernel(tiles, mixed, masked, above, below, *refs):
+    sublayer(1, None, tiles, mixed, None, masked, above, below, *refs)
+
+
+def left_half_kernel(at_first, tiles, mixed, got, masked, above, below, *refs):
+    sublayer(0, at_first, tiles, mixed, got, masked, above, below, *refs)
+
+
+def sublayer(
+    h, at_first, tiles, mixed, got, masked, above, below, taps, dw_bias, ln_gain, ln_bias,
+    w_up, b_up, w_down, b_down, layer_scale, output, d_out, lnout_out, hidden_out, d_pre_out,
+    d_branch_out, sums, *refs,
 ):
-    fill_window(win, mixed, left, right, ROWS_M)
-    win_out[...] = win[HALO : HALO + ROWS_D].astype(BF16)
-
-    def start(r, j, lanes):
-        return jnp.broadcast_to(dw_bias[:, lanes], (WB // 2, 128))
-
-    def store(r, j, lanes, value):
-        spat[r * WB + j : r * WB + j + WB // 2, lanes] = value
-
-    depthwise(win, taps, ROWS_D, start, False, store)
+    if h == 0:
+        win_out, send, win, grid, spat, edges = refs
+        is_first = at_first[0] > 0
+        halo = got[...].astype(F32)
+    else:
+        win, grid, spat = refs
+        is_first = None
+    for r in range(ROWS_M):
+        win[r, 8 : 8 + WB, :] = mixed[r * WB : (r + 1) * WB, :].astype(F32)
+        if h == 0:
+            win[r, 2:8, :] = halo[6 * r : 6 * r + 6]
+    grid[:, 8 : 8 + WB, :] = cot_rows(masked, above, below).astype(F32).reshape(ROWS_D, WB, C)
+    pixel = lax.broadcasted_iota(jnp.int32, (PIX_H, 1), 0)
+    row, col = pixel // HALF, pixel % HALF + HALF * h - HALO
+    weight = occupied(tiles, row, jnp.maximum(col, 0))
+    if h == 0:
+        win_out[...] = win[HALO : HALO + ROWS_D].astype(BF16)
+        for r in range(ROWS_D):
+            at = RIGHT_COT + HALO * r
+            grid[r, 8 - HALO : 8, :] = halo[at : at + HALO]
+        hits = halo[RIGHT_HIT : RIGHT_HIT + 1]
+        before = jnp.where(row < TS, hits[:, 0:1], hits[:, 128:129])
+        weight = jnp.where(col < 0, before, weight)
+    here = slice(8 - HALO + HALF * h, 8 - HALO + HALF * h + HALF)
+    cotan = grid[:, here, :].reshape(ROWS_D * HALF, C)
+
+    def start(r, h, lanes):
+        return jnp.broadcast_to(dw_bias[:, lanes], (HALF, 128))
+
+    def store(r, h, lanes, value):
+        spat[r * HALF : (r + 1) * HALF, lanes] = value
+
+    depthwise(win, taps, ROWS_D, 2, (h,), start, False, store, is_first)
     spatial = spat[...]
     center = spatial - jnp.mean(spatial, axis=1, keepdims=True)
     inv_std = lax.rsqrt(jnp.mean(center * center, axis=1, keepdims=True) + EPS_NORM)
@@ -231,8 +276,10 @@
         1.0 + 3.0 * square
     )
     hidden_out[...] = hidden
-    n = 2 * HALO * WB
-    d_branch_b = jnp.concatenate([above[n:, :], d_branch_own[...], below[n:, :]], axis=0)
+    scale = layer_scale[...]
+    d_branch = cotan * scale
+    d_branch_b = d_branch.astype(BF16)
+    d_branch_out[...] = d_branch_b[OWN]
     d_pre = mm(d_branch_b, w_down[...], ((1,), (1,))) * slope
     d_pre_b = d_pre.astype(BF16)
     d_pre_out[...] = d_pre_b[OWN]
@@ -244,19 +291,24 @@
         - standard * jnp.mean(e * standard, axis=1, keepdims=True)
     )
     d_out[...] = d_spatial
-    grid[...] = d_spatial.reshape(ROWS_D, WB, C)
-    column_edges(grid, edges, ROWS_D, d_first, d_last)
-    weight = occ[...]
-    scale = layer_scale[...]
-    cotan = cot[...].astype(F32)
     branch = (mm(hidden, w_down[...]) + b_down[...]) * weight
-    output[...] = (mixed[2 * HALO * WB : 2 * HALO * WB + PIX, :].astype(F32) + scale * branch).astype(BF16)
+    base = win[2 * HALO : 2 * HALO + HB, here, :].reshape(PIX_H, C)
+    out = base + scale * branch
+    output[...] = out.astype(BF16)
+    if h == 0:
+        edges[...] = jnp.zeros_like(edges)
+        for r in range(ROWS_D):
+            edges[6 * r : 6 * r + 6, :] = d_spatial[r * HALF : r * HALF + 6]
+        for r in range(HB):
+            at = LEFT_OUT + HALO * r
+            edges[at : at + HALO, :] = out[r * HALF : r * HALF + HALO]
+        send[...] = edges[...].astype(BF16)
     d_lnout = d_lnout[OWN]
     sums[0:1, :C] = rowsum(d_spatial[OWN])
     sums[1:2, :C] = rowsum(d_lnout * standard[OWN])
     sums[2:3, :C] = rowsum(d_lnout)
-    sums[3:4, :C] = rowsum(cotan * scale * weight)
-    sums[4:5, :C] = rowsum(cotan * branch)
+    sums[3:4, :C] = rowsum(d_branch[OWN])
+    sums[4:5, :C] = rowsum(cotan[OWN] * branch)
     sums[5:6, :] = rowsum(d_pre[OWN])
 
 
@@ -266,23 +318,29 @@
 
 
 def gradient_kernel(
-    core, order, lnout, hidden, d_pre, d_branch, win_in, d_spatial, sums, mine, other, win, down, small
+    flags, order, win_in, *refs
 ):
-    is_zero = core[0] == 0
+    halves = [refs[:6], refs[6:12]]
+    mine, other, win, down, small = refs[12:]
+    lnout, hidden, d_pre, d_branch = [
+        jnp.concatenate([halves[0][i][...], halves[1][i][...]], axis=0) for i in range(4)
+    ]
+    is_zero = flags[0] == 0
+    is_first = flags[1] > 0
 
     def put(row, x, zero, one):
         size = zero.shape[0]
         mine[x, row : row + size, :] = jnp.where(is_zero, zero, one).astype(BF16)
         other[x, row : row + size, :] = jnp.where(is_zero, one, zero).astype(BF16)
 
-    ordered = mm(lnout[...], order[...]).astype(BF16)
-    ups = [mm(ordered[:, 128 * r : 128 * r + 128], d_pre[...], ((0,), (0,))) for r in range(3)]
+    ordered = mm(lnout, order[...]).astype(BF16)
+    ups = [mm(ordered[:, 128 * r : 128 * r + 128], d_pre, ((0,), (0,))) for r in range(3)]
     for q in range(4):
         for k, (r, t) in enumerate(UP_TILES[q]):
             for x in range(N_X):
                 pair = [ups[r][64 * c + 16 * x : 64 * c + 16 * x + 16, 128 * t : 128 * t + 128] for c in range(2)]
                 put((q * 8 + k) * 16, x, *pair)
-    full = mm(hidden[...], d_branch[...], ((0,), (0,)))
+    full = mm(hidden, d_branch, ((0,), (0,)))
     for t in range(TILES_L):
         down[t] = full[:, 128 * t : 128 * t + 128]
     for yh in range(2):
@@ -302,17 +360,28 @@
                     put(512 + (yh * 8 + k) * 32 + 16 * two, x, *pair)
     win[...] = win_in[...].astype(F32)
     small[...] = jnp.zeros_like(small)
+    masks = [border_mask(is_first, dj, 0, HALF) for dj in range(7)]
     for t in range(TILES_L):
         lanes = slice(128 * t, 128 * t + 128)
-        d_rows = [d_spatial[(HALO + r) * WB : (HALO + r + 1) * WB, lanes] for r in range(HB)]
+        d_rows = [
+            [d[(HALO + r) * HALF : (HALO + r + 1) * HALF, lanes] for r in range(HB)]
+            for d in (halves[0][4], halves[1][4])
+        ]
         for dj in range(7):
-            cols = [win[r, 5 + dj : 5 + dj + WB, lanes] for r in range(HB + 6)]
+            cols = [
+                [win[r, 2 + dj + HALF * h : 2 + dj + HALF * h + HALF, lanes] for r in range(HB + 6)]
+                for h in range(2)
+            ]
+            if dj != 3:
+                cols[0] = [col * masks[dj] for col in cols[0]]
             for di in range(7):
-                acc = cols[di] * d_rows[0]
-                for r in range(1, HB):
-                    acc = acc + cols[r + di] * d_rows[r]
+                acc = cols[0][di] * d_rows[0][0]
+                for h in range(2):
+                    for r in range(1 - h, HB):
+                        acc = acc + cols[h][r + di] * d_rows[h][r]
                 at = 56 * t + 7 * di + dj
                 small[at : at + 1, :] = rowsum(acc)
+    sums = halves[0][5][...] + halves[1][5][...]
     for i in range(5):
         for t in range(TILES_L):
             small[161 + 3 * i + t : 162 + 3 * i + t, :] = sums[i : i + 1, 128 * t : 128 * t + 128]
@@ -326,9 +395,8 @@
         put(1024, x, *pair)
 
 
-def spread_kernel(part, d_first, d_last, out, d_first_out, d_last_out, total):
-    d_first_out[...] = d_first[...]
-    d_last_out[...] = d_last[...]
+def spread_kernel(part, send, out, send_out, total):
+    send_out[...] = send[...]
     total[...] = (
         (part[0].astype(F32) + part[1].astype(F32)) + (part[2].astype(F32) + part[3].astype(F32))
     )
@@ -362,16 +430,33 @@
         vectors[5][pl.ds(128 * t, 128)] = small[176 + t, :]
 
 
-def grad_mixed_kernel(d_all, left, right, cot, taps, out, win):
-    fill_window(win, d_all, left, right, ROWS_D)
-
-    def start(r, j, lanes):
-        return cot[r * WB : (r + 1) * WB, lanes].astype(F32)[j : j + WB // 2]
-
-    def store(r, j, lanes, value):
-        out[r * WB + j : r * WB + j + WB // 2, lanes] = value
-
-    depthwise(win, taps, HB, start, True, store)
+def finish_kernel(
+    at_ends, after, d_left, d_right, out_left, out_right, got, cot, taps, grad, output, win
+):
+    halo = got[...].astype(F32)
+    column = lax.broadcasted_iota(jnp.int32, (HALF, 1), 0)
+    here = jnp.where((column < HALO) & (at_ends[0] > 0), 0.0, 1.0)
+    beyond = lax.broadcasted_iota(jnp.int32, (6, 1), 0)
+    there = jnp.where((beyond >= HALO) & (at_ends[1] > 0), 0.0, 1.0)
+    for r in range(HB):
+        at = LEFT_OUT + HALO * r
+        win[r, 8 : 8 + HALF, :] = out_left[r * HALF : (r + 1) * HALF, :].astype(F32)
+        win[r, 8 + HALF : 8 + WB, :] = out_right[r * HALF : (r + 1) * HALF, :].astype(F32)
+        win[r, 8 + WB : 8 + WB + HALO, :] = halo[at : at + HALO]
+    output[...] = win[:HB, 8 + HALO : 8 + HALO + WB, :].reshape(PIX, C).astype(BF16)
+    for r in range(ROWS_D):
+        win[r, 8 : 8 + HALF, :] = d_left[r * HALF : (r + 1) * HALF, :] * here
+        win[r, 8 + HALF : 8 + WB, :] = d_right[r * HALF : (r + 1) * HALF, :]
+        win[r, 8 + WB : 14 + WB, :] = halo[6 * r : 6 * r + 6] * there
+
+    def start(r, h, lanes):
+        return cot[r * WB : (r + 1) * WB, lanes].astype(F32)[HALF * h : HALF * h + HALF]
+
+    def store(r, h, lanes, value):
+        at = r * WB + HALF * h
+        grad[at : at + HALF, lanes] = value
+
+    depthwise(win, taps, HB, 8, (0, 1), start, True, store)
 
 
 def core_sum_kernel(mine, got, out):
@@ -397,9 +482,10 @@
     pooled = lax.all_to_all(copies, ROW, 0, 0, tiled=True).reshape(N_ROW * WB, C)
 
     shared = ((3 * HALO * WB, C), BF16)
-    d_branch, occ, feat_first, feat_last = call(
-        prepare_kernel, [((PIX, C), BF16), ((PIX, 1), F32), shared, shared],
-        tile_list.reshape(-1), copies, flat, cot, row(layer_scale), smem=(0,), fence=(1,), nbytes=800_000,
+    tiles = tile_list.reshape(-1)
+    masked, feat_first, feat_last = call(
+        prepare_kernel, [((PIX, C), BF16), shared, shared],
+        tiles, copies, flat, cot, smem=(0,), fence=(1,), nbytes=800_000,
     )
     above, below = neighbours(feat_first, feat_last, ROW)
     (query,) = call(
@@ -408,37 +494,49 @@
     )
     at_row = lax.axis_index(ROW)
     valid = jnp.stack([at_row > 0, at_row < N_ROW - 1]).astype(jnp.int32)
-    edge = ((64, C), BF16)
-    mixed, first, last = call(
-        attention_kernel, [((ROWS_M * WB, C), BF16), edge, edge],
-        logit_scale, valid, pooled, query, flat, above, below, w_key, w_value, w_out,
-        scratch=[pltpu.VMEM((ROWS_M, WB, C), F32), pltpu.VMEM((2, 64, C), F32)],
-        smem=(0, 1), flops=10**9, nbytes=2_000_000, trans=500_000,
-    )
-    left, right = neighbours(first, last, COL)
-
-    d_edge = ((48, C), BF16)
-    output, d_all, d_first, d_last, win, lnout, hidden, d_pre, sums = call(
-        sublayer_kernel,
-        [
-            ((PIX, C), BF16), ((ROWS_D * WB, C), F32), d_edge, d_edge, ((ROWS_D, WCOL, C), BF16),
-            ((PIX, C), BF16), ((PIX, HID), BF16), ((PIX, HID), BF16), ((8, HID), F32),
+    mixed, send = call(
+        attention_kernel, [((ROWS_M * WB, C), BF16), ((RIGHT, C), BF16)],
+        logit_scale, valid, tiles, pooled, query, flat, masked, above, below, w_key, w_value, w_out,
+        scratch=[
+            pltpu.VMEM((ROWS_M, WB, C), F32), pltpu.VMEM((ROWS_D, WB, C), F32),
+            pltpu.VMEM((RIGHT, C), F32),
         ],
-        mixed, left, right, d_branch, above, below, cot, occ, dw_kernel, row(dw_bias),
-        row(ln_gain), row(ln_bias), w_up, row(b_up), w_down, row(b_down), row(layer_scale),
-        scratch=[
-            pltpu.VMEM((ROWS_M, WCOL, C), F32), pltpu.VMEM((ROWS_D * WB, C), F32),
-            pltpu.VMEM((ROWS_D, WB, C), F32), pltpu.VMEM((2, 48, C), F32),
-        ],
-        flops=10**9, nbytes=4_000_000, trans=300_000, vmem=24,
-    )
-
-    core = lax.axis_index("c").reshape(1)
+        smem=(0, 1, 2), flops=10**9, nbytes=2_000_000, trans=500_000,
+    )
+    n_col = lax.axis_size(COL)
+    at_col = lax.axis_index(COL)
+    got = lax.ppermute(send, COL, [(i, (i + 1) % n_col) for i in range(n_col)])
+    ends = jnp.stack([at_col == 0, at_col == n_col - 1]).astype(jnp.int32)
+
+    half_outs = [
+        ((PIX_H, C), BF16), ((ROWS_D * HALF, C), F32), ((PIX_H, C), BF16), ((PIX_H, HID), BF16),
+        ((PIX_H, HID), BF16), ((PIX_H, C), BF16), ((8, HID), F32),
+    ]
+    half_scratch = [
+        pltpu.VMEM((ROWS_M, WCOL, C), F32), pltpu.VMEM((ROWS_D, WCOL, C), F32),
+        pltpu.VMEM((ROWS_D * HALF, C), F32),
+    ]
+    params = (
+        dw_kernel, row(dw_bias), row(ln_gain), row(ln_bias), w_up, row(b_up), w_down, row(b_down),
+        row(layer_scale),
+    )
+    cost = dict(flops=10**9, nbytes=4_000_000, trans=150_000)
+    out_right, d_right, *stats_right, sums_right = call(
+        right_half_kernel, half_outs, tiles, mixed, masked, above, below, *params,
+        scratch=half_scratch, smem=(0,), **cost,
+    )
+    out_left, d_left, *stats_left, sums_left, win, send = call(
+        left_half_kernel, half_outs + [((ROWS_D, WCOL, C), BF16), ((LEFT, C), BF16)],
+        ends, tiles, mixed, got, masked, above, below, *params,
+        scratch=half_scratch + [pltpu.VMEM((LEFT, C), F32)], smem=(0, 1), **cost,
+    )
+
+    flags = jnp.stack([lax.axis_index("c"), ends[0]])
     order = jnp.asarray(up_order(), BF16)
     record = ((N_X, REC, 128), BF16)
     mine, other = call(
         gradient_kernel, [record, record],
-        core, order, lnout, hidden, d_pre, d_branch, win, d_all, sums,
+        flags, order, win, *stats_left, d_left, sums_left, *stats_right, d_right, sums_right,
         scratch=[
             pltpu.VMEM((ROWS_D, WCOL, C), F32),
             pltpu.VMEM((TILES_L, HID, 128), F32),
@@ -449,12 +547,12 @@
     got = lax.ppermute(other, "c", [(0, 1), (1, 0)])
     (part,) = call(core_sum_kernel, [record], mine, got, nbytes=3_000_000)
     part = lax.all_to_all(part, "x", 0, 0, tiled=True)
-    part, d_first, d_last = call(
-        spread_kernel, [((N_YZ, 16 + SMALL, 128), BF16), d_edge, d_edge], part, d_first, d_last,
+    part, send = call(
+        spread_kernel, [((N_YZ, 16 + SMALL, 128), BF16), ((LEFT, C), BF16)], part, send,
         scratch=[pltpu.VMEM((REC, 128), F32)], nbytes=2_000_000,
     )
     part = lax.all_to_all(part, YZ, 0, 0, tiled=True)
-    d_left, d_right = neighbours(d_first, d_last, COL)
+    got = lax.ppermute(send, COL, [(i, (i - 1) % n_col) for i in range(n_col)])
     share, small = call(
         gather_kernel, [((16, 128), F32), ((N_X * N_C, SMALL, 128), F32)], part, nbytes=800_000
     )
@@ -463,15 +561,16 @@
         final_kernel, [((49, C), F32)] + [((C,), F32)] * 5 + [((HID,), F32)],
         small.reshape(-1, 128), nbytes=200_000,
     )
-    share = share.reshape(2, 8 * 128)
-    share = jnp.where(lax.axis_index("yh") == 0, share[:, :SHARE], share[:, 8 * 128 - SHARE :])
-    (grad_mixed,) = call(
-        grad_mixed_kernel, [((PIX, C), F32)], d_all, d_left, d_right, cot, dw_kernel,
-        scratch=[pltpu.VMEM((ROWS_D, WCOL, C), F32)], flops=10**7, nbytes=1_000_000,
+    shares = share.reshape(2, 8 * 128)
+    shares = jnp.where(lax.axis_index("yh") == 0, shares[:, :SHARE], shares[:, 8 * 128 - SHARE :])
+    grad_mixed, output = call(
+        finish_kernel, [((PIX, C), F32), ((PIX, C), BF16)],
+        ends, share, d_left, d_right, out_left, out_right, got, cot, dw_kernel,
+        scratch=[pltpu.VMEM((ROWS_D, WCOL, C), F32)], smem=(0,), fence=(1,), flops=10**7, nbytes=1_000_000,
     )
     bias, gain, shift, b_down_grad, scale_grad, b_up_grad = vectors[1:]
     return (
-        output.reshape(HB, WB, C), grad_mixed.reshape(HB, WB, C), share[0], share[1],
+        output.reshape(HB, WB, C), grad_mixed.reshape(HB, WB, C), shares[0], shares[1],
         vectors[0], bias, gain, shift, b_up_grad, b_down_grad, scale_grad,
     )
 

time: 127 us -> 121 us (0.953)
  starting transfers between devices: 54.8 us -> 49.8 us
  waiting for transfers between devices: 32.3 us -> 28.5 us
  Pallas kernels: 19 us -> 21.8 us
    ppermute x3 -> x1, waiting for transfers between devices: 21.5 us -> 4.57 us  [neighbours(): lax.ppermute(before_edge, axes, down)]
    ppermute x0 -> x2, starting transfers between devices: none -> 12.4 us  [the longest x1 8.94 us: body(): got = lax.ppermute(send, COL, [(i, (i - 1) % n_col) for i in range(n_col)])]
    ppermute x3 -> x1, starting transfers between devices: 13.6 us -> 3.55 us  [neighbours(): lax.ppermute(after_edge, axes, up)]
    all_to_all x1, waiting for transfers between devices: 0.01 us -> 9.85 us  [body(): part = lax.all_to_all(part, YZ, 0, 0, tiled=True)]
    ppermute x0 -> x2, waiting for transfers between devices: none -> 8.2 us  [the longest x1 8.2 us: body(): got = lax.ppermute(send, COL, [(i, (i + 1) % n_col) for i in range(n_col)])]
    all_to_all x1, starting transfers between devices: 16.3 us -> 10.1 us  [body(): part = lax.all_to_all(part, YZ, 0, 0, tiled=True)]
    all_to_all x1, waiting for transfers between devices: 4.32 us -> 1.31 us  [body(): small = lax.all_to_all(small, CX, 0, 0, tiled=True)]
    pallas_call x11 -> x12, Pallas kernels: 19 us -> 21.8 us  [call(): pl.pallas_call(kernel, out_shape=[jax.ShapeDtypeStruct(s, d) for s, d in...]
  transfers between devices with their start and end apart: 10 -> 8, of which waited for: 8 -> 6; matrix products, arithmetic and copies ran while one was open for 1% -> 1% of each run, Pallas kernels for 3% -> 7%
where the time goes in v4:
time: 121 us; the launch traced here: 120 us
  starting transfers between devices  49.8 us (41%)
  waiting for transfers between devices  28.5 us (24%)
  Pallas kernels  21.8 us (18%)
  blocking collectives  17.4 us (14%)
  local copies, waits for them, and re-layouts  1.62 us (1%)
    pallas_call x12, Pallas kernels, call(): pl.pallas_call(kernel, out_shape=[jax.ShapeDtypeStruct(s, d) for s, d in...  21.8 us
    all_to_all x1, blocking collectives, body(): part = lax.all_to_all(part, 'x', 0, 0, tiled=True)  17.4 us
    all_to_all x1, starting transfers between devices, body(): lax.all_to_all(copies, ROW, 0, 0, tiled=True).reshape(N_ROW * WB, C)  10.6 us
    all_to_all x1, starting transfers between devices, body(): part = lax.all_to_all(part, YZ, 0, 0, tiled=True)  10.1 us
    all_to_all x1, waiting for transfers between devices, body(): part = lax.all_to_all(part, YZ, 0, 0, tiled=True)  9.85 us
    ppermute x1, starting transfers between devices, body(): got = lax.ppermute(send, COL, [(i, (i - 1) % n_col) for i in range(n_col)])  8.94 us
    all_to_all x1, starting transfers between devices, body(): small = lax.all_to_all(small, CX, 0, 0, tiled=True)  8.78 us
    ppermute x1, waiting for transfers between devices, body(): got = lax.ppermute(send, COL, [(i, (i + 1) % n_col) for i in range(n_col)])  8.2 us
  transfers between devices with their start and end apart: 8, of which 6 were waited for; matrix products, arithmetic and copies ran while one was open for 1% of the time, Pallas kernels for 7%

profile of v4, /device:TPU:1, one launch (start us, length us, event | category | flops | bytes accessed | tf_op | source)
XLA Modules:
  0.0 120.5 jit_solution(16604633637996311998)
XLA Ops:
  0.7 0.9 copy-done
  1.5 0.8 shard_map.257.after
  2.4 10.6 %all-to-all-start = ((bf16[32,16,384]{2,1,0:T(8,128)(2,1)}), bf16[32,16,384]{2,1,0:T(8,128)(2,1)S(1)}, u32[]{:S(2)}, u32[]{:S(2)}) async-start(bf16[32,16,384]{2,1,0:T(8,128)(2,1)} %shard_map.257.after), calls=%async_computation | async-start | bytes 786432 | tf_op jit(solution)/shard_map/all_to_all | solution.py:482
  13.6 3.5 %collective-permute-start = (bf16[144,384]{1,0:T(8,128)(2,1)S(1)}, bf16[144,384]{1,0:T(8,128)(2,1)S(1)}, u32[]{:S(2)}, u32[]{:S(2)}) collective-permute-start(bf16[144,384]{1,0:T(8,128)(2,1)S(1)} %get-tuple-element.47), channel_id=1, source_target_pairs={{0,16},{16,32},{32,48},{48,64},{64,80},{80,96},{96,112},{112,128},... | collective-permute-start | bytes 331784 | tf_op jit(solution)/shard_map/ppermute | solution.py:470
  17.1 1.9 %collective-permute-start.1 = (bf16[144,384]{1,0:T(8,128)(2,1)S(1)}, bf16[144,384]{1,0:T(8,128)(2,1)S(1)}, u32[]{:S(2)}, u32[]{:S(2)}) collective-permute-start(bf16[144,384]{1,0:T(8,128)(2,1)S(1)} %get-tuple-element.48), channel_id=1, source_target_pairs={{16,0},{32,16},{48,32},{64,48},{80,64},{96,80},{112,96},{128,112},... | collective-permute-start | bytes 331784 | tf_op jit(solution)/shard_map/ppermute | solution.py:470
  19.3 4.6 %collective-permute-done.1.below = bf16[144,384]{1,0:T(8,128)(2,1)S(1)} collective-permute-done((bf16[144,384]{1,0:T(8,128)(2,1)S(1)}, bf16[144,384]{1,0:T(8,128)(2,1)S(1)}, u32[]{:S(2)}, u32[]{:S(2)}) %collective-permute-start.1) | collective-permute-done | bytes 110624 | tf_op jit(solution)/shard_map/ppermute | solution.py:470
  24.6 2.3 %all-to-all-done = bf16[32,16,384]{2,1,0:T(8,128)(2,1)S(1)} async-done(((bf16[32,16,384]{2,1,0:T(8,128)(2,1)}), bf16[32,16,384]{2,1,0:T(8,128)(2,1)S(1)}, u32[]{:S(2)}, u32[]{:S(2)}) %all-to-all-start) | async-done | bytes 393248 | tf_op jit(solution)/shard_map/all_to_all | solution.py:482
  26.9 2.8 %shard_map.260 = (bf16[320,384]{1,0:T(8,128)(2,1)S(1)}, bf16[176,384]{1,0:T(8,128)(2,1)S(1)}) custom-call(f32[6]{0:T(128)S(1)} %copy-done.11, s32[2]{0:T(128)S(1)} %add_convert_fusion.1.valid, s32[8]{0:T(128)S(1)} %bitcast.24, bf16[512,384]{1,0:T(8,128)(2,1)S(1)} %bitcast.18, bf16[2,160,384]{2,1,0:T(8,128)(2,1)S(1)} %shard_map.259.query, ...), custom_call_target="tpu_custom_call" | custom-call | flops 1000000000 | bytes 2000000 | tf_op jit(solution)/shard_map/pallas_call | solution.py:65
  29.8 3.4 %collective-permute-start.2 = (bf16[176,384]{1,0:T(8,128)(2,1)S(1)}, bf16[176,384]{1,0:T(8,128)(2,1)S(1)}, u32[]{:S(2)}, u32[]{:S(2)}) collective-permute-start(bf16[176,384]{1,0:T(8,128)(2,1)S(1)} %get-tuple-element.51), channel_id=1, source_target_pairs={{0,1},{1,2},{2,3},{3,4},{4,5},{5,6},{6,7},{7,8},{8,9},{9,10},{10,1... | collective-permute-start | bytes 405512 | tf_op jit(solution)/shard_map/ppermute | solution.py:508
  33.5 3.8 %shard_map.262 = (bf16[64,384]{1,0:T(8,128)(2,1)S(1)}, f32[112,384]{1,0:T(8,128)S(1)}, bf16[64,384]{1,0:T(8,128)(2,1)S(1)}, bf16[64,1280]{1,0:T(8,128)(2,1)S(1)}...) custom-call(s32[8]{0:T(128)S(1)} %bitcast.25, ...), custom_call_target="tpu_custom_call" | custom-call | flops 1000000000 | bytes 4000000 | tf_op jit(solution)/shard_map/pallas_call | solution.py:65
  37.3 8.2 %collective-permute-done.2.got = bf16[176,384]{1,0:T(8,128)(2,1)S(1)} collective-permute-done((bf16[176,384]{1,0:T(8,128)(2,1)S(1)}, bf16[176,384]{1,0:T(8,128)(2,1)S(1)}, u32[]{:S(2)}, u32[]{:S(2)}) %collective-permute-start.2) | collective-permute-done | bytes 135200 | tf_op jit(solution)/shard_map/ppermute | solution.py:508
  45.5 4.0 %shard_map.261 = (bf16[64,384]{1,0:T(8,128)(2,1)S(1)}, f32[112,384]{1,0:T(8,128)S(1)}, bf16[64,384]{1,0:T(8,128)(2,1)S(1)}, bf16[64,1280]{1,0:T(8,128)(2,1)S(1)}...) custom-call(s32[2]{0:T(128)S(1)} %add_convert_fusion.at_first.at_end, ...), custom_call_target="tpu_custom_call" | custom-call | flops 1000000000 | bytes 4000000 | tf_op jit(solution)/shard_map/pallas_call | solution.py:65
  49.5 3.0 %shard_map.263 = (bf16[4,1056,128]{2,1,0:T(8,128)(2,1)S(1)}, bf16[4,1056,128]{2,1,0:T(8,128)(2,1)S(1)}) custom-call(s32[2]{0:T(128)S(1)} %pad_add_fusion.flags, bf16[384,384]{1,0:T(8,128)(2,1)S(1)} %copy-done.12, bf16[14,32,384]{2,1,0:T(8,128)(2,1)S(1)} %get-tuple-element.52.win_in, bf16[64,384]{1,0:T(8,128)(2,1)S(1)} %get-tuple-element.53.refs_0_, ...), custom_call_target="tpu_custom_call" | custom-call | flops 2000000000 | bytes 4000000 | tf_op jit(solution)/shard_map/pallas_call | solution.py:65
  52.5 2.5 %collective-permute-start.3 = (bf16[4,1056,128]{2,1,0:T(8,128)(2,1)S(1)}, bf16[4,1056,128]{2,1,0:T(8,128)(2,1)S(1)}, u32[]{:S(2)}, u32[]{:S(2)}) collective-permute-start(bf16[4,1056,128]{2,1,0:T(8,128)(2,1)S(1)} %get-tuple-element.66), channel_id=1, source_target_pairs={{0,16},{16,0},{1,17},{17,1},{2,18},{18,2},{3,19},{19,3},{4,20},{20... | collective-permute-start | bytes 3244040 | tf_op jit(solution)/shard_map/ppermute | solution.py:547
  55.1 2.3 %collective-permute-done.3.got = bf16[4,1056,128]{2,1,0:T(8,128)(2,1)S(1)} collective-permute-done((bf16[4,1056,128]{2,1,0:T(8,128)(2,1)S(1)}, bf16[4,1056,128]{2,1,0:T(8,128)(2,1)S(1)}, u32[]{:S(2)}, u32[]{:S(2)}) %collective-permute-start.3) | collective-permute-done | bytes 1081376 | tf_op jit(solution)/shard_map/ppermute | solution.py:547
  57.6 17.4 %all_to_all.20.part = bf16[4,1056,128]{2,1,0:T(8,128)(2,1)S(1)} all-to-all(bf16[4,1056,128]{2,1,0:T(8,128)(2,1)S(1)} %shard_map.264), channel_id=1, replica_groups=mesh['yl'=4,'x'=4,'c'=2,'z'=8,'yh'=2] {'x'}, dimensions={0} | all-to-all | bytes 2162688 | tf_op jit(solution)/shard_map/all_to_all | solution.py:549
  75.1 1.3 %shard_map.265 = (bf16[64,40,128]{2,1,0:T(8,128)(2,1)}, bf16[112,384]{1,0:T(8,128)(2,1)S(1)}) custom-call(bf16[4,1056,128]{2,1,0:T(8,128)(2,1)S(1)} %all_to_all.20.part, bf16[112,384]{1,0:T(8,128)(2,1)S(1)} %get-tuple-element.67.send), custom_call_target="tpu_custom_call" | custom-call | bytes 2000000 | tf_op jit(solution)/shard_map/pallas_call | solution.py:65
  76.4 10.1 %all-to-all-start.2 = ((bf16[64,40,128]{2,1,0:T(8,128)(2,1)}), bf16[64,40,128]{2,1,0:T(8,128)(2,1)S(1)}, u32[]{:S(2)}, u32[]{:S(2)}) async-start(bf16[64,40,128]{2,1,0:T(8,128)(2,1)} %get-tuple-element.68), calls=%async_computation.2 | async-start | bytes 1310720 | tf_op jit(solution)/shard_map/all_to_all | solution.py:554
  86.5 8.9 %collective-permute-start.4 = (bf16[112,384]{1,0:T(8,128)(2,1)S(1)}, bf16[112,384]{1,0:T(8,128)(2,1)S(1)}, u32[]{:S(2)}, u32[]{:S(2)}) collective-permute-start(bf16[112,384]{1,0:T(8,128)(2,1)S(1)} %get-tuple-element.72), channel_id=1, source_target_pairs={{0,15},{1,0},{2,1},{3,2},{4,3},{5,4},{6,5},{7,6},{8,7},{9,8},{10,9... | collective-permute-start | bytes 258056 | tf_op jit(solution)/shard_map/ppermute | solution.py:555
  95.4 9.8 %all-to-all-done.2.part = bf16[64,40,128]{2,1,0:T(8,128)(2,1)S(1)} async-done(((bf16[64,40,128]{2,1,0:T(8,128)(2,1)}), bf16[64,40,128]{2,1,0:T(8,128)(2,1)S(1)}, u32[]{:S(2)}, u32[]{:S(2)}) %all-to-all-start.2) | async-done | bytes 655392 | tf_op jit(solution)/shard_map/all_to_all | solution.py:554
  105.3 0.7 shard_map.266
  106.0 8.8 %all-to-all-start.3 = ((f32[8,24,128]{2,1,0:T(8,128)}), f32[8,24,128]{2,1,0:T(8,128)S(1)}, u32[]{:S(2)}, u32[]{:S(2)}) async-start(f32[8,24,128]{2,1,0:T(8,128)} %get-tuple-element.75), calls=%async_computation.3 | async-start | bytes 196608 | tf_op jit(solution)/shard_map/all_to_all | solution.py:559
  115.5 3.0 %shard_map.267 = (f32[128,384]{1,0:T(8,128)}, bf16[128,384]{1,0:T(8,128)(2,1)}) custom-call(s32[2]{0:T(128)S(1)} %add_convert_fusion.at_first.at_ends, f32[16,128]{1,0:T(8,128)S(1)} %get-tuple-element.69.after, f32[112,384]{1,0:T(8,128)S(1)} %get-tuple-element.57.refs_4_.d_left, f32[112,384]{1,0:T(8,128)S(1)} %get-tuple-element.63.refs_10_.d_right, ...), custom_call_target="tpu_custom_call" | custom-call | flops 10000000 | bytes 1000000 | tf_op jit(solution)/shard_map/pallas_call | solution.py:65
  118.5 1.3 %all-to-all-done.3 = f32[8,24,128]{2,1,0:T(8,128)S(1)} async-done(((f32[8,24,128]{2,1,0:T(8,128)}), f32[8,24,128]{2,1,0:T(8,128)S(1)}, u32[]{:S(2)}, u32[]{:S(2)}) %all-to-all-start.3) | async-done | bytes 98336 | tf_op jit(solution)/shard_map/all_to_all | solution.py:559
  (55 shorter events, 3.3 us)
Async XLA Ops:
  1.5 11.4 %copy-start.1 = (bf16[8,16,384]{2,1,0:T(8,128)(2,1)S(1)}, bf16[8,16,384]{2,1,0:T(8,128)(2,1)}, u32[]{:S(2)}) copy-start(bf16[8,16,384]{2,1,0:T(8,128)(2,1)} %feat.1) | copy-start | bytes 294916
  1.5 11.4 %copy-start.2 = (bf16[8,16,384]{2,1,0:T(8,128)(2,1)S(1)}, bf16[8,16,384]{2,1,0:T(8,128)(2,1)}, u32[]{:S(2)}) copy-start(bf16[8,16,384]{2,1,0:T(8,128)(2,1)} %param.33) | copy-start | bytes 294916
  1.5 11.4 %copy-start.5 = (s32[1,1,8]{2,1,0:T(1,128)S(1)}, s32[1,1,8]{2,1,0:T(1,128)}, u32[]{:S(2)}) copy-start(s32[1,1,8]{2,1,0:T(1,128)} %param.34) | copy-start | bytes 100
  1.5 22.3 %copy-start.3 = (bf16[384,384]{1,0:T(8,128)(2,1)S(1)}, bf16[384,384]{1,0:T(8,128)(2,1)}, u32[]{:S(2)}) copy-start(bf16[384,384]{1,0:T(8,128)(2,1)} %w_query.1) | copy-start | bytes 884740
  2.4 24.5 %copy-start.8 = (bf16[384,384]{1,0:T(8,128)(2,1)S(1)}, bf16[384,384]{1,0:T(8,128)(2,1)}, u32[]{:S(2)}) copy-start(bf16[384,384]{1,0:T(8,128)(2,1)} %w_key.1) | copy-start | bytes 884740
  2.4 24.5 %copy-start.9 = (bf16[384,384]{1,0:T(8,128)(2,1)S(1)}, bf16[384,384]{1,0:T(8,128)(2,1)}, u32[]{:S(2)}) copy-start(bf16[384,384]{1,0:T(8,128)(2,1)} %w_value.1) | copy-start | bytes 884740
  2.4 24.5 %copy-start.10 = (bf16[384,384]{1,0:T(8,128)(2,1)S(1)}, bf16[384,384]{1,0:T(8,128)(2,1)}, u32[]{:S(2)}) copy-start(bf16[384,384]{1,0:T(8,128)(2,1)} %w_out.1) | copy-start | bytes 884740
  2.4 24.5 %copy-start.11 = (f32[6]{0:T(128)S(1)}, f32[6]{0:T(128)}, u32[]{:S(2)}) copy-start(f32[6]{0:T(128)} %scale.1) | copy-start | bytes 76
  2.4 24.5 %all-to-all-start = ((bf16[32,16,384]{2,1,0:T(8,128)(2,1)}), bf16[32,16,384]{2,1,0:T(8,128)(2,1)S(1)}, u32[]{:S(2)}, u32[]{:S(2)}) async-start(bf16[32,16,384]{2,1,0:T(8,128)(2,1)} %shard_map.257.after), calls=%async_computation | async-start | bytes 786432 | tf_op jit(solution)/shard_map/all_to_all | solution.py:482
  13.6 5.7 %collective-permute-start = (bf16[144,384]{1,0:T(8,128)(2,1)S(1)}, bf16[144,384]{1,0:T(8,128)(2,1)S(1)}, u32[]{:S(2)}, u32[]{:S(2)}) collective-permute-start(bf16[144,384]{1,0:T(8,128)(2,1)S(1)} %get-tuple-element.47), channel_id=1, source_target_pairs={{0,16},{16,32},{32,48},{48,64},{64,80},{80,96},{96,112},{112,128},... | collective-permute-start | bytes 331784 | tf_op jit(solution)/shard_map/ppermute | solution.py:470
  17.1 6.7 %collective-permute-start.1 = (bf16[144,384]{1,0:T(8,128)(2,1)S(1)}, bf16[144,384]{1,0:T(8,128)(2,1)S(1)}, u32[]{:S(2)}, u32[]{:S(2)}) collective-permute-start(bf16[144,384]{1,0:T(8,128)(2,1)S(1)} %get-tuple-element.48), channel_id=1, source_target_pairs={{16,0},{32,16},{48,32},{64,48},{80,64},{96,80},{112,96},{128,112},... | collective-permute-start | bytes 331784 | tf_op jit(solution)/shard_map/ppermute | solution.py:470
  26.8 6.5 %copy-start.14 = (f32[384]{0:T(512)S(1)}, f32[384]{0:T(512)}, u32[]{:S(2)}) copy-start(f32[384]{0:T(512)} %param.25) | copy-start | bytes 4612
  26.9 6.5 %copy-start.17 = (f32[384]{0:T(512)S(1)}, f32[384]{0:T(512)}, u32[]{:S(2)}) copy-start(f32[384]{0:T(512)} %param.31) | copy-start | bytes 4612
  26.9 6.5 %copy-start.18 = (f32[384]{0:T(512)S(1)}, f32[384]{0:T(512)}, u32[]{:S(2)}) copy-start(f32[384]{0:T(512)} %param.32) | copy-start | bytes 4612
  26.9 6.5 %copy-start.13 = (f32[1280]{0:T(1024)S(1)}, f32[1280]{0:T(1024)}, u32[]{:S(2)}) copy-start(f32[1280]{0:T(1024)} %param.29) | copy-start | bytes 15364
  26.9 6.5 %copy-start.4 = (f32[49,384]{1,0:T(8,128)S(1)}, f32[49,384]{1,0:T(8,128)}, u32[]{:S(2)}) copy-start(f32[49,384]{1,0:T(8,128)} %taps.1) | copy-start | bytes 225796
  26.9 6.5 %copy-start.6 = (bf16[384,1280]{1,0:T(8,128)(2,1)S(1)}, bf16[384,1280]{1,0:T(8,128)(2,1)}, u32[]{:S(2)}) copy-start(bf16[384,1280]{1,0:T(8,128)(2,1)} %refs_4_.3) | copy-start | bytes 2949124
  26.9 6.5 %copy-start.7 = (bf16[1280,384]{1,0:T(8,128)(2,1)S(1)}, bf16[1280,384]{1,0:T(8,128)(2,1)}, u32[]{:S(2)}) copy-start(bf16[1280,384]{1,0:T(8,128)(2,1)} %refs_6_.3) | copy-start | bytes 2949124
  29.8 15.7 %collective-permute-start.2 = (bf16[176,384]{1,0:T(8,128)(2,1)S(1)}, bf16[176,384]{1,0:T(8,128)(2,1)S(1)}, u32[]{:S(2)}, u32[]{:S(2)}) collective-permute-start(bf16[176,384]{1,0:T(8,128)(2,1)S(1)} %get-tuple-element.51), channel_id=1, source_target_pairs={{0,1},{1,2},{2,3},{3,4},{4,5},{5,6},{6,7},{7,8},{8,9},{9,10},{10,1... | collective-permute-start | bytes 405512 | tf_op jit(solution)/shard_map/ppermute | solution.py:508
  37.3 12.2 %copy-start.12 = (bf16[384,384]{1,0:T(8,128)(2,1)S(1)}, bf16[384,384]{1,0:T(8,128)(2,1)}, u32[]{:S(2)}) copy-start(bf16[384,384]{1,0:T(8,128)(2,1)} %constant.33.clone.order) | copy-start | bytes 884740
  52.5 4.9 %collective-permute-start.3 = (bf16[4,1056,128]{2,1,0:T(8,128)(2,1)S(1)}, bf16[4,1056,128]{2,1,0:T(8,128)(2,1)S(1)}, u32[]{:S(2)}, u32[]{:S(2)}) collective-permute-start(bf16[4,1056,128]{2,1,0:T(8,128)(2,1)S(1)} %get-tuple-element.66), channel_id=1, source_target_pairs={{0,16},{16,0},{1,17},{17,1},{2,18},{18,2},{3,19},{19,3},{4,20},{20... | collective-permute-start | bytes 3244040 | tf_op jit(solution)/shard_map/ppermute | solution.py:547
  76.4 28.9 %all-to-all-start.2 = ((bf16[64,40,128]{2,1,0:T(8,128)(2,1)}), bf16[64,40,128]{2,1,0:T(8,128)(2,1)S(1)}, u32[]{:S(2)}, u32[]{:S(2)}) async-start(bf16[64,40,128]{2,1,0:T(8,128)(2,1)} %get-tuple-element.68), calls=%async_computation.2 | async-start | bytes 1310720 | tf_op jit(solution)/shard_map/all_to_all | solution.py:554
  86.5 29.0 %collective-permute-start.4 = (bf16[112,384]{1,0:T(8,128)(2,1)S(1)}, bf16[112,384]{1,0:T(8,128)(2,1)S(1)}, u32[]{:S(2)}, u32[]{:S(2)}) collective-permute-start(bf16[112,384]{1,0:T(8,128)(2,1)S(1)} %get-tuple-element.72), channel_id=1, source_target_pairs={{0,15},{1,0},{2,1},{3,2},{4,3},{5,4},{6,5},{7,6},{8,7},{9,8},{10,9... | collective-permute-start | bytes 258056 | tf_op jit(solution)/shard_map/ppermute | solution.py:555
  106.0 13.8 %all-to-all-start.3 = ((f32[8,24,128]{2,1,0:T(8,128)}), f32[8,24,128]{2,1,0:T(8,128)S(1)}, u32[]{:S(2)}, u32[]{:S(2)}) async-start(f32[8,24,128]{2,1,0:T(8,128)} %get-tuple-element.75), calls=%async_computation.3 | async-start | bytes 196608 | tf_op jit(solution)/shard_map/all_to_all | solution.py:559
  (3 other events, 13.9 us)

commit v5 on v4

--- a/solution.py
+++ b/solution.py
@@ -55,19 +55,39 @@
 )
 
 
-def call(kernel, outs, *args, scratch=(), smem=(), fence=(), flops=0, nbytes=0, trans=0, vmem=16):
+def call(
+    kernel, outs, *args, scratch=(), smem=(), fence=(), hbm=(), flops=0, nbytes=0, trans=0, vmem=16
+):
+    n_in, n_out, n_scratch = len(args), len(outs), len(scratch)
+
+    def run(*refs):
+        targets = list(refs[n_in : n_in + n_out])
+        extra = refs[n_in + n_out + n_scratch :]
+        copies = []
+        for j, i in enumerate(hbm):
+            copies.append(pltpu.make_async_copy(extra[2 * j], targets[i], extra[2 * j + 1]))
+            targets[i] = extra[2 * j]
+        kernel(*refs[:n_in], *targets, *refs[n_in + n_out : n_in + n_out + n_scratch])
+        for copy in copies:
+            copy.start()
+        for copy in copies:
+            copy.wait()
+
     specs = [
         pl.BlockSpec(
             memory_space=pltpu.SMEM if i in smem else pl.ANY if i in fence else pltpu.VMEM
         )
-        for i in range(len(args))
+        for i in range(n_in)
     ]
+    buffers = [b for i in hbm for b in (pltpu.VMEM(*outs[i]), pltpu.SemaphoreType.DMA(()))]
     return pl.pallas_call(
-        kernel,
+        run,
         out_shape=[jax.ShapeDtypeStruct(s, d) for s, d in outs],
         in_specs=specs,
-        out_specs=[pl.BlockSpec(memory_space=pltpu.VMEM) for _ in outs],
-        scratch_shapes=list(scratch),
+        out_specs=[
+            pl.BlockSpec(memory_space=pltpu.HBM if i in hbm else pltpu.VMEM) for i in range(n_out)
+        ],
+        scratch_shapes=list(scratch) + buffers,
         compiler_params=pltpu.CompilerParams(vmem_limit_bytes=vmem * 1024 * 1024),
         cost_estimate=pl.CostEstimate(flops=flops, bytes_accessed=nbytes, transcendentals=trans),
     )(*args)
@@ -131,51 +151,58 @@
         out[h] = half.astype(BF16)
 
 
-def attention_kernel(
-    scale, valid, tiles, pooled, query, feat, masked, above, below, w_key, w_value, w_out,
-    mixed, send, grid, cot_grid, edges,
+def right_attention_kernel(
+    scale, valid, pooled, query, feat, above, below, w_key, w_value, w_out, tiles, masked,
+    mixed, send, cot_grid, edges,
 ):
-    rows = pooled[...]
-    all_keys = split_columns(head_scaled(mm(rows, w_key[...])))
-    all_values = split_columns(mm(rows, w_value[...]))
-    all_feat = split_columns(stacked_rows(feat, above, below).astype(F32))
-    half = WB // 2
-    n_query, n_keys = ROWS_M * half, N_ROW * half
-    same = (
-        lax.broadcasted_iota(jnp.int32, (n_query, n_keys), 0) % half
-        == lax.broadcasted_iota(jnp.int32, (n_query, n_keys), 1) % half
-    )
-    lower = lax.broadcasted_iota(jnp.int32, (n_query, 128), 1) < 64
-    row = lax.broadcasted_iota(jnp.int32, (n_query, 1), 0) // half
-    inside = ((row >= 2 * HALO) | (valid[0] > 0)) & ((row < 2 * HALO + HB) | (valid[1] > 0))
-    for h in range(2):
-        keys, values = all_keys[h].astype(BF16), all_values[h].astype(BF16)
-        pairs = []
-        for pair in range(HEADS // 2):
-            lanes = slice(128 * pair, 128 * pair + 128)
-            q = query[h, :, lanes].astype(F32)
-            parts = []
-            for sub in range(2):
-                q_half = jnp.where(lower if sub == 0 else ~lower, q, 0.0).astype(BF16)
-                scores = mm(q_half, keys[:, lanes], ((1,), (1,)))
-                weight = jnp.where(same, jnp.exp(scores * scale[2 * pair + sub]), 0.0)
-                total = jnp.sum(weight, axis=1, keepdims=True)
-                parts.append(mm(weight.astype(BF16), values[:, lanes]) / total)
-            pairs.append(jnp.where(lower, parts[0], parts[1]).astype(BF16))
-        attended = jnp.concatenate(pairs, axis=1)
-        out = jnp.where(inside, all_feat[h] + mm(attended, w_out[...]), 0.0)
-        grid[:, half * h : half * h + half, :] = out.reshape(ROWS_M, half, C)
-    mixed[...] = grid[...].reshape(ROWS_M * WB, C).astype(BF16)
+    out = attention(1, scale, valid, pooled, query, feat, above, below, w_key, w_value, w_out)
+    mixed[...] = out.astype(BF16)
     cot_grid[...] = cot_rows(masked, above, below).astype(F32).reshape(ROWS_D, WB, C)
     edges[...] = jnp.zeros_like(edges)
     for r in range(ROWS_M):
-        edges[6 * r : 6 * r + 6, :] = grid[r, WB - 6 :, :]
+        edges[6 * r : 6 * r + 6, :] = out[HALF * r + HALF - 6 : HALF * r + HALF]
     for r in range(ROWS_D):
         at = RIGHT_COT + HALO * r
         edges[at : at + HALO, :] = cot_grid[r, WB - HALO :, :]
     tile_row = lax.broadcasted_iota(jnp.int32, (1, C), 1) // 128 * TS
     edges[RIGHT_HIT : RIGHT_HIT + 1, :] = occupied(tiles, tile_row, jnp.full((1, C), WB - 1))
     send[...] = edges[...].astype(BF16)
+
+
+def left_attention_kernel(
+    scale, valid, pooled, query, feat, above, below, w_key, w_value, w_out, after, mixed
+):
+    out = attention(0, scale, valid, pooled, query, feat, above, below, w_key, w_value, w_out)
+    mixed[...] = out.astype(BF16)
+
+
+def attention(h, scale, valid, pooled, query, feat, above, below, w_key, w_value, w_out):
+    rows = split_columns(pooled[...].astype(F32))[h].astype(BF16)
+    keys = head_scaled(mm(rows, w_key[...])).astype(BF16)
+    values = mm(rows, w_value[...]).astype(BF16)
+    half_feat = split_columns(stacked_rows(feat, above, below).astype(F32))[h]
+    n_query, n_keys = ROWS_M * HALF, N_ROW * HALF
+    same = (
+        lax.broadcasted_iota(jnp.int32, (n_query, n_keys), 0) % HALF
+        == lax.broadcasted_iota(jnp.int32, (n_query, n_keys), 1) % HALF
+    )
+    lower = lax.broadcasted_iota(jnp.int32, (n_query, 128), 1) < 64
+    row = lax.broadcasted_iota(jnp.int32, (n_query, 1), 0) // HALF
+    inside = ((row >= 2 * HALO) | (valid[0] > 0)) & ((row < 2 * HALO + HB) | (valid[1] > 0))
+    pairs = []
+    for pair in range(HEADS // 2):
+        lanes = slice(128 * pair, 128 * pair + 128)
+        q = query[h, :, lanes].astype(F32)
+        parts = []
+        for sub in range(2):
+            q_half = jnp.where(lower if sub == 0 else ~lower, q, 0.0).astype(BF16)
+            scores = mm(q_half, keys[:, lanes], ((1,), (1,)))
+            weight = jnp.where(same, jnp.exp(scores * scale[2 * pair + sub]), 0.0)
+            total = jnp.sum(weight, axis=1, keepdims=True)
+            parts.append(mm(weight.astype(BF16), values[:, lanes]) / total)
+        pairs.append(jnp.where(lower, parts[0], parts[1]).astype(BF16))
+    attended = jnp.concatenate(pairs, axis=1)
+    return jnp.where(inside, half_feat + mm(attended, w_out[...]), 0.0)
 
 
 def cot_rows(masked, above, below):
@@ -215,36 +242,38 @@
     return jnp.sum(a, axis=0, keepdims=True)
 
 
-def right_half_kernel(tiles, mixed, masked, above, below, *refs):
-    sublayer(1, None, tiles, mixed, None, masked, above, below, *refs)
-
-
-def left_half_kernel(at_first, tiles, mixed, got, masked, above, below, *refs):
-    sublayer(0, at_first, tiles, mixed, got, masked, above, below, *refs)
+def right_half_kernel(tiles, mixed_left, mixed_right, masked, above, below, *refs):
+    sublayer(1, None, tiles, mixed_left, mixed_right, None, masked, above, below, *refs)
+
+
+def left_half_kernel(at_first, tiles, mixed_left, mixed_right, got, masked, above, below, *refs):
+    sublayer(0, at_first, tiles, mixed_left, mixed_right, got, masked, above, below, *refs)
 
 
 def sublayer(
-    h, at_first, tiles, mixed, got, masked, above, below, taps, dw_bias, ln_gain, ln_bias,
-    w_up, b_up, w_down, b_down, layer_scale, output, d_out, lnout_out, hidden_out, d_pre_out,
-    d_branch_out, sums, *refs,
+    h, at_first, tiles, mixed_left, mixed_right, got, masked, above, below, taps, dw_bias, ln_gain,
+    ln_bias, w_up, b_up, w_down, b_down, layer_scale, output, d_out, lnout_out, hidden_out,
+    d_pre_out, d_branch_out, sums, tap_sums, *refs,
 ):
+    is_first = None
     if h == 0:
-        win_out, send, win, grid, spat, edges = refs
+        send, win, grid, spat, edges = refs
         is_first = at_first[0] > 0
         halo = got[...].astype(F32)
     else:
         win, grid, spat = refs
-        is_first = None
-    for r in range(ROWS_M):
-        win[r, 8 : 8 + WB, :] = mixed[r * WB : (r + 1) * WB, :].astype(F32)
-        if h == 0:
+    for i, mixed in enumerate((mixed_left, mixed_right)):
+        values = mixed[...].astype(F32)
+        for r in range(ROWS_M):
+            win[r, 8 + HALF * i : 8 + HALF * i + HALF, :] = values[r * HALF : (r + 1) * HALF]
+    if h == 0:
+        for r in range(ROWS_M):
             win[r, 2:8, :] = halo[6 * r : 6 * r + 6]
     grid[:, 8 : 8 + WB, :] = cot_rows(masked, above, below).astype(F32).reshape(ROWS_D, WB, C)
     pixel = lax.broadcasted_iota(jnp.int32, (PIX_H, 1), 0)
     row, col = pixel // HALF, pixel % HALF + HALF * h - HALO
     weight = occupied(tiles, row, jnp.maximum(col, 0))
     if h == 0:
-        win_out[...] = win[HALO : HALO + ROWS_D].astype(BF16)
         for r in range(ROWS_D):
             at = RIGHT_COT + HALO * r
             grid[r, 8 - HALO : 8, :] = halo[at : at + HALO]
@@ -310,6 +339,24 @@
     sums[3:4, :C] = rowsum(d_branch[OWN])
     sums[4:5, :C] = rowsum(cotan[OWN] * branch)
     sums[5:6, :] = rowsum(d_pre[OWN])
+    tap_sums[...] = jnp.zeros_like(tap_sums)
+    for t in range(TILES_L):
+        lanes = slice(128 * t, 128 * t + 128)
+        d_rows = [
+            d_spatial[(HALO + r) * HALF : (HALO + r + 1) * HALF, lanes] for r in range(HB)
+        ]
+        for dj in range(7):
+            at = 2 + HALF * h + dj
+            cols = [win[HALO + r, at : at + HALF, lanes] for r in range(ROWS_D)]
+            if h == 0 and dj != 3:
+                mask = border_mask(is_first, dj, 0, HALF)
+                cols = [col * mask for col in cols]
+            for di in range(7):
+                acc = cols[di] * d_rows[0]
+                for r in range(1, HB):
+                    acc = acc + cols[r + di] * d_rows[r]
+                row = 56 * t + 7 * di + dj
+                tap_sums[row : row + 1, :] = rowsum(acc)
 
 
 def up_order():
@@ -318,15 +365,14 @@
 
 
 def gradient_kernel(
-    flags, order, win_in, *refs
+    core, order, *refs
 ):
     halves = [refs[:6], refs[6:12]]
-    mine, other, win, down, small = refs[12:]
+    mine, other, down, small = refs[12:]
     lnout, hidden, d_pre, d_branch = [
         jnp.concatenate([halves[0][i][...], halves[1][i][...]], axis=0) for i in range(4)
     ]
-    is_zero = flags[0] == 0
-    is_first = flags[1] > 0
+    is_zero = core[0] == 0
 
     def put(row, x, zero, one):
         size = zero.shape[0]
@@ -358,29 +404,8 @@
                         for c in range(2)
                     ]
                     put(512 + (yh * 8 + k) * 32 + 16 * two, x, *pair)
-    win[...] = win_in[...].astype(F32)
     small[...] = jnp.zeros_like(small)
-    masks = [border_mask(is_first, dj, 0, HALF) for dj in range(7)]
-    for t in range(TILES_L):
-        lanes = slice(128 * t, 128 * t + 128)
-        d_rows = [
-            [d[(HALO + r) * HALF : (HALO + r + 1) * HALF, lanes] for r in range(HB)]
-            for d in (halves[0][4], halves[1][4])
-        ]
-        for dj in range(7):
-            cols = [
-                [win[r, 2 + dj + HALF * h : 2 + dj + HALF * h + HALF, lanes] for r in range(HB + 6)]
-                for h in range(2)
-            ]
-            if dj != 3:
-                cols[0] = [col * masks[dj] for col in cols[0]]
-            for di in range(7):
-                acc = cols[0][di] * d_rows[0][0]
-                for h in range(2):
-                    for r in range(1 - h, HB):
-                        acc = acc + cols[h][r + di] * d_rows[h][r]
-                at = 56 * t + 7 * di + dj
-                small[at : at + 1, :] = rowsum(acc)
+    small[:168, :] = halves[0][4][...] + halves[1][4][...]
     sums = halves[0][5][...] + halves[1][5][...]
     for i in range(5):
         for t in range(TILES_L):
@@ -395,8 +420,7 @@
         put(1024, x, *pair)
 
 
-def spread_kernel(part, send, out, send_out, total):
-    send_out[...] = send[...]
+def spread_kernel(part, after, out, total):
     total[...] = (
         (part[0].astype(F32) + part[1].astype(F32)) + (part[2].astype(F32) + part[3].astype(F32))
     )
@@ -459,7 +483,8 @@
     depthwise(win, taps, HB, 8, (0, 1), start, True, store)
 
 
-def core_sum_kernel(mine, got, out):
+def core_sum_kernel(mine, got, send, out, send_out):
+    send_out[...] = send[...]
     out[...] = (mine[...].astype(F32) + got[...].astype(F32)).astype(BF16)
 
 
@@ -494,23 +519,25 @@
     )
     at_row = lax.axis_index(ROW)
     valid = jnp.stack([at_row > 0, at_row < N_ROW - 1]).astype(jnp.int32)
-    mixed, send = call(
-        attention_kernel, [((ROWS_M * WB, C), BF16), ((RIGHT, C), BF16)],
-        logit_scale, valid, tiles, pooled, query, flat, masked, above, below, w_key, w_value, w_out,
-        scratch=[
-            pltpu.VMEM((ROWS_M, WB, C), F32), pltpu.VMEM((ROWS_D, WB, C), F32),
-            pltpu.VMEM((RIGHT, C), F32),
-        ],
-        smem=(0, 1, 2), flops=10**9, nbytes=2_000_000, trans=500_000,
+    inputs = (logit_scale, valid, pooled, query, flat, above, below, w_key, w_value, w_out)
+    half_mixed = ((ROWS_M * HALF, C), BF16)
+    cost = dict(flops=5 * 10**8, nbytes=1_500_000, trans=250_000)
+    mixed_right, send = call(
+        right_attention_kernel, [half_mixed, ((RIGHT, C), BF16)], *inputs, tiles, masked,
+        scratch=[pltpu.VMEM((ROWS_D, WB, C), F32), pltpu.VMEM((RIGHT, C), F32)],
+        smem=(0, 1, 10), **cost,
     )
     n_col = lax.axis_size(COL)
     at_col = lax.axis_index(COL)
     got = lax.ppermute(send, COL, [(i, (i + 1) % n_col) for i in range(n_col)])
+    (mixed_left,) = call(
+        left_attention_kernel, [half_mixed], *inputs, mixed_right, smem=(0, 1), fence=(10,), **cost
+    )
     ends = jnp.stack([at_col == 0, at_col == n_col - 1]).astype(jnp.int32)
 
     half_outs = [
         ((PIX_H, C), BF16), ((ROWS_D * HALF, C), F32), ((PIX_H, C), BF16), ((PIX_H, HID), BF16),
-        ((PIX_H, HID), BF16), ((PIX_H, C), BF16), ((8, HID), F32),
+        ((PIX_H, HID), BF16), ((PIX_H, C), BF16), ((8, HID), F32), ((168, 128), F32),
     ]
     half_scratch = [
         pltpu.VMEM((ROWS_M, WCOL, C), F32), pltpu.VMEM((ROWS_D, WCOL, C), F32),
@@ -521,38 +548,39 @@
         row(layer_scale),
     )
     cost = dict(flops=10**9, nbytes=4_000_000, trans=150_000)
-    out_right, d_right, *stats_right, sums_right = call(
-        right_half_kernel, half_outs, tiles, mixed, masked, above, below, *params,
+    out_right, d_right, *stats_right, sums_right, taps_right = call(
+        right_half_kernel, half_outs, tiles, mixed_left, mixed_right, masked, above, below, *params,
         scratch=half_scratch, smem=(0,), **cost,
     )
-    out_left, d_left, *stats_left, sums_left, win, send = call(
-        left_half_kernel, half_outs + [((ROWS_D, WCOL, C), BF16), ((LEFT, C), BF16)],
-        ends, tiles, mixed, got, masked, above, below, *params,
+    out_left, d_left, *stats_left, sums_left, taps_left, send = call(
+        left_half_kernel, half_outs + [((LEFT, C), BF16)],
+        ends, tiles, mixed_left, mixed_right, got, masked, above, below, *params,
         scratch=half_scratch + [pltpu.VMEM((LEFT, C), F32)], smem=(0, 1), **cost,
     )
 
-    flags = jnp.stack([lax.axis_index("c"), ends[0]])
+    core = lax.axis_index("c").reshape(1)
     order = jnp.asarray(up_order(), BF16)
     record = ((N_X, REC, 128), BF16)
     mine, other = call(
         gradient_kernel, [record, record],
-        flags, order, win, *stats_left, d_left, sums_left, *stats_right, d_right, sums_right,
+        core, order, *stats_left, taps_left, sums_left, *stats_right, taps_right, sums_right,
         scratch=[
-            pltpu.VMEM((ROWS_D, WCOL, C), F32),
             pltpu.VMEM((TILES_L, HID, 128), F32),
             pltpu.VMEM((8 * SMALL, 128), F32),
         ],
         smem=(0,), flops=2 * 10**9, nbytes=4_000_000,
     )
     got = lax.ppermute(other, "c", [(0, 1), (1, 0)])
-    (part,) = call(core_sum_kernel, [record], mine, got, nbytes=3_000_000)
+    part, send = call(
+        core_sum_kernel, [record, ((LEFT, C), BF16)], mine, got, send, nbytes=3_000_000
+    )
     part = lax.all_to_all(part, "x", 0, 0, tiled=True)
-    part, send = call(
-        spread_kernel, [((N_YZ, 16 + SMALL, 128), BF16), ((LEFT, C), BF16)], part, send,
-        scratch=[pltpu.VMEM((REC, 128), F32)], nbytes=2_000_000,
-    )
-    part = lax.all_to_all(part, YZ, 0, 0, tiled=True)
     got = lax.ppermute(send, COL, [(i, (i - 1) % n_col) for i in range(n_col)])
+    (spread,) = call(
+        spread_kernel, [((N_YZ, 16 + SMALL, 128), BF16)], part, got, fence=(1,),
+        scratch=[pltpu.VMEM((REC, 128), F32)], hbm=(0,), nbytes=2_000_000,
+    )
+    part = lax.all_to_all(spread, YZ, 0, 0, tiled=True)
     share, small = call(
         gather_kernel, [((16, 128), F32), ((N_X * N_C, SMALL, 128), F32)], part, nbytes=800_000
     )
@@ -565,7 +593,7 @@
     shares = jnp.where(lax.axis_index("yh") == 0, shares[:, :SHARE], shares[:, 8 * 128 - SHARE :])
     grad_mixed, output = call(
         finish_kernel, [((PIX, C), F32), ((PIX, C), BF16)],
-        ends, share, d_left, d_right, out_left, out_right, got, cot, dw_kernel,
+        ends, spread, d_left, d_right, out_left, out_right, got, cot, dw_kernel,
         scratch=[pltpu.VMEM((ROWS_D, WCOL, C), F32)], smem=(0,), fence=(1,), flops=10**7, nbytes=1_000_000,
     )
     bias, gain, shift, b_down_grad, scale_grad, b_up_grad = vectors[1:]

time: 121 us -> 121 us (level)
  blocking collectives: 17.4 us -> 0 us
  waiting for transfers between devices: 28.5 us -> 42.5 us
  starting transfers between devices: 49.8 us -> 51.6 us
    all_to_all x1 -> x0, blocking collectives: 17.4 us -> none  [body(): part = lax.all_to_all(part, 'x', 0, 0, tiled=True)]
    all_to_all x1 -> x2, waiting for transfers between devices: 9.85 us -> 19.4 us  [the longest x1 16.7 us: body(): part = lax.all_to_all(spread, YZ, 0, 0, tiled=True)]
    ppermute x1, waiting for transfers between devices: 0.01 us -> 3.87 us  [body(): got = lax.ppermute(send, COL, [(i, (i - 1) % n_col) for i in range(n_col)])]
    all_to_all x1 -> x2, starting transfers between devices: 10.1 us -> 13.8 us  [the longest x1 10.2 us: body(): part = lax.all_to_all(spread, YZ, 0, 0, tiled=True)]
    all_to_all x1, waiting for transfers between devices: 1.31 us -> 4.32 us  [body(): small = lax.all_to_all(small, CX, 0, 0, tiled=True)]
    ppermute x1, waiting for transfers between devices: 8.2 us -> 5.88 us  [body(): got = lax.ppermute(send, COL, [(i, (i + 1) % n_col) for i in range(n_col)])]
    all_to_all x1, starting transfers between devices: 8.78 us -> 7.03 us  [body(): small = lax.all_to_all(small, CX, 0, 0, tiled=True)]
    pallas_call x12 -> x13, Pallas kernels: 21.8 us -> 23 us  [call(): pl.pallas_call(run, out_shape=[jax.ShapeDtypeStruct(s, d) for s, d in out...]
  transfers between devices with their start and end apart: 8 -> 9, of which waited for: 6 -> 8; matrix products, arithmetic and copies ran while one was open for 1% -> 1% of each run, Pallas kernels for 7% -> 9%
where the time goes in v5:
time: 121 us; the launch traced here: 120 us
  starting transfers between devices  51.6 us (43%)
  waiting for transfers between devices  42.5 us (35%)
  Pallas kernels  23 us (19%)
  local copies, waits for them, and re-layouts  1.61 us (1%)
    pallas_call x13, Pallas kernels, call(): pl.pallas_call(run, out_shape=[jax.ShapeDtypeStruct(s, d) for s, d in out...  23 us
    all_to_all x1, waiting for transfers between devices, body(): part = lax.all_to_all(spread, YZ, 0, 0, tiled=True)  16.7 us
    all_to_all x1, starting transfers between devices, body(): lax.all_to_all(copies, ROW, 0, 0, tiled=True).reshape(N_ROW * WB, C)  10.6 us
    all_to_all x1, starting transfers between devices, body(): part = lax.all_to_all(spread, YZ, 0, 0, tiled=True)  10.2 us
    ppermute x1, starting transfers between devices, body(): got = lax.ppermute(send, COL, [(i, (i - 1) % n_col) for i in range(n_col)])  8.67 us
    all_to_all x1, starting transfers between devices, body(): small = lax.all_to_all(small, CX, 0, 0, tiled=True)  7.03 us
    ppermute x1, waiting for transfers between devices, body(): got = lax.ppermute(send, COL, [(i, (i + 1) % n_col) for i in range(n_col)])  5.88 us
    ppermute x1, waiting for transfers between devices, neighbours(): lax.ppermute(before_edge, axes, down)  4.48 us
  transfers between devices with their start and end apart: 9, of which 8 were waited for; matrix products, arithmetic and copies ran while one was open for 1% of the time, Pallas kernels for 9%

profile of v5, /device:TPU:1, one launch (start us, length us, event | category | flops | bytes accessed | tf_op | source)
XLA Modules:
  0.0 120.0 jit_solution(6822457082748238450)
XLA Ops:
  2.4 10.6 %all-to-all-start = ((bf16[32,16,384]{2,1,0:T(8,128)(2,1)}), bf16[32,16,384]{2,1,0:T(8,128)(2,1)S(1)}, u32[]{:S(2)}, u32[]{:S(2)}) async-start(bf16[32,16,384]{2,1,0:T(8,128)(2,1)} %shard_map.257.refs_1_), calls=%async_computation | async-start | bytes 786432 | tf_op jit(solution)/shard_map/all_to_all | solution.py:507
  13.6 3.5 %collective-permute-start = (bf16[144,384]{1,0:T(8,128)(2,1)S(1)}, bf16[144,384]{1,0:T(8,128)(2,1)S(1)}, u32[]{:S(2)}, u32[]{:S(2)}) collective-permute-start(bf16[144,384]{1,0:T(8,128)(2,1)S(1)} %get-tuple-element.48), channel_id=1, source_target_pairs={{0,16},{16,32},{32,48},{48,64},{64,80},{80,96},{96,112},{112,128},... | collective-permute-start | bytes 331784 | tf_op jit(solution)/shard_map/ppermute | solution.py:495
  17.2 1.9 %collective-permute-start.1 = (bf16[144,384]{1,0:T(8,128)(2,1)S(1)}, bf16[144,384]{1,0:T(8,128)(2,1)S(1)}, u32[]{:S(2)}, u32[]{:S(2)}) collective-permute-start(bf16[144,384]{1,0:T(8,128)(2,1)S(1)} %get-tuple-element.49), channel_id=1, source_target_pairs={{16,0},{32,16},{48,32},{64,48},{80,64},{96,80},{112,96},{128,112},... | collective-permute-start | bytes 331784 | tf_op jit(solution)/shard_map/ppermute | solution.py:495
  19.4 4.5 %collective-permute-done.1.refs_2_.refs_6_.refs_7_.refs_5_ = bf16[144,384]{1,0:T(8,128)(2,1)S(1)} collective-permute-done((bf16[144,384]{1,0:T(8,128)(2,1)S(1)}, bf16[144,384]{1,0:T(8,128)(2,1)S(1)}, u32[]{:S(2)}, u32[]{:S(2)}) %collective-permute-start.1) | collective-permute-done | bytes 110624 | tf_op jit(solution)/shard_map/ppermute | solution.py:495
  24.6 2.3 %all-to-all-done = bf16[32,16,384]{2,1,0:T(8,128)(2,1)S(1)} async-done(((bf16[32,16,384]{2,1,0:T(8,128)(2,1)}), bf16[32,16,384]{2,1,0:T(8,128)(2,1)S(1)}, u32[]{:S(2)}, u32[]{:S(2)}) %all-to-all-start) | async-done | bytes 393248 | tf_op jit(solution)/shard_map/all_to_all | solution.py:507
  26.9 1.8 %shard_map.260 = (bf16[160,384]{1,0:T(8,128)(2,1)S(1)}, bf16[176,384]{1,0:T(8,128)(2,1)S(1)}) custom-call(f32[6]{0:T(128)S(1)} %copy-done.9, s32[2]{0:T(128)S(1)} %add_convert_fusion.1.refs_1_, bf16[512,384]{1,0:T(8,128)(2,1)S(1)} %bitcast.14, bf16[2,160,384]{2,1,0:T(8,128)(2,1)S(1)} %shard_map.259.refs_3_, bf16[128,384]{1,0:T(8,128)(2,1)S(1)} %bitcast.18, ...), custom_call_target="tpu_custom_call" | custom-call | flops 500000000 | bytes 1500000 | tf_op jit(solution)/shard_map/pallas_call | solution.py:83
  28.8 3.5 %collective-permute-start.2 = (bf16[176,384]{1,0:T(8,128)(2,1)S(1)}, bf16[176,384]{1,0:T(8,128)(2,1)S(1)}, u32[]{:S(2)}, u32[]{:S(2)}) collective-permute-start(bf16[176,384]{1,0:T(8,128)(2,1)S(1)} %get-tuple-element.52), channel_id=1, source_target_pairs={{0,1},{1,2},{2,3},{3,4},{4,5},{5,6},{6,7},{7,8},{8,9},{9,10},{10,1... | collective-permute-start | bytes 405512 | tf_op jit(solution)/shard_map/ppermute | solution.py:532
  32.3 1.8 %shard_map.261.refs_2_.refs_1_ = bf16[160,384]{1,0:T(8,128)(2,1)S(1)} custom-call(f32[6]{0:T(128)S(1)} %copy-done.9, s32[2]{0:T(128)S(1)} %add_convert_fusion.1.refs_1_, bf16[512,384]{1,0:T(8,128)(2,1)S(1)} %bitcast.15, bf16[2,160,384]{2,1,0:T(8,128)(2,1)S(1)} %shard_map.259.refs_3_, bf16[128,384]{1,0:T(8,128)(2,1)S(1)} %bitcast.19, ...), custom_call_target="tpu_custom_call" | custom-call | flops 500000000 | bytes 1500000 | tf_op jit(solution)/shard_map/pallas_call | solution.py:83
  34.1 4.5 %shard_map.263 = (bf16[64,384]{1,0:T(8,128)(2,1)S(1)}, f32[112,384]{1,0:T(8,128)S(1)}, bf16[64,384]{1,0:T(8,128)(2,1)S(1)}, bf16[64,1280]{1,0:T(8,128)(2,1)S(1)}...) custom-call(s32[8]{0:T(128)S(1)} %bitcast.25, ...), custom_call_target="tpu_custom_call" | custom-call | flops 1000000000 | bytes 4000000 | tf_op jit(solution)/shard_map/pallas_call | solution.py:83
  38.7 5.9 %collective-permute-done.2.refs_4_ = bf16[176,384]{1,0:T(8,128)(2,1)S(1)} collective-permute-done((bf16[176,384]{1,0:T(8,128)(2,1)S(1)}, bf16[176,384]{1,0:T(8,128)(2,1)S(1)}, u32[]{:S(2)}, u32[]{:S(2)}) %collective-permute-start.2) | collective-permute-done | bytes 135200 | tf_op jit(solution)/shard_map/ppermute | solution.py:532
  44.6 4.8 %shard_map.262 = (bf16[64,384]{1,0:T(8,128)(2,1)S(1)}, f32[112,384]{1,0:T(8,128)S(1)}, bf16[64,384]{1,0:T(8,128)(2,1)S(1)}, bf16[64,1280]{1,0:T(8,128)(2,1)S(1)}...) custom-call(s32[2]{0:T(128)S(1)} %add_convert_fusion.refs_0_, ...), custom_call_target="tpu_custom_call" | custom-call | flops 1000000000 | bytes 4000000 | tf_op jit(solution)/shard_map/pallas_call | solution.py:83
  50.4 2.5 %collective-permute-start.3 = (bf16[4,1056,128]{2,1,0:T(8,128)(2,1)S(1)}, bf16[4,1056,128]{2,1,0:T(8,128)(2,1)S(1)}, u32[]{:S(2)}, u32[]{:S(2)}) collective-permute-start(bf16[4,1056,128]{2,1,0:T(8,128)(2,1)S(1)} %get-tuple-element.66), channel_id=1, source_target_pairs={{0,16},{16,0},{1,17},{17,1},{2,18},{18,2},{3,19},{19,3},{4,20},{20... | collective-permute-start | bytes 3244040 | tf_op jit(solution)/shard_map/ppermute | solution.py:573
  53.0 2.3 %collective-permute-done.3.refs_1_ = bf16[4,1056,128]{2,1,0:T(8,128)(2,1)S(1)} collective-permute-done((bf16[4,1056,128]{2,1,0:T(8,128)(2,1)S(1)}, bf16[4,1056,128]{2,1,0:T(8,128)(2,1)S(1)}, u32[]{:S(2)}, u32[]{:S(2)}) %collective-permute-start.3) | collective-permute-done | bytes 1081376 | tf_op jit(solution)/shard_map/ppermute | solution.py:573
  55.3 1.3 %shard_map.265 = (bf16[4,1056,128]{2,1,0:T(8,128)(2,1)}, bf16[112,384]{1,0:T(8,128)(2,1)S(1)}) custom-call(bf16[4,1056,128]{2,1,0:T(8,128)(2,1)S(1)} %get-tuple-element.65.refs_0_, bf16[4,1056,128]{2,1,0:T(8,128)(2,1)S(1)} %collective-permute-done.3.refs_1_, bf16[112,384]{1,0:T(8,128)(2,1)S(1)} %get-tuple-element.67.refs_2_), custom_call_target="tpu_custom_call" | custom-call | bytes 3000000 | tf_op jit(solution)/shard_map/pallas_call | solution.py:83
  56.5 3.5 %all-to-all-start.1 = ((bf16[4,1056,128]{2,1,0:T(8,128)(2,1)}), bf16[4,1056,128]{2,1,0:T(8,128)(2,1)S(1)}, u32[]{:S(2)}, u32[]{:S(2)}) async-start(bf16[4,1056,128]{2,1,0:T(8,128)(2,1)} %get-tuple-element.68), calls=%async_computation.1 | async-start | bytes 2162688 | tf_op jit(solution)/shard_map/all_to_all | solution.py:577
  60.0 8.7 %collective-permute-start.4 = (bf16[112,384]{1,0:T(8,128)(2,1)S(1)}, bf16[112,384]{1,0:T(8,128)(2,1)S(1)}, u32[]{:S(2)}, u32[]{:S(2)}) collective-permute-start(bf16[112,384]{1,0:T(8,128)(2,1)S(1)} %get-tuple-element.69), channel_id=1, source_target_pairs={{0,15},{1,0},{2,1},{3,2},{4,3},{5,4},{6,5},{7,6},{8,7},{9,8},{10,9... | collective-permute-start | bytes 258056 | tf_op jit(solution)/shard_map/ppermute | solution.py:578
  68.7 3.9 %collective-permute-done.4.refs_1_.refs_6_ = bf16[112,384]{1,0:T(8,128)(2,1)S(1)} collective-permute-done((bf16[112,384]{1,0:T(8,128)(2,1)S(1)}, bf16[112,384]{1,0:T(8,128)(2,1)S(1)}, u32[]{:S(2)}, u32[]{:S(2)}) %collective-permute-start.4) | collective-permute-done | bytes 86048 | tf_op jit(solution)/shard_map/ppermute | solution.py:578
  72.6 2.6 %all-to-all-done.1.refs_0_ = bf16[4,1056,128]{2,1,0:T(8,128)(2,1)S(1)} async-done(((bf16[4,1056,128]{2,1,0:T(8,128)(2,1)}), bf16[4,1056,128]{2,1,0:T(8,128)(2,1)S(1)}, u32[]{:S(2)}, u32[]{:S(2)}) %all-to-all-start.1) | async-done | bytes 1081376 | tf_op jit(solution)/shard_map/all_to_all | solution.py:577
  75.2 1.3 %shard_map.266.refs_1_ = bf16[64,40,128]{2,1,0:T(8,128)(2,1)} custom-call(bf16[4,1056,128]{2,1,0:T(8,128)(2,1)S(1)} %all-to-all-done.1.refs_0_, bf16[112,384]{1,0:T(8,128)(2,1)S(1)} %collective-permute-done.4.refs_1_.refs_6_), custom_call_target="tpu_custom_call" | custom-call | bytes 2000000 | tf_op jit(solution)/shard_map/pallas_call | solution.py:83
  76.5 10.2 %all-to-all-start.2 = ((bf16[64,40,128]{2,1,0:T(8,128)(2,1)}), bf16[64,40,128]{2,1,0:T(8,128)(2,1)S(1)}, u32[]{:S(2)}, u32[]{:S(2)}) async-start(bf16[64,40,128]{2,1,0:T(8,128)(2,1)} %shard_map.266.refs_1_), calls=%async_computation.2 | async-start | bytes 1310720 | tf_op jit(solution)/shard_map/all_to_all | solution.py:583
  86.8 3.0 %shard_map.267 = (f32[128,384]{1,0:T(8,128)}, bf16[128,384]{1,0:T(8,128)(2,1)}) custom-call(s32[2]{0:T(128)S(1)} %add_convert_fusion.refs_0_, bf16[64,40,128]{2,1,0:T(8,128)(2,1)} %shard_map.266.refs_1_, f32[112,384]{1,0:T(8,128)S(1)} %get-tuple-element.70.refs_2_, f32[112,384]{1,0:T(8,128)S(1)} %get-tuple-element.71.refs_3_, ...), custom_call_target="tpu_custom_call" | custom-call | flops 10000000 | bytes 1000000 | tf_op jit(solution)/shard_map/pallas_call | solution.py:83
  89.8 16.7 %all-to-all-done.2.refs_0_ = bf16[64,40,128]{2,1,0:T(8,128)(2,1)S(1)} async-done(((bf16[64,40,128]{2,1,0:T(8,128)(2,1)}), bf16[64,40,128]{2,1,0:T(8,128)(2,1)S(1)}, u32[]{:S(2)}, u32[]{:S(2)}) %all-to-all-start.2) | async-done | bytes 655392 | tf_op jit(solution)/shard_map/all_to_all | solution.py:583
  107.3 7.0 %all-to-all-start.3 = ((f32[8,24,128]{2,1,0:T(8,128)}), f32[8,24,128]{2,1,0:T(8,128)S(1)}, u32[]{:S(2)}, u32[]{:S(2)}) async-start(f32[8,24,128]{2,1,0:T(8,128)} %get-tuple-element.77), calls=%async_computation.3 | async-start | bytes 196608 | tf_op jit(solution)/shard_map/all_to_all | solution.py:587
  115.0 4.3 %all-to-all-done.3 = f32[8,24,128]{2,1,0:T(8,128)S(1)} async-done(((f32[8,24,128]{2,1,0:T(8,128)}), f32[8,24,128]{2,1,0:T(8,128)S(1)}, u32[]{:S(2)}, u32[]{:S(2)}) %all-to-all-start.3) | async-done | bytes 98336 | tf_op jit(solution)/shard_map/all_to_all | solution.py:587
  (56 shorter events, 6.3 us)
Async XLA Ops:
  1.5 11.4 %copy-start.1 = (bf16[8,16,384]{2,1,0:T(8,128)(2,1)S(1)}, bf16[8,16,384]{2,1,0:T(8,128)(2,1)}, u32[]{:S(2)}) copy-start(bf16[8,16,384]{2,1,0:T(8,128)(2,1)} %refs_0_.3) | copy-start | bytes 294916
  1.5 11.4 %copy-start.5 = (bf16[8,16,384]{2,1,0:T(8,128)(2,1)S(1)}, bf16[8,16,384]{2,1,0:T(8,128)(2,1)}, u32[]{:S(2)}) copy-start(bf16[8,16,384]{2,1,0:T(8,128)(2,1)} %param.33) | copy-start | bytes 294916
  1.5 11.5 %copy-start.8 = (s32[1,1,8]{2,1,0:T(1,128)S(1)}, s32[1,1,8]{2,1,0:T(1,128)}, u32[]{:S(2)}) copy-start(s32[1,1,8]{2,1,0:T(1,128)} %param.34) | copy-start | bytes 100
  1.5 17.6 %copy-start.14 = (f32[384]{0:T(512)S(1)}, f32[384]{0:T(512)}, u32[]{:S(2)}) copy-start(f32[384]{0:T(512)} %param.25) | copy-start | bytes 4612
  1.6 17.6 %copy-start.15 = (f32[384]{0:T(512)S(1)}, f32[384]{0:T(512)}, u32[]{:S(2)}) copy-start(f32[384]{0:T(512)} %param.26) | copy-start | bytes 4612
  1.6 17.6 %copy-start.16 = (f32[384]{0:T(512)S(1)}, f32[384]{0:T(512)}, u32[]{:S(2)}) copy-start(f32[384]{0:T(512)} %param.27) | copy-start | bytes 4612
  1.6 17.6 %copy-start.17 = (f32[384]{0:T(512)S(1)}, f32[384]{0:T(512)}, u32[]{:S(2)}) copy-start(f32[384]{0:T(512)} %param.31) | copy-start | bytes 4612
  1.6 17.6 %copy-start.18 = (f32[384]{0:T(512)S(1)}, f32[384]{0:T(512)}, u32[]{:S(2)}) copy-start(f32[384]{0:T(512)} %param.32) | copy-start | bytes 4612
  1.6 17.7 %copy-start.13 = (f32[1280]{0:T(1024)S(1)}, f32[1280]{0:T(1024)}, u32[]{:S(2)}) copy-start(f32[1280]{0:T(1024)} %param.29) | copy-start | bytes 15364
  1.6 22.3 %copy-start.6 = (bf16[384,384]{1,0:T(8,128)(2,1)S(1)}, bf16[384,384]{1,0:T(8,128)(2,1)}, u32[]{:S(2)}) copy-start(bf16[384,384]{1,0:T(8,128)(2,1)} %refs_3_.1) | copy-start | bytes 884740
  2.4 24.5 %copy-start.2 = (bf16[384,384]{1,0:T(8,128)(2,1)S(1)}, bf16[384,384]{1,0:T(8,128)(2,1)}, u32[]{:S(2)}) copy-start(bf16[384,384]{1,0:T(8,128)(2,1)} %refs_7_.3) | copy-start | bytes 884740
  2.4 24.5 %copy-start.3 = (bf16[384,384]{1,0:T(8,128)(2,1)S(1)}, bf16[384,384]{1,0:T(8,128)(2,1)}, u32[]{:S(2)}) copy-start(bf16[384,384]{1,0:T(8,128)(2,1)} %refs_8_.5) | copy-start | bytes 884740
  2.4 24.5 %copy-start.4 = (bf16[384,384]{1,0:T(8,128)(2,1)S(1)}, bf16[384,384]{1,0:T(8,128)(2,1)}, u32[]{:S(2)}) copy-start(bf16[384,384]{1,0:T(8,128)(2,1)} %refs_9_.3) | copy-start | bytes 884740
  2.4 24.5 %copy-start.9 = (f32[6]{0:T(128)S(1)}, f32[6]{0:T(128)}, u32[]{:S(2)}) copy-start(f32[6]{0:T(128)} %refs_0_.5) | copy-start | bytes 76
  2.4 24.5 %all-to-all-start = ((bf16[32,16,384]{2,1,0:T(8,128)(2,1)}), bf16[32,16,384]{2,1,0:T(8,128)(2,1)S(1)}, u32[]{:S(2)}, u32[]{:S(2)}) async-start(bf16[32,16,384]{2,1,0:T(8,128)(2,1)} %shard_map.257.refs_1_), calls=%async_computation | async-start | bytes 786432 | tf_op jit(solution)/shard_map/all_to_all | solution.py:507
  13.6 5.8 %collective-permute-start = (bf16[144,384]{1,0:T(8,128)(2,1)S(1)}, bf16[144,384]{1,0:T(8,128)(2,1)S(1)}, u32[]{:S(2)}, u32[]{:S(2)}) collective-permute-start(bf16[144,384]{1,0:T(8,128)(2,1)S(1)} %get-tuple-element.48), channel_id=1, source_target_pairs={{0,16},{16,32},{32,48},{48,64},{64,80},{80,96},{96,112},{112,128},... | collective-permute-start | bytes 331784 | tf_op jit(solution)/shard_map/ppermute | solution.py:495
  17.2 6.7 %collective-permute-start.1 = (bf16[144,384]{1,0:T(8,128)(2,1)S(1)}, bf16[144,384]{1,0:T(8,128)(2,1)S(1)}, u32[]{:S(2)}, u32[]{:S(2)}) collective-permute-start(bf16[144,384]{1,0:T(8,128)(2,1)S(1)} %get-tuple-element.49), channel_id=1, source_target_pairs={{16,0},{32,16},{48,32},{64,48},{80,64},{96,80},{112,96},{128,112},... | collective-permute-start | bytes 331784 | tf_op jit(solution)/shard_map/ppermute | solution.py:495
  28.8 15.8 %collective-permute-start.2 = (bf16[176,384]{1,0:T(8,128)(2,1)S(1)}, bf16[176,384]{1,0:T(8,128)(2,1)S(1)}, u32[]{:S(2)}, u32[]{:S(2)}) collective-permute-start(bf16[176,384]{1,0:T(8,128)(2,1)S(1)} %get-tuple-element.52), channel_id=1, source_target_pairs={{0,1},{1,2},{2,3},{3,4},{4,5},{5,6},{6,7},{7,8},{8,9},{9,10},{10,1... | collective-permute-start | bytes 405512 | tf_op jit(solution)/shard_map/ppermute | solution.py:532
  38.7 10.7 %copy-start.12 = (bf16[384,384]{1,0:T(8,128)(2,1)S(1)}, bf16[384,384]{1,0:T(8,128)(2,1)}, u32[]{:S(2)}) copy-start(bf16[384,384]{1,0:T(8,128)(2,1)} %constant.33.clone.refs_1_) | copy-start | bytes 884740
  50.4 4.9 %collective-permute-start.3 = (bf16[4,1056,128]{2,1,0:T(8,128)(2,1)S(1)}, bf16[4,1056,128]{2,1,0:T(8,128)(2,1)S(1)}, u32[]{:S(2)}, u32[]{:S(2)}) collective-permute-start(bf16[4,1056,128]{2,1,0:T(8,128)(2,1)S(1)} %get-tuple-element.66), channel_id=1, source_target_pairs={{0,16},{16,0},{1,17},{17,1},{2,18},{18,2},{3,19},{19,3},{4,20},{20... | collective-permute-start | bytes 3244040 | tf_op jit(solution)/shard_map/ppermute | solution.py:573
  56.5 18.7 %all-to-all-start.1 = ((bf16[4,1056,128]{2,1,0:T(8,128)(2,1)}), bf16[4,1056,128]{2,1,0:T(8,128)(2,1)S(1)}, u32[]{:S(2)}, u32[]{:S(2)}) async-start(bf16[4,1056,128]{2,1,0:T(8,128)(2,1)} %get-tuple-element.68), calls=%async_computation.1 | async-start | bytes 2162688 | tf_op jit(solution)/shard_map/all_to_all | solution.py:577
  60.0 12.6 %collective-permute-start.4 = (bf16[112,384]{1,0:T(8,128)(2,1)S(1)}, bf16[112,384]{1,0:T(8,128)(2,1)S(1)}, u32[]{:S(2)}, u32[]{:S(2)}) collective-permute-start(bf16[112,384]{1,0:T(8,128)(2,1)S(1)} %get-tuple-element.69), channel_id=1, source_target_pairs={{0,15},{1,0},{2,1},{3,2},{4,3},{5,4},{6,5},{7,6},{8,7},{9,8},{10,9... | collective-permute-start | bytes 258056 | tf_op jit(solution)/shard_map/ppermute | solution.py:578
  76.5 30.0 %all-to-all-start.2 = ((bf16[64,40,128]{2,1,0:T(8,128)(2,1)}), bf16[64,40,128]{2,1,0:T(8,128)(2,1)S(1)}, u32[]{:S(2)}, u32[]{:S(2)}) async-start(bf16[64,40,128]{2,1,0:T(8,128)(2,1)} %shard_map.266.refs_1_), calls=%async_computation.2 | async-start | bytes 1310720 | tf_op jit(solution)/shard_map/all_to_all | solution.py:583
  107.3 12.0 %all-to-all-start.3 = ((f32[8,24,128]{2,1,0:T(8,128)}), f32[8,24,128]{2,1,0:T(8,128)S(1)}, u32[]{:S(2)}, u32[]{:S(2)}) async-start(f32[8,24,128]{2,1,0:T(8,128)} %get-tuple-element.77), calls=%async_computation.3 | async-start | bytes 196608 | tf_op jit(solution)/shard_map/all_to_all | solution.py:587
  (4 other events, 17.0 us)

commit v6 on v5

--- a/solution.py
+++ b/solution.py
@@ -56,7 +56,7 @@
 
 
 def call(
-    kernel, outs, *args, scratch=(), smem=(), fence=(), hbm=(), flops=0, nbytes=0, trans=0, vmem=16
+    kernel, outs, *args, scratch=(), smem=(), fence=(), hbm=(), own=(), flops=0, nbytes=0, trans=0, vmem=16
 ):
     n_in, n_out, n_scratch = len(args), len(outs), len(scratch)
 
@@ -85,7 +85,7 @@
         out_shape=[jax.ShapeDtypeStruct(s, d) for s, d in outs],
         in_specs=specs,
         out_specs=[
-            pl.BlockSpec(memory_space=pltpu.HBM if i in hbm else pltpu.VMEM) for i in range(n_out)
+            pl.BlockSpec(memory_space=pltpu.HBM if i in hbm or i in own else pltpu.VMEM) for i in range(n_out)
         ],
         scratch_shapes=list(scratch) + buffers,
         compiler_params=pltpu.CompilerParams(vmem_limit_bytes=vmem * 1024 * 1024),
@@ -216,6 +216,18 @@
     return jnp.where(crosses & is_first, 0.0, 1.0)
 
 
+def eight_columns(win, rows, at, lanes):
+    shift = at % 8
+    low = [win[r, at - shift : at - shift + 8, lanes] for r in rows]
+    if shift == 0:
+        return low
+    sub = lax.broadcasted_iota(jnp.int32, (8, 128), 0)
+    high = [win[r, at - shift + 8 : at - shift + 16, lanes] for r in rows]
+    return [
+        pltpu.roll(jnp.where(sub < shift, b, a), 8 - shift, axis=0) for a, b in zip(low, high)
+    ]
+
+
 def depthwise(win, taps, n_out, base, halves, start, flip, store, is_first=None):
     masks = [None] * 7
     if is_first is not None:
@@ -226,7 +238,7 @@
             acc = [start(r, h, lanes) for r in range(n_out)]
             for dj in range(7):
                 at = base + HALF * h + dj
-                cols = [win[r, at : at + HALF, lanes] for r in range(n_out + 6)]
+                cols = eight_columns(win, range(n_out + 6), at, lanes)
                 if h == 0 and dj != 3 and is_first is not None:
                     cols = [col * masks[dj] for col in cols]
                 for di in range(7):
@@ -347,7 +359,7 @@
         ]
         for dj in range(7):
             at = 2 + HALF * h + dj
-            cols = [win[HALO + r, at : at + HALF, lanes] for r in range(ROWS_D)]
+            cols = eight_columns(win, range(HALO, HALO + ROWS_D), at, lanes)
             if h == 0 and dj != 3:
                 mask = border_mask(is_first, dj, 0, HALF)
                 cols = [col * mask for col in cols]
@@ -420,11 +432,12 @@
         put(1024, x, *pair)
 
 
-def spread_kernel(part, after, out, total):
+def spread_kernel(part, after, out, total, buffer, done):
     total[...] = (
         (part[0].astype(F32) + part[1].astype(F32)) + (part[2].astype(F32) + part[3].astype(F32))
     )
     small = total[1024 : 1024 + SMALL, :]
+    copies = []
     for yl in range(N_YL):
         for z in range(N_Z):
             for yh in range(N_YH):
@@ -432,7 +445,12 @@
                 up = total[pl.ds(q * 128 + yl * 4 + z // 2, 8, stride=16), :]
                 down = total[pl.ds(512 + yh * 256 + yl * 8 + z, 8, stride=32), :]
                 record = jnp.concatenate([up, down, small], axis=0)
-                out[(yl * N_Z + z) * N_YH + yh] = record.astype(BF16)
+                buffer[(yl * N_Z + z) * N_YH + yh] = record.astype(BF16)
+        block = pl.ds(yl * N_Z * N_YH, N_Z * N_YH)
+        copies.append(pltpu.make_async_copy(buffer.at[block], out.at[block], done.at[yl]))
+        copies[-1].start()
+    for copy in copies:
+        copy.wait()
 
 
 def gather_kernel(part, share, small):
@@ -483,9 +501,15 @@
     depthwise(win, taps, HB, 8, (0, 1), start, True, store)
 
 
-def core_sum_kernel(mine, got, send, out, send_out):
+def core_sum_kernel(mine, got, send, out, send_out, buffer, done):
+    copies = []
+    for x in range(N_X):
+        buffer[x] = (mine[x].astype(F32) + got[x].astype(F32)).astype(BF16)
+        copies.append(pltpu.make_async_copy(buffer.at[x], out.at[x], done.at[x]))
+        copies[-1].start()
     send_out[...] = send[...]
-    out[...] = (mine[...].astype(F32) + got[...].astype(F32)).astype(BF16)
+    for copy in copies:
+        copy.wait()
 
 
 def neighbours(before_edge, after_edge, axes):
@@ -572,13 +596,18 @@
     )
     got = lax.ppermute(other, "c", [(0, 1), (1, 0)])
     part, send = call(
-        core_sum_kernel, [record, ((LEFT, C), BF16)], mine, got, send, nbytes=3_000_000
+        core_sum_kernel, [record, ((LEFT, C), BF16)], mine, got, send, own=(0,), nbytes=3_000_000,
+        scratch=[pltpu.VMEM((N_X, REC, 128), BF16), pltpu.SemaphoreType.DMA((N_X,))],
     )
     part = lax.all_to_all(part, "x", 0, 0, tiled=True)
     got = lax.ppermute(send, COL, [(i, (i - 1) % n_col) for i in range(n_col)])
     (spread,) = call(
         spread_kernel, [((N_YZ, 16 + SMALL, 128), BF16)], part, got, fence=(1,),
-        scratch=[pltpu.VMEM((REC, 128), F32)], hbm=(0,), nbytes=2_000_000,
+        scratch=[
+            pltpu.VMEM((REC, 128), F32), pltpu.VMEM((N_YZ, 16 + SMALL, 128), BF16),
+            pltpu.SemaphoreType.DMA((N_YL,)),
+        ],
+        own=(0,), nbytes=2_000_000,
     )
     part = lax.all_to_all(spread, YZ, 0, 0, tiled=True)
     share, small = call(

time: 121 us -> 119 us (0.983)
  Pallas kernels: 23 us -> 19.4 us
  waiting for transfers between devices: 42.5 us -> 44.7 us
    pallas_call x13, Pallas kernels: 23 us -> 19.4 us  [call(): pl.pallas_call(run, out_shape=[jax.ShapeDtypeStruct(s, d) for s, d in out...]
    ppermute x1, waiting for transfers between devices: 5.88 us -> 7.2 us  [body(): got = lax.ppermute(send, COL, [(i, (i + 1) % n_col) for i in range(n_col)])]
  transfers between devices with their start and end apart: 9 -> 9, of which waited for: 8 -> 8; matrix products, arithmetic and copies ran while one was open for 1% -> 1% of each run, Pallas kernels for 9% -> 7%
where the time goes in v6:
time: 119 us; the launch traced here: 118 us
  starting transfers between devices  51.4 us (43%)
  waiting for transfers between devices  44.7 us (38%)
  Pallas kernels  19.4 us (16%)
  local copies, waits for them, and re-layouts  1.61 us (1%)
    pallas_call x13, Pallas kernels, call(): pl.pallas_call(run, out_shape=[jax.ShapeDtypeStruct(s, d) for s, d in out...  19.4 us
    all_to_all x1, waiting for transfers between devices, body(): part = lax.all_to_all(spread, YZ, 0, 0, tiled=True)  17.7 us
    all_to_all x1, starting transfers between devices, body(): lax.all_to_all(copies, ROW, 0, 0, tiled=True).reshape(N_ROW * WB, C)  10.6 us
    all_to_all x1, starting transfers between devices, body(): part = lax.all_to_all(spread, YZ, 0, 0, tiled=True)  10.2 us
    ppermute x1, starting transfers between devices, body(): got = lax.ppermute(send, COL, [(i, (i - 1) % n_col) for i in range(n_col)])  8.67 us
    ppermute x1, waiting for transfers between devices, body(): got = lax.ppermute(send, COL, [(i, (i + 1) % n_col) for i in range(n_col)])  7.2 us
    all_to_all x1, starting transfers between devices, body(): small = lax.all_to_all(small, CX, 0, 0, tiled=True)  7.03 us
    ppermute x1, waiting for transfers between devices, neighbours(): lax.ppermute(before_edge, axes, down)  4.48 us
  transfers between devices with their start and end apart: 9, of which 8 were waited for; matrix products, arithmetic and copies ran while one was open for 1% of the time, Pallas kernels for 7%

profile of v6, /device:TPU:1, one launch (start us, length us, event | category | flops | bytes accessed | tf_op | source)
XLA Modules:
  0.0 118.4 jit_solution(7798653882129504910)
XLA Ops:
  2.4 10.6 %all-to-all-start = ((bf16[32,16,384]{2,1,0:T(8,128)(2,1)}), bf16[32,16,384]{2,1,0:T(8,128)(2,1)S(1)}, u32[]{:S(2)}, u32[]{:S(2)}) async-start(bf16[32,16,384]{2,1,0:T(8,128)(2,1)} %shard_map.257.refs_1_), calls=%async_computation | async-start | bytes 786432 | tf_op jit(solution)/shard_map/all_to_all | solution.py:531
  13.6 3.5 %collective-permute-start = (bf16[144,384]{1,0:T(8,128)(2,1)S(1)}, bf16[144,384]{1,0:T(8,128)(2,1)S(1)}, u32[]{:S(2)}, u32[]{:S(2)}) collective-permute-start(bf16[144,384]{1,0:T(8,128)(2,1)S(1)} %get-tuple-element.48), channel_id=1, source_target_pairs={{0,16},{16,32},{32,48},{48,64},{64,80},{80,96},{96,112},{112,128},... | collective-permute-start | bytes 331784 | tf_op jit(solution)/shard_map/ppermute | solution.py:519
  17.2 1.9 %collective-permute-start.1 = (bf16[144,384]{1,0:T(8,128)(2,1)S(1)}, bf16[144,384]{1,0:T(8,128)(2,1)S(1)}, u32[]{:S(2)}, u32[]{:S(2)}) collective-permute-start(bf16[144,384]{1,0:T(8,128)(2,1)S(1)} %get-tuple-element.49), channel_id=1, source_target_pairs={{16,0},{32,16},{48,32},{64,48},{80,64},{96,80},{112,96},{128,112},... | collective-permute-start | bytes 331784 | tf_op jit(solution)/shard_map/ppermute | solution.py:519
  19.4 4.5 %collective-permute-done.1.refs_2_.refs_6_.refs_7_.refs_5_ = bf16[144,384]{1,0:T(8,128)(2,1)S(1)} collective-permute-done((bf16[144,384]{1,0:T(8,128)(2,1)S(1)}, bf16[144,384]{1,0:T(8,128)(2,1)S(1)}, u32[]{:S(2)}, u32[]{:S(2)}) %collective-permute-start.1) | collective-permute-done | bytes 110624 | tf_op jit(solution)/shard_map/ppermute | solution.py:519
  24.6 2.3 %all-to-all-done = bf16[32,16,384]{2,1,0:T(8,128)(2,1)S(1)} async-done(((bf16[32,16,384]{2,1,0:T(8,128)(2,1)}), bf16[32,16,384]{2,1,0:T(8,128)(2,1)S(1)}, u32[]{:S(2)}, u32[]{:S(2)}) %all-to-all-start) | async-done | bytes 393248 | tf_op jit(solution)/shard_map/all_to_all | solution.py:531
  26.9 1.8 %shard_map.260 = (bf16[160,384]{1,0:T(8,128)(2,1)S(1)}, bf16[176,384]{1,0:T(8,128)(2,1)S(1)}) custom-call(f32[6]{0:T(128)S(1)} %copy-done.9, s32[2]{0:T(128)S(1)} %add_convert_fusion.1.refs_1_, bf16[512,384]{1,0:T(8,128)(2,1)S(1)} %bitcast.14, bf16[2,160,384]{2,1,0:T(8,128)(2,1)S(1)} %shard_map.259.refs_3_, bf16[128,384]{1,0:T(8,128)(2,1)S(1)} %bitcast.18, ...), custom_call_target="tpu_custom_call" | custom-call | flops 500000000 | bytes 1500000 | tf_op jit(solution)/shard_map/pallas_call | solution.py:83
  28.7 3.4 %collective-permute-start.2 = (bf16[176,384]{1,0:T(8,128)(2,1)S(1)}, bf16[176,384]{1,0:T(8,128)(2,1)S(1)}, u32[]{:S(2)}, u32[]{:S(2)}) collective-permute-start(bf16[176,384]{1,0:T(8,128)(2,1)S(1)} %get-tuple-element.52), channel_id=1, source_target_pairs={{0,1},{1,2},{2,3},{3,4},{4,5},{5,6},{6,7},{7,8},{8,9},{9,10},{10,1... | collective-permute-start | bytes 405512 | tf_op jit(solution)/shard_map/ppermute | solution.py:556
  32.1 1.8 %shard_map.261.refs_2_.refs_1_ = bf16[160,384]{1,0:T(8,128)(2,1)S(1)} custom-call(f32[6]{0:T(128)S(1)} %copy-done.9, s32[2]{0:T(128)S(1)} %add_convert_fusion.1.refs_1_, bf16[512,384]{1,0:T(8,128)(2,1)S(1)} %bitcast.15, bf16[2,160,384]{2,1,0:T(8,128)(2,1)S(1)} %shard_map.259.refs_3_, bf16[128,384]{1,0:T(8,128)(2,1)S(1)} %bitcast.19, ...), custom_call_target="tpu_custom_call" | custom-call | flops 500000000 | bytes 1500000 | tf_op jit(solution)/shard_map/pallas_call | solution.py:83
  33.9 3.4 %shard_map.263 = (bf16[64,384]{1,0:T(8,128)(2,1)S(1)}, f32[112,384]{1,0:T(8,128)S(1)}, bf16[64,384]{1,0:T(8,128)(2,1)S(1)}, bf16[64,1280]{1,0:T(8,128)(2,1)S(1)}...) custom-call(s32[8]{0:T(128)S(1)} %bitcast.25, ...), custom_call_target="tpu_custom_call" | custom-call | flops 1000000000 | bytes 4000000 | tf_op jit(solution)/shard_map/pallas_call | solution.py:83
  37.4 7.2 %collective-permute-done.2.refs_4_ = bf16[176,384]{1,0:T(8,128)(2,1)S(1)} collective-permute-done((bf16[176,384]{1,0:T(8,128)(2,1)S(1)}, bf16[176,384]{1,0:T(8,128)(2,1)S(1)}, u32[]{:S(2)}, u32[]{:S(2)}) %collective-permute-start.2) | collective-permute-done | bytes 135200 | tf_op jit(solution)/shard_map/ppermute | solution.py:556
  44.6 3.5 %shard_map.262 = (bf16[64,384]{1,0:T(8,128)(2,1)S(1)}, f32[112,384]{1,0:T(8,128)S(1)}, bf16[64,384]{1,0:T(8,128)(2,1)S(1)}, bf16[64,1280]{1,0:T(8,128)(2,1)S(1)}...) custom-call(s32[2]{0:T(128)S(1)} %add_convert_fusion.refs_0_, ...), custom_call_target="tpu_custom_call" | custom-call | flops 1000000000 | bytes 4000000 | tf_op jit(solution)/shard_map/pallas_call | solution.py:83
  49.1 2.5 %collective-permute-start.3 = (bf16[4,1056,128]{2,1,0:T(8,128)(2,1)S(1)}, bf16[4,1056,128]{2,1,0:T(8,128)(2,1)S(1)}, u32[]{:S(2)}, u32[]{:S(2)}) collective-permute-start(bf16[4,1056,128]{2,1,0:T(8,128)(2,1)S(1)} %get-tuple-element.66), channel_id=1, source_target_pairs={{0,16},{16,0},{1,17},{17,1},{2,18},{18,2},{3,19},{19,3},{4,20},{20... | collective-permute-start | bytes 3244040 | tf_op jit(solution)/shard_map/ppermute | solution.py:597
  51.7 2.3 %collective-permute-done.3.refs_1_ = bf16[4,1056,128]{2,1,0:T(8,128)(2,1)S(1)} collective-permute-done((bf16[4,1056,128]{2,1,0:T(8,128)(2,1)S(1)}, bf16[4,1056,128]{2,1,0:T(8,128)(2,1)S(1)}, u32[]{:S(2)}, u32[]{:S(2)}) %collective-permute-start.3) | collective-permute-done | bytes 1081376 | tf_op jit(solution)/shard_map/ppermute | solution.py:597
  54.0 1.1 shard_map.265
  55.1 3.5 %all-to-all-start.1 = ((bf16[4,1056,128]{2,1,0:T(8,128)(2,1)}), bf16[4,1056,128]{2,1,0:T(8,128)(2,1)S(1)}, u32[]{:S(2)}, u32[]{:S(2)}) async-start(bf16[4,1056,128]{2,1,0:T(8,128)(2,1)} %get-tuple-element.68), calls=%async_computation.1 | async-start | bytes 2162688 | tf_op jit(solution)/shard_map/all_to_all | solution.py:602
  58.6 8.7 %collective-permute-start.4 = (bf16[112,384]{1,0:T(8,128)(2,1)S(1)}, bf16[112,384]{1,0:T(8,128)(2,1)S(1)}, u32[]{:S(2)}, u32[]{:S(2)}) collective-permute-start(bf16[112,384]{1,0:T(8,128)(2,1)S(1)} %get-tuple-element.69), channel_id=1, source_target_pairs={{0,15},{1,0},{2,1},{3,2},{4,3},{5,4},{6,5},{7,6},{8,7},{9,8},{10,9... | collective-permute-start | bytes 258056 | tf_op jit(solution)/shard_map/ppermute | solution.py:603
  67.3 3.9 %collective-permute-done.4.refs_1_.refs_6_ = bf16[112,384]{1,0:T(8,128)(2,1)S(1)} collective-permute-done((bf16[112,384]{1,0:T(8,128)(2,1)S(1)}, bf16[112,384]{1,0:T(8,128)(2,1)S(1)}, u32[]{:S(2)}, u32[]{:S(2)}) %collective-permute-start.4) | collective-permute-done | bytes 86048 | tf_op jit(solution)/shard_map/ppermute | solution.py:603
  71.2 2.6 %all-to-all-done.1.refs_0_ = bf16[4,1056,128]{2,1,0:T(8,128)(2,1)S(1)} async-done(((bf16[4,1056,128]{2,1,0:T(8,128)(2,1)}), bf16[4,1056,128]{2,1,0:T(8,128)(2,1)S(1)}, u32[]{:S(2)}, u32[]{:S(2)}) %all-to-all-start.1) | async-done | bytes 1081376 | tf_op jit(solution)/shard_map/all_to_all | solution.py:602
  73.8 1.2 shard_map.266.refs_1_
  75.0 10.2 %all-to-all-start.2 = ((bf16[64,40,128]{2,1,0:T(8,128)(2,1)}), bf16[64,40,128]{2,1,0:T(8,128)(2,1)S(1)}, u32[]{:S(2)}, u32[]{:S(2)}) async-start(bf16[64,40,128]{2,1,0:T(8,128)(2,1)} %shard_map.266.refs_1_), calls=%async_computation.2 | async-start | bytes 1310720 | tf_op jit(solution)/shard_map/all_to_all | solution.py:612
  85.2 2.1 %shard_map.267 = (f32[128,384]{1,0:T(8,128)}, bf16[128,384]{1,0:T(8,128)(2,1)}) custom-call(s32[2]{0:T(128)S(1)} %add_convert_fusion.refs_0_, bf16[64,40,128]{2,1,0:T(8,128)(2,1)} %shard_map.266.refs_1_, f32[112,384]{1,0:T(8,128)S(1)} %get-tuple-element.70.refs_2_, f32[112,384]{1,0:T(8,128)S(1)} %get-tuple-element.71.refs_3_, ...), custom_call_target="tpu_custom_call" | custom-call | flops 10000000 | bytes 1000000 | tf_op jit(solution)/shard_map/pallas_call | solution.py:83
  87.3 17.7 %all-to-all-done.2.refs_0_ = bf16[64,40,128]{2,1,0:T(8,128)(2,1)S(1)} async-done(((bf16[64,40,128]{2,1,0:T(8,128)(2,1)}), bf16[64,40,128]{2,1,0:T(8,128)(2,1)S(1)}, u32[]{:S(2)}, u32[]{:S(2)}) %all-to-all-start.2) | async-done | bytes 655392 | tf_op jit(solution)/shard_map/all_to_all | solution.py:612
  105.7 7.0 %all-to-all-start.3 = ((f32[8,24,128]{2,1,0:T(8,128)}), f32[8,24,128]{2,1,0:T(8,128)S(1)}, u32[]{:S(2)}, u32[]{:S(2)}) async-start(f32[8,24,128]{2,1,0:T(8,128)} %get-tuple-element.77), calls=%async_computation.3 | async-start | bytes 196608 | tf_op jit(solution)/shard_map/all_to_all | solution.py:616
  113.4 4.3 %all-to-all-done.3 = f32[8,24,128]{2,1,0:T(8,128)S(1)} async-done(((f32[8,24,128]{2,1,0:T(8,128)}), f32[8,24,128]{2,1,0:T(8,128)S(1)}, u32[]{:S(2)}, u32[]{:S(2)}) %all-to-all-start.3) | async-done | bytes 98336 | tf_op jit(solution)/shard_map/all_to_all | solution.py:616
  (56 shorter events, 6.3 us)
Async XLA Ops:
  1.5 11.4 %copy-start.1 = (bf16[8,16,384]{2,1,0:T(8,128)(2,1)S(1)}, bf16[8,16,384]{2,1,0:T(8,128)(2,1)}, u32[]{:S(2)}) copy-start(bf16[8,16,384]{2,1,0:T(8,128)(2,1)} %refs_0_.3) | copy-start | bytes 294916
  1.5 11.4 %copy-start.5 = (bf16[8,16,384]{2,1,0:T(8,128)(2,1)S(1)}, bf16[8,16,384]{2,1,0:T(8,128)(2,1)}, u32[]{:S(2)}) copy-start(bf16[8,16,384]{2,1,0:T(8,128)(2,1)} %param.33) | copy-start | bytes 294916
  1.5 11.5 %copy-start.8 = (s32[1,1,8]{2,1,0:T(1,128)S(1)}, s32[1,1,8]{2,1,0:T(1,128)}, u32[]{:S(2)}) copy-start(s32[1,1,8]{2,1,0:T(1,128)} %param.34) | copy-start | bytes 100
  1.5 17.6 %copy-start.14 = (f32[384]{0:T(512)S(1)}, f32[384]{0:T(512)}, u32[]{:S(2)}) copy-start(f32[384]{0:T(512)} %param.25) | copy-start | bytes 4612
  1.6 17.6 %copy-start.15 = (f32[384]{0:T(512)S(1)}, f32[384]{0:T(512)}, u32[]{:S(2)}) copy-start(f32[384]{0:T(512)} %param.26) | copy-start | bytes 4612
  1.6 17.6 %copy-start.16 = (f32[384]{0:T(512)S(1)}, f32[384]{0:T(512)}, u32[]{:S(2)}) copy-start(f32[384]{0:T(512)} %param.27) | copy-start | bytes 4612
  1.6 17.6 %copy-start.17 = (f32[384]{0:T(512)S(1)}, f32[384]{0:T(512)}, u32[]{:S(2)}) copy-start(f32[384]{0:T(512)} %param.31) | copy-start | bytes 4612
  1.6 17.6 %copy-start.18 = (f32[384]{0:T(512)S(1)}, f32[384]{0:T(512)}, u32[]{:S(2)}) copy-start(f32[384]{0:T(512)} %param.32) | copy-start | bytes 4612
  1.6 17.7 %copy-start.13 = (f32[1280]{0:T(1024)S(1)}, f32[1280]{0:T(1024)}, u32[]{:S(2)}) copy-start(f32[1280]{0:T(1024)} %param.29) | copy-start | bytes 15364
  1.6 22.3 %copy-start.6 = (bf16[384,384]{1,0:T(8,128)(2,1)S(1)}, bf16[384,384]{1,0:T(8,128)(2,1)}, u32[]{:S(2)}) copy-start(bf16[384,384]{1,0:T(8,128)(2,1)} %refs_3_.1) | copy-start | bytes 884740
  2.4 24.5 %copy-start.2 = (bf16[384,384]{1,0:T(8,128)(2,1)S(1)}, bf16[384,384]{1,0:T(8,128)(2,1)}, u32[]{:S(2)}) copy-start(bf16[384,384]{1,0:T(8,128)(2,1)} %refs_7_.3) | copy-start | bytes 884740
  2.4 24.5 %copy-start.3 = (bf16[384,384]{1,0:T(8,128)(2,1)S(1)}, bf16[384,384]{1,0:T(8,128)(2,1)}, u32[]{:S(2)}) copy-start(bf16[384,384]{1,0:T(8,128)(2,1)} %refs_8_.5) | copy-start | bytes 884740
  2.4 24.5 %copy-start.4 = (bf16[384,384]{1,0:T(8,128)(2,1)S(1)}, bf16[384,384]{1,0:T(8,128)(2,1)}, u32[]{:S(2)}) copy-start(bf16[384,384]{1,0:T(8,128)(2,1)} %refs_9_.3) | copy-start | bytes 884740
  2.4 24.5 %copy-start.9 = (f32[6]{0:T(128)S(1)}, f32[6]{0:T(128)}, u32[]{:S(2)}) copy-start(f32[6]{0:T(128)} %refs_0_.5) | copy-start | bytes 76
  2.4 24.5 %all-to-all-start = ((bf16[32,16,384]{2,1,0:T(8,128)(2,1)}), bf16[32,16,384]{2,1,0:T(8,128)(2,1)S(1)}, u32[]{:S(2)}, u32[]{:S(2)}) async-start(bf16[32,16,384]{2,1,0:T(8,128)(2,1)} %shard_map.257.refs_1_), calls=%async_computation | async-start | bytes 786432 | tf_op jit(solution)/shard_map/all_to_all | solution.py:531
  13.6 5.8 %collective-permute-start = (bf16[144,384]{1,0:T(8,128)(2,1)S(1)}, bf16[144,384]{1,0:T(8,128)(2,1)S(1)}, u32[]{:S(2)}, u32[]{:S(2)}) collective-permute-start(bf16[144,384]{1,0:T(8,128)(2,1)S(1)} %get-tuple-element.48), channel_id=1, source_target_pairs={{0,16},{16,32},{32,48},{48,64},{64,80},{80,96},{96,112},{112,128},... | collective-permute-start | bytes 331784 | tf_op jit(solution)/shard_map/ppermute | solution.py:519
  17.2 6.7 %collective-permute-start.1 = (bf16[144,384]{1,0:T(8,128)(2,1)S(1)}, bf16[144,384]{1,0:T(8,128)(2,1)S(1)}, u32[]{:S(2)}, u32[]{:S(2)}) collective-permute-start(bf16[144,384]{1,0:T(8,128)(2,1)S(1)} %get-tuple-element.49), channel_id=1, source_target_pairs={{16,0},{32,16},{48,32},{64,48},{80,64},{96,80},{112,96},{128,112},... | collective-permute-start | bytes 331784 | tf_op jit(solution)/shard_map/ppermute | solution.py:519
  28.7 15.8 %collective-permute-start.2 = (bf16[176,384]{1,0:T(8,128)(2,1)S(1)}, bf16[176,384]{1,0:T(8,128)(2,1)S(1)}, u32[]{:S(2)}, u32[]{:S(2)}) collective-permute-start(bf16[176,384]{1,0:T(8,128)(2,1)S(1)} %get-tuple-element.52), channel_id=1, source_target_pairs={{0,1},{1,2},{2,3},{3,4},{4,5},{5,6},{6,7},{7,8},{8,9},{9,10},{10,1... | collective-permute-start | bytes 405512 | tf_op jit(solution)/shard_map/ppermute | solution.py:556
  37.4 10.7 %copy-start.12 = (bf16[384,384]{1,0:T(8,128)(2,1)S(1)}, bf16[384,384]{1,0:T(8,128)(2,1)}, u32[]{:S(2)}) copy-start(bf16[384,384]{1,0:T(8,128)(2,1)} %constant.33.clone.refs_1_) | copy-start | bytes 884740
  49.1 4.9 %collective-permute-start.3 = (bf16[4,1056,128]{2,1,0:T(8,128)(2,1)S(1)}, bf16[4,1056,128]{2,1,0:T(8,128)(2,1)S(1)}, u32[]{:S(2)}, u32[]{:S(2)}) collective-permute-start(bf16[4,1056,128]{2,1,0:T(8,128)(2,1)S(1)} %get-tuple-element.66), channel_id=1, source_target_pairs={{0,16},{16,0},{1,17},{17,1},{2,18},{18,2},{3,19},{19,3},{4,20},{20... | collective-permute-start | bytes 3244040 | tf_op jit(solution)/shard_map/ppermute | solution.py:597
  55.1 18.7 %all-to-all-start.1 = ((bf16[4,1056,128]{2,1,0:T(8,128)(2,1)}), bf16[4,1056,128]{2,1,0:T(8,128)(2,1)S(1)}, u32[]{:S(2)}, u32[]{:S(2)}) async-start(bf16[4,1056,128]{2,1,0:T(8,128)(2,1)} %get-tuple-element.68), calls=%async_computation.1 | async-start | bytes 2162688 | tf_op jit(solution)/shard_map/all_to_all | solution.py:602
  58.6 12.6 %collective-permute-start.4 = (bf16[112,384]{1,0:T(8,128)(2,1)S(1)}, bf16[112,384]{1,0:T(8,128)(2,1)S(1)}, u32[]{:S(2)}, u32[]{:S(2)}) collective-permute-start(bf16[112,384]{1,0:T(8,128)(2,1)S(1)} %get-tuple-element.69), channel_id=1, source_target_pairs={{0,15},{1,0},{2,1},{3,2},{4,3},{5,4},{6,5},{7,6},{8,7},{9,8},{10,9... | collective-permute-start | bytes 258056 | tf_op jit(solution)/shard_map/ppermute | solution.py:603
  75.0 30.0 %all-to-all-start.2 = ((bf16[64,40,128]{2,1,0:T(8,128)(2,1)}), bf16[64,40,128]{2,1,0:T(8,128)(2,1)S(1)}, u32[]{:S(2)}, u32[]{:S(2)}) async-start(bf16[64,40,128]{2,1,0:T(8,128)(2,1)} %shard_map.266.refs_1_), calls=%async_computation.2 | async-start | bytes 1310720 | tf_op jit(solution)/shard_map/all_to_all | solution.py:612
  105.7 12.0 %all-to-all-start.3 = ((f32[8,24,128]{2,1,0:T(8,128)}), f32[8,24,128]{2,1,0:T(8,128)S(1)}, u32[]{:S(2)}, u32[]{:S(2)}) async-start(f32[8,24,128]{2,1,0:T(8,128)} %get-tuple-element.77), calls=%async_computation.3 | async-start | bytes 196608 | tf_op jit(solution)/shard_map/all_to_all | solution.py:616
  (4 other events, 16.5 us)

commit v7 on v6

--- a/solution.py
+++ b/solution.py
@@ -145,10 +145,17 @@
     return jnp.concatenate([above[:n, :], feat[...], below[:n, :]], axis=0)
 
 
-def query_kernel(feat, above, below, w_query, out):
-    query = head_scaled(mm(stacked_rows(feat, above, below), w_query[...]))
-    for h, half in enumerate(split_columns(query)):
-        out[h] = half.astype(BF16)
+def right_query_kernel(feat, above, below, w_query, out):
+    out[...] = half_query(1, feat, above, below, w_query)
+
+
+def left_query_kernel(feat, above, below, w_query, after, out):
+    out[...] = half_query(0, feat, above, below, w_query)
+
+
+def half_query(h, feat, above, below, w_query):
+    rows = split_columns(stacked_rows(feat, above, below).astype(F32))[h].astype(BF16)
+    return head_scaled(mm(rows, w_query[...])).astype(BF16)
 
 
 def right_attention_kernel(
@@ -192,7 +199,7 @@
     pairs = []
     for pair in range(HEADS // 2):
         lanes = slice(128 * pair, 128 * pair + 128)
-        q = query[h, :, lanes].astype(F32)
+        q = query[:, lanes].astype(F32)
         parts = []
         for sub in range(2):
             q_half = jnp.where(lower if sub == 0 else ~lower, q, 0.0).astype(BF16)
@@ -537,14 +544,13 @@
         tiles, copies, flat, cot, smem=(0,), fence=(1,), nbytes=800_000,
     )
     above, below = neighbours(feat_first, feat_last, ROW)
+    half_mixed = ((ROWS_M * HALF, C), BF16)
     (query,) = call(
-        query_kernel, [((2, ROWS_M * WB // 2, C), BF16)], flat, above, below, w_query,
-        flops=2 * 10**8, nbytes=900_000,
+        right_query_kernel, [half_mixed], flat, above, below, w_query, flops=10**8, nbytes=900_000
     )
     at_row = lax.axis_index(ROW)
     valid = jnp.stack([at_row > 0, at_row < N_ROW - 1]).astype(jnp.int32)
     inputs = (logit_scale, valid, pooled, query, flat, above, below, w_key, w_value, w_out)
-    half_mixed = ((ROWS_M * HALF, C), BF16)
     cost = dict(flops=5 * 10**8, nbytes=1_500_000, trans=250_000)
     mixed_right, send = call(
         right_attention_kernel, [half_mixed, ((RIGHT, C), BF16)], *inputs, tiles, masked,
@@ -554,6 +560,11 @@
     n_col = lax.axis_size(COL)
     at_col = lax.axis_index(COL)
     got = lax.ppermute(send, COL, [(i, (i + 1) % n_col) for i in range(n_col)])
+    (query,) = call(
+        left_query_kernel, [half_mixed], flat, above, below, w_query, mixed_right, fence=(4,),
+        flops=10**8, nbytes=900_000,
+    )
+    inputs = inputs[:3] + (query,) + inputs[4:]
     (mixed_left,) = call(
         left_attention_kernel, [half_mixed], *inputs, mixed_right, smem=(0, 1), fence=(10,), **cost
     )

time: 119 us -> 119 us (level)
    pallas_call x13 -> x14, Pallas kernels: 19.4 us -> 19.3 us  [call(): pl.pallas_call(run, out_shape=[jax.ShapeDtypeStruct(s, d) for s, d in out...]
where the time goes in v7:
time: 119 us; the launch traced here: 118 us
  starting transfers between devices  51.3 us (43%)
  waiting for transfers between devices  44.6 us (37%)
  Pallas kernels  19.3 us (16%)
  local copies, waits for them, and re-layouts  1.61 us (1%)
    pallas_call x14, Pallas kernels, call(): pl.pallas_call(run, out_shape=[jax.ShapeDtypeStruct(s, d) for s, d in out...  19.3 us
    all_to_all x1, waiting for transfers between devices, body(): part = lax.all_to_all(spread, YZ, 0, 0, tiled=True)  17.7 us
    all_to_all x1, starting transfers between devices, body(): lax.all_to_all(copies, ROW, 0, 0, tiled=True).reshape(N_ROW * WB, C)  10.6 us
    all_to_all x1, starting transfers between devices, body(): part = lax.all_to_all(spread, YZ, 0, 0, tiled=True)  10.2 us
    ppermute x1, starting transfers between devices, body(): got = lax.ppermute(send, COL, [(i, (i - 1) % n_col) for i in range(n_col)])  8.68 us
    all_to_all x1, starting transfers between devices, body(): small = lax.all_to_all(small, CX, 0, 0, tiled=True)  7.03 us
    ppermute x1, waiting for transfers between devices, body(): got = lax.ppermute(send, COL, [(i, (i + 1) % n_col) for i in range(n_col)])  6.87 us
    ppermute x1, waiting for transfers between devices, neighbours(): lax.ppermute(before_edge, axes, down)  4.48 us
  transfers between devices with their start and end apart: 9, of which 8 were waited for; matrix products, arithmetic and copies ran while one was open for 1% of the time, Pallas kernels for 7%

profile of v7, /device:TPU:1, one launch (start us, length us, event | category | flops | bytes accessed | tf_op | source)
XLA Modules:
  0.0 118.0 jit_solution(3710108042140621323)
XLA Ops:
  2.4 10.6 %all-to-all-start = ((bf16[32,16,384]{2,1,0:T(8,128)(2,1)}), bf16[32,16,384]{2,1,0:T(8,128)(2,1)S(1)}, u32[]{:S(2)}, u32[]{:S(2)}) async-start(bf16[32,16,384]{2,1,0:T(8,128)(2,1)} %shard_map.257.refs_1_), calls=%async_computation | async-start | bytes 786432 | tf_op jit(solution)/shard_map/all_to_all | solution.py:538
  13.6 3.5 %collective-permute-start = (bf16[144,384]{1,0:T(8,128)(2,1)S(1)}, bf16[144,384]{1,0:T(8,128)(2,1)S(1)}, u32[]{:S(2)}, u32[]{:S(2)}) collective-permute-start(bf16[144,384]{1,0:T(8,128)(2,1)S(1)} %get-tuple-element.48), channel_id=1, source_target_pairs={{0,16},{16,32},{32,48},{48,64},{64,80},{80,96},{96,112},{112,128},... | collective-permute-start | bytes 331784 | tf_op jit(solution)/shard_map/ppermute | solution.py:526
  17.2 1.9 %collective-permute-start.1 = (bf16[144,384]{1,0:T(8,128)(2,1)S(1)}, bf16[144,384]{1,0:T(8,128)(2,1)S(1)}, u32[]{:S(2)}, u32[]{:S(2)}) collective-permute-start(bf16[144,384]{1,0:T(8,128)(2,1)S(1)} %get-tuple-element.49), channel_id=1, source_target_pairs={{16,0},{32,16},{48,32},{64,48},{80,64},{96,80},{112,96},{128,112},... | collective-permute-start | bytes 331784 | tf_op jit(solution)/shard_map/ppermute | solution.py:526
  19.4 4.5 %collective-permute-done.1.refs_2_.refs_6_.refs_7_.refs_5_ = bf16[144,384]{1,0:T(8,128)(2,1)S(1)} collective-permute-done((bf16[144,384]{1,0:T(8,128)(2,1)S(1)}, bf16[144,384]{1,0:T(8,128)(2,1)S(1)}, u32[]{:S(2)}, u32[]{:S(2)}) %collective-permute-start.1) | collective-permute-done | bytes 110624 | tf_op jit(solution)/shard_map/ppermute | solution.py:526
  24.4 2.5 %all-to-all-done = bf16[32,16,384]{2,1,0:T(8,128)(2,1)S(1)} async-done(((bf16[32,16,384]{2,1,0:T(8,128)(2,1)}), bf16[32,16,384]{2,1,0:T(8,128)(2,1)S(1)}, u32[]{:S(2)}, u32[]{:S(2)}) %all-to-all-start) | async-done | bytes 393248 | tf_op jit(solution)/shard_map/all_to_all | solution.py:538
  26.9 1.8 %shard_map.260 = (bf16[160,384]{1,0:T(8,128)(2,1)S(1)}, bf16[176,384]{1,0:T(8,128)(2,1)S(1)}) custom-call(f32[6]{0:T(128)S(1)} %copy-done.8, s32[2]{0:T(128)S(1)} %add_convert_fusion.1.refs_1_, bf16[512,384]{1,0:T(8,128)(2,1)S(1)} %bitcast.19, bf16[160,384]{1,0:T(8,128)(2,1)S(1)} %shard_map.259.refs_3_, bf16[128,384]{1,0:T(8,128)(2,1)S(1)} %bitcast.16, ...), custom_call_target="tpu_custom_call" | custom-call | flops 500000000 | bytes 1500000 | tf_op jit(solution)/shard_map/pallas_call | solution.py:83
  28.7 3.2 %collective-permute-start.2 = (bf16[176,384]{1,0:T(8,128)(2,1)S(1)}, bf16[176,384]{1,0:T(8,128)(2,1)S(1)}, u32[]{:S(2)}, u32[]{:S(2)}) collective-permute-start(bf16[176,384]{1,0:T(8,128)(2,1)S(1)} %get-tuple-element.52), channel_id=1, source_target_pairs={{0,1},{1,2},{2,3},{3,4},{4,5},{5,6},{6,7},{7,8},{8,9},{9,10},{10,1... | collective-permute-start | bytes 405512 | tf_op jit(solution)/shard_map/ppermute | solution.py:562
  32.5 1.8 %shard_map.262.refs_2_.refs_1_ = bf16[160,384]{1,0:T(8,128)(2,1)S(1)} custom-call(f32[6]{0:T(128)S(1)} %copy-done.8, s32[2]{0:T(128)S(1)} %add_convert_fusion.1.refs_1_, bf16[512,384]{1,0:T(8,128)(2,1)S(1)} %bitcast.20, bf16[160,384]{1,0:T(8,128)(2,1)S(1)} %shard_map.261.refs_3_, bf16[128,384]{1,0:T(8,128)(2,1)S(1)} %bitcast.18, ...), custom_call_target="tpu_custom_call" | custom-call | flops 500000000 | bytes 1500000 | tf_op jit(solution)/shard_map/pallas_call | solution.py:83
  34.3 3.2 %shard_map.264 = (bf16[64,384]{1,0:T(8,128)(2,1)S(1)}, f32[112,384]{1,0:T(8,128)S(1)}, bf16[64,384]{1,0:T(8,128)(2,1)S(1)}, bf16[64,1280]{1,0:T(8,128)(2,1)S(1)}...) custom-call(s32[8]{0:T(128)S(1)} %bitcast.26, ...), custom_call_target="tpu_custom_call" | custom-call | flops 1000000000 | bytes 4000000 | tf_op jit(solution)/shard_map/pallas_call | solution.py:83
  37.5 6.9 %collective-permute-done.2.refs_4_ = bf16[176,384]{1,0:T(8,128)(2,1)S(1)} collective-permute-done((bf16[176,384]{1,0:T(8,128)(2,1)S(1)}, bf16[176,384]{1,0:T(8,128)(2,1)S(1)}, u32[]{:S(2)}, u32[]{:S(2)}) %collective-permute-start.2) | collective-permute-done | bytes 135200 | tf_op jit(solution)/shard_map/ppermute | solution.py:562
  44.4 3.3 %shard_map.263 = (bf16[64,384]{1,0:T(8,128)(2,1)S(1)}, f32[112,384]{1,0:T(8,128)S(1)}, bf16[64,384]{1,0:T(8,128)(2,1)S(1)}, bf16[64,1280]{1,0:T(8,128)(2,1)S(1)}...) custom-call(s32[2]{0:T(128)S(1)} %add_convert_fusion.refs_0_, ...), custom_call_target="tpu_custom_call" | custom-call | flops 1000000000 | bytes 4000000 | tf_op jit(solution)/shard_map/pallas_call | solution.py:83
  48.7 2.5 %collective-permute-start.3 = (bf16[4,1056,128]{2,1,0:T(8,128)(2,1)S(1)}, bf16[4,1056,128]{2,1,0:T(8,128)(2,1)S(1)}, u32[]{:S(2)}, u32[]{:S(2)}) collective-permute-start(bf16[4,1056,128]{2,1,0:T(8,128)(2,1)S(1)} %get-tuple-element.66), channel_id=1, source_target_pairs={{0,16},{16,0},{1,17},{17,1},{2,18},{18,2},{3,19},{19,3},{4,20},{20... | collective-permute-start | bytes 3244040 | tf_op jit(solution)/shard_map/ppermute | solution.py:608
  51.3 2.3 %collective-permute-done.3.refs_1_ = bf16[4,1056,128]{2,1,0:T(8,128)(2,1)S(1)} collective-permute-done((bf16[4,1056,128]{2,1,0:T(8,128)(2,1)S(1)}, bf16[4,1056,128]{2,1,0:T(8,128)(2,1)S(1)}, u32[]{:S(2)}, u32[]{:S(2)}) %collective-permute-start.3) | collective-permute-done | bytes 1081376 | tf_op jit(solution)/shard_map/ppermute | solution.py:608
  53.6 1.1 shard_map.266
  54.7 3.5 %all-to-all-start.1 = ((bf16[4,1056,128]{2,1,0:T(8,128)(2,1)}), bf16[4,1056,128]{2,1,0:T(8,128)(2,1)S(1)}, u32[]{:S(2)}, u32[]{:S(2)}) async-start(bf16[4,1056,128]{2,1,0:T(8,128)(2,1)} %get-tuple-element.68), calls=%async_computation.1 | async-start | bytes 2162688 | tf_op jit(solution)/shard_map/all_to_all | solution.py:613
  58.2 8.7 %collective-permute-start.4 = (bf16[112,384]{1,0:T(8,128)(2,1)S(1)}, bf16[112,384]{1,0:T(8,128)(2,1)S(1)}, u32[]{:S(2)}, u32[]{:S(2)}) collective-permute-start(bf16[112,384]{1,0:T(8,128)(2,1)S(1)} %get-tuple-element.69), channel_id=1, source_target_pairs={{0,15},{1,0},{2,1},{3,2},{4,3},{5,4},{6,5},{7,6},{8,7},{9,8},{10,9... | collective-permute-start | bytes 258056 | tf_op jit(solution)/shard_map/ppermute | solution.py:614
  66.9 3.9 %collective-permute-done.4.refs_1_.refs_6_ = bf16[112,384]{1,0:T(8,128)(2,1)S(1)} collective-permute-done((bf16[112,384]{1,0:T(8,128)(2,1)S(1)}, bf16[112,384]{1,0:T(8,128)(2,1)S(1)}, u32[]{:S(2)}, u32[]{:S(2)}) %collective-permute-start.4) | collective-permute-done | bytes 86048 | tf_op jit(solution)/shard_map/ppermute | solution.py:614
  70.8 2.6 %all-to-all-done.1.refs_0_ = bf16[4,1056,128]{2,1,0:T(8,128)(2,1)S(1)} async-done(((bf16[4,1056,128]{2,1,0:T(8,128)(2,1)}), bf16[4,1056,128]{2,1,0:T(8,128)(2,1)S(1)}, u32[]{:S(2)}, u32[]{:S(2)}) %all-to-all-start.1) | async-done | bytes 1081376 | tf_op jit(solution)/shard_map/all_to_all | solution.py:613
  73.4 1.2 %shard_map.267.refs_1_ = bf16[64,40,128]{2,1,0:T(8,128)(2,1)} custom-call(bf16[4,1056,128]{2,1,0:T(8,128)(2,1)S(1)} %all-to-all-done.1.refs_0_, bf16[112,384]{1,0:T(8,128)(2,1)S(1)} %collective-permute-done.4.refs_1_.refs_6_), custom_call_target="tpu_custom_call" | custom-call | bytes 2000000 | tf_op jit(solution)/shard_map/pallas_call | solution.py:83
  74.6 10.2 %all-to-all-start.2 = ((bf16[64,40,128]{2,1,0:T(8,128)(2,1)}), bf16[64,40,128]{2,1,0:T(8,128)(2,1)S(1)}, u32[]{:S(2)}, u32[]{:S(2)}) async-start(bf16[64,40,128]{2,1,0:T(8,128)(2,1)} %shard_map.267.refs_1_), calls=%async_computation.2 | async-start | bytes 1310720 | tf_op jit(solution)/shard_map/all_to_all | solution.py:623
  84.8 2.1 %shard_map.268 = (f32[128,384]{1,0:T(8,128)}, bf16[128,384]{1,0:T(8,128)(2,1)}) custom-call(s32[2]{0:T(128)S(1)} %add_convert_fusion.refs_0_, bf16[64,40,128]{2,1,0:T(8,128)(2,1)} %shard_map.267.refs_1_, f32[112,384]{1,0:T(8,128)S(1)} %get-tuple-element.70.refs_2_, f32[112,384]{1,0:T(8,128)S(1)} %get-tuple-element.71.refs_3_, ...), custom_call_target="tpu_custom_call" | custom-call | flops 10000000 | bytes 1000000 | tf_op jit(solution)/shard_map/pallas_call | solution.py:83
  86.9 17.7 %all-to-all-done.2.refs_0_ = bf16[64,40,128]{2,1,0:T(8,128)(2,1)S(1)} async-done(((bf16[64,40,128]{2,1,0:T(8,128)(2,1)}), bf16[64,40,128]{2,1,0:T(8,128)(2,1)S(1)}, u32[]{:S(2)}, u32[]{:S(2)}) %all-to-all-start.2) | async-done | bytes 655392 | tf_op jit(solution)/shard_map/all_to_all | solution.py:623
  105.3 7.0 %all-to-all-start.3 = ((f32[8,24,128]{2,1,0:T(8,128)}), f32[8,24,128]{2,1,0:T(8,128)S(1)}, u32[]{:S(2)}, u32[]{:S(2)}) async-start(f32[8,24,128]{2,1,0:T(8,128)} %get-tuple-element.77), calls=%async_computation.3 | async-start | bytes 196608 | tf_op jit(solution)/shard_map/all_to_all | solution.py:627
  113.0 4.3 %all-to-all-done.3 = f32[8,24,128]{2,1,0:T(8,128)S(1)} async-done(((f32[8,24,128]{2,1,0:T(8,128)}), f32[8,24,128]{2,1,0:T(8,128)S(1)}, u32[]{:S(2)}, u32[]{:S(2)}) %all-to-all-start.3) | async-done | bytes 98336 | tf_op jit(solution)/shard_map/all_to_all | solution.py:627
  (57 shorter events, 6.6 us)
Async XLA Ops:
  1.5 11.4 %copy-start.1 = (bf16[8,16,384]{2,1,0:T(8,128)(2,1)S(1)}, bf16[8,16,384]{2,1,0:T(8,128)(2,1)}, u32[]{:S(2)}) copy-start(bf16[8,16,384]{2,1,0:T(8,128)(2,1)} %refs_0_.3) | copy-start | bytes 294916
  1.5 11.4 %copy-start.3 = (bf16[8,16,384]{2,1,0:T(8,128)(2,1)S(1)}, bf16[8,16,384]{2,1,0:T(8,128)(2,1)}, u32[]{:S(2)}) copy-start(bf16[8,16,384]{2,1,0:T(8,128)(2,1)} %param.33) | copy-start | bytes 294916
  1.5 11.5 %copy-start.9 = (s32[1,1,8]{2,1,0:T(1,128)S(1)}, s32[1,1,8]{2,1,0:T(1,128)}, u32[]{:S(2)}) copy-start(s32[1,1,8]{2,1,0:T(1,128)} %param.34) | copy-start | bytes 100
  1.5 17.6 %copy-start.14 = (f32[384]{0:T(512)S(1)}, f32[384]{0:T(512)}, u32[]{:S(2)}) copy-start(f32[384]{0:T(512)} %param.25) | copy-start | bytes 4612
  1.6 17.6 %copy-start.15 = (f32[384]{0:T(512)S(1)}, f32[384]{0:T(512)}, u32[]{:S(2)}) copy-start(f32[384]{0:T(512)} %param.26) | copy-start | bytes 4612
  1.6 17.6 %copy-start.16 = (f32[384]{0:T(512)S(1)}, f32[384]{0:T(512)}, u32[]{:S(2)}) copy-start(f32[384]{0:T(512)} %param.27) | copy-start | bytes 4612
  1.6 17.6 %copy-start.17 = (f32[384]{0:T(512)S(1)}, f32[384]{0:T(512)}, u32[]{:S(2)}) copy-start(f32[384]{0:T(512)} %param.31) | copy-start | bytes 4612
  1.6 17.6 %copy-start.18 = (f32[384]{0:T(512)S(1)}, f32[384]{0:T(512)}, u32[]{:S(2)}) copy-start(f32[384]{0:T(512)} %param.32) | copy-start | bytes 4612
  1.6 17.7 %copy-start.13 = (f32[1280]{0:T(1024)S(1)}, f32[1280]{0:T(1024)}, u32[]{:S(2)}) copy-start(f32[1280]{0:T(1024)} %param.29) | copy-start | bytes 15364
  1.6 22.3 %copy-start.2 = (bf16[384,384]{1,0:T(8,128)(2,1)S(1)}, bf16[384,384]{1,0:T(8,128)(2,1)}, u32[]{:S(2)}) copy-start(bf16[384,384]{1,0:T(8,128)(2,1)} %refs_3_.3) | copy-start | bytes 884740
  2.4 24.5 %copy-start.4 = (bf16[384,384]{1,0:T(8,128)(2,1)S(1)}, bf16[384,384]{1,0:T(8,128)(2,1)}, u32[]{:S(2)}) copy-start(bf16[384,384]{1,0:T(8,128)(2,1)} %refs_7_.3) | copy-start | bytes 884740
  2.4 24.5 %copy-start.5 = (bf16[384,384]{1,0:T(8,128)(2,1)S(1)}, bf16[384,384]{1,0:T(8,128)(2,1)}, u32[]{:S(2)}) copy-start(bf16[384,384]{1,0:T(8,128)(2,1)} %refs_8_.5) | copy-start | bytes 884740
  2.4 24.5 %copy-start.6 = (bf16[384,384]{1,0:T(8,128)(2,1)S(1)}, bf16[384,384]{1,0:T(8,128)(2,1)}, u32[]{:S(2)}) copy-start(bf16[384,384]{1,0:T(8,128)(2,1)} %refs_9_.3) | copy-start | bytes 884740
  2.4 24.5 %copy-start.8 = (f32[6]{0:T(128)S(1)}, f32[6]{0:T(128)}, u32[]{:S(2)}) copy-start(f32[6]{0:T(128)} %refs_0_.5) | copy-start | bytes 76
  2.4 24.5 %all-to-all-start = ((bf16[32,16,384]{2,1,0:T(8,128)(2,1)}), bf16[32,16,384]{2,1,0:T(8,128)(2,1)S(1)}, u32[]{:S(2)}, u32[]{:S(2)}) async-start(bf16[32,16,384]{2,1,0:T(8,128)(2,1)} %shard_map.257.refs_1_), calls=%async_computation | async-start | bytes 786432 | tf_op jit(solution)/shard_map/all_to_all | solution.py:538
  13.6 5.8 %collective-permute-start = (bf16[144,384]{1,0:T(8,128)(2,1)S(1)}, bf16[144,384]{1,0:T(8,128)(2,1)S(1)}, u32[]{:S(2)}, u32[]{:S(2)}) collective-permute-start(bf16[144,384]{1,0:T(8,128)(2,1)S(1)} %get-tuple-element.48), channel_id=1, source_target_pairs={{0,16},{16,32},{32,48},{48,64},{64,80},{80,96},{96,112},{112,128},... | collective-permute-start | bytes 331784 | tf_op jit(solution)/shard_map/ppermute | solution.py:526
  17.2 6.7 %collective-permute-start.1 = (bf16[144,384]{1,0:T(8,128)(2,1)S(1)}, bf16[144,384]{1,0:T(8,128)(2,1)S(1)}, u32[]{:S(2)}, u32[]{:S(2)}) collective-permute-start(bf16[144,384]{1,0:T(8,128)(2,1)S(1)} %get-tuple-element.49), channel_id=1, source_target_pairs={{16,0},{32,16},{48,32},{64,48},{80,64},{96,80},{112,96},{128,112},... | collective-permute-start | bytes 331784 | tf_op jit(solution)/shard_map/ppermute | solution.py:526
  28.7 15.7 %collective-permute-start.2 = (bf16[176,384]{1,0:T(8,128)(2,1)S(1)}, bf16[176,384]{1,0:T(8,128)(2,1)S(1)}, u32[]{:S(2)}, u32[]{:S(2)}) collective-permute-start(bf16[176,384]{1,0:T(8,128)(2,1)S(1)} %get-tuple-element.52), channel_id=1, source_target_pairs={{0,1},{1,2},{2,3},{3,4},{4,5},{5,6},{6,7},{7,8},{8,9},{9,10},{10,1... | collective-permute-start | bytes 405512 | tf_op jit(solution)/shard_map/ppermute | solution.py:562
  37.5 10.2 %copy-start.12 = (bf16[384,384]{1,0:T(8,128)(2,1)S(1)}, bf16[384,384]{1,0:T(8,128)(2,1)}, u32[]{:S(2)}) copy-start(bf16[384,384]{1,0:T(8,128)(2,1)} %constant.33.clone.refs_1_) | copy-start | bytes 884740
  48.7 4.8 %collective-permute-start.3 = (bf16[4,1056,128]{2,1,0:T(8,128)(2,1)S(1)}, bf16[4,1056,128]{2,1,0:T(8,128)(2,1)S(1)}, u32[]{:S(2)}, u32[]{:S(2)}) collective-permute-start(bf16[4,1056,128]{2,1,0:T(8,128)(2,1)S(1)} %get-tuple-element.66), channel_id=1, source_target_pairs={{0,16},{16,0},{1,17},{17,1},{2,18},{18,2},{3,19},{19,3},{4,20},{20... | collective-permute-start | bytes 3244040 | tf_op jit(solution)/shard_map/ppermute | solution.py:608
  54.7 18.7 %all-to-all-start.1 = ((bf16[4,1056,128]{2,1,0:T(8,128)(2,1)}), bf16[4,1056,128]{2,1,0:T(8,128)(2,1)S(1)}, u32[]{:S(2)}, u32[]{:S(2)}) async-start(bf16[4,1056,128]{2,1,0:T(8,128)(2,1)} %get-tuple-element.68), calls=%async_computation.1 | async-start | bytes 2162688 | tf_op jit(solution)/shard_map/all_to_all | solution.py:613
  58.2 12.6 %collective-permute-start.4 = (bf16[112,384]{1,0:T(8,128)(2,1)S(1)}, bf16[112,384]{1,0:T(8,128)(2,1)S(1)}, u32[]{:S(2)}, u32[]{:S(2)}) collective-permute-start(bf16[112,384]{1,0:T(8,128)(2,1)S(1)} %get-tuple-element.69), channel_id=1, source_target_pairs={{0,15},{1,0},{2,1},{3,2},{4,3},{5,4},{6,5},{7,6},{8,7},{9,8},{10,9... | collective-permute-start | bytes 258056 | tf_op jit(solution)/shard_map/ppermute | solution.py:614
  74.6 30.0 %all-to-all-start.2 = ((bf16[64,40,128]{2,1,0:T(8,128)(2,1)}), bf16[64,40,128]{2,1,0:T(8,128)(2,1)S(1)}, u32[]{:S(2)}, u32[]{:S(2)}) async-start(bf16[64,40,128]{2,1,0:T(8,128)(2,1)} %shard_map.267.refs_1_), calls=%async_computation.2 | async-start | bytes 1310720 | tf_op jit(solution)/shard_map/all_to_all | solution.py:623
  105.3 12.0 %all-to-all-start.3 = ((f32[8,24,128]{2,1,0:T(8,128)}), f32[8,24,128]{2,1,0:T(8,128)S(1)}, u32[]{:S(2)}, u32[]{:S(2)}) async-start(f32[8,24,128]{2,1,0:T(8,128)} %get-tuple-element.77), calls=%async_computation.3 | async-start | bytes 196608 | tf_op jit(solution)/shard_map/all_to_all | solution.py:627
  (4 other events, 6.9 us)
